TPU v7x, 512 devices: a whole 4x8x8 slice. The times are simulated.
512 devices in a mesh: dp: 16 (over z, core), expert: 32 (over y, x).
Axes of the slice: x: 4, y: 8, z: 8, core: 2. Of those that a mesh axis runs over, the one named last changes fastest.
Arguments:
- grad_values: bfloat16 [4096, 7168], P(('dp', 'expert')), may hold values from -6 to 6
- grad_scales: bfloat16 [4096], P(('dp', 'expert')), may hold values from 0.099609375 to 2
- hidden_act: bfloat16 [16, 128, 4096], P('dp', None, 'expert'), may hold values from -4 to 4
- down_weight: bfloat16 [4096, 7168], P('expert'), may hold values from -0.0625 to 0.0625
- slot_token: int32 [16, 2, 128], P('dp'), may hold values from 0 to 255, as said below
- slot_count: int32 [16, 2], P('dp'), may hold values from 32 to 128, as said below
- slot_gate: float32 [16, 2, 128], P('dp'), may hold values from 0.05 to 1
Outputs:
- hidden_grad: bfloat16 [16, 128, 4096], P('dp', None, 'expert')
- weight_grad: bfloat16 [4096, 7168], P('expert')
- gate_grad: float32 [4096, 2], P(('dp', 'expert'))
Inputs may be any that keep to these rules, and one draw needn't show every extreme that they name: `slot_token`: within one expert and group the 128 slots name distinct tokens of the group. `slot_count`: live slots are the first ones of each expert and group; some expert of some group has all 128 slots live.
All inputs are finite; a program needn't handle non-finite values.
Results may differ from a plain program's by a relative error of at most 0.0057.
Values may be sent and summed in bfloat16 or wider, within the bound.
No kernel may reach another device: no remote copies, remote signals or barrier semaphores. Data moves between devices by JAX's collectives and lax.ppermute only.
A program may use at most 64 MiB of HBM per device.

v0:
```python
import jax
import jax.numpy as jnp
from jax import lax
from jax.sharding import PartitionSpec as P


def on_device(grad_values, grad_scales, hidden_act, down_weight, slot_token, slot_count, slot_gate):
    position = lax.axis_index("expert")
    expert_total = slot_token.shape[1]
    sharing = lax.axis_size("expert") // expert_total
    owner_expert = position // sharing
    slot_tok = lax.dynamic_index_in_dim(slot_token[0], owner_expert, 0, keepdims=False)
    slot_num = lax.dynamic_index_in_dim(slot_count[0], owner_expert, 0, keepdims=False)
    slot_gw = lax.dynamic_index_in_dim(slot_gate[0], owner_expert, 0, keepdims=False)
    slots = slot_tok.shape[0]
    slot_live = jnp.arange(slots, dtype=jnp.int32) < slot_num
    tok_rows = grad_values.shape[0]
    group_rows = tok_rows * lax.axis_size("expert")
    values_all, scales_all = (
        lax.all_gather(grad_values, "expert", axis=0, tiled=True),
        lax.all_gather(grad_scales, "expert", axis=0, tiled=True),
    )
    picked = jnp.take(values_all, slot_tok, axis=0).astype(jnp.float32)
    picked = picked * jnp.take(scales_all, slot_tok).astype(jnp.float32)[:, None]
    routed = jnp.where(slot_live[:, None], picked, 0.0).astype(jnp.bfloat16)
    project = lax.dot_general(
        routed, down_weight, (((1,), (1,)), ((), ())), preferred_element_type=jnp.float32
    )
    hidden = hidden_act[0]
    hidden_grad = (slot_gw[:, None] * project).astype(jnp.bfloat16)[None]
    weighted = (slot_gw[:, None] * hidden.astype(jnp.float32)).astype(jnp.bfloat16)
    weight_part = lax.dot_general(
        weighted, routed, (((0,), (0,)), ((), ())), preferred_element_type=jnp.float32
    )
    weight_grad = lax.psum(weight_part, "dp").astype(jnp.bfloat16)
    partial_sum = jnp.sum(hidden.astype(jnp.float32) * project, axis=1)
    onehot = (slot_tok[:, None] == jnp.arange(group_rows, dtype=jnp.int32)[None, :]).astype(
        jnp.float32
    )
    per_token = jnp.dot(partial_sum, onehot, precision=lax.Precision.HIGHEST)
    expert_cols = (jnp.arange(expert_total, dtype=jnp.int32) == owner_expert).astype(jnp.float32)
    per_pair = per_token[:, None] * expert_cols[None, :]
    gate_grad = lax.psum_scatter(per_pair, "expert", scatter_dimension=0, tiled=True)
    return (hidden_grad, weight_grad, gate_grad)


def solution(mesh):
    return jax.shard_map(
        on_device,
        mesh=mesh,
        in_specs=(
            P(("dp", "expert"), None),
            P(("dp", "expert")),
            P("dp", None, "expert"),
            P("expert", None),
            P("dp", None, None),
            P("dp", None),
            P("dp", None, None),
        ),
        out_specs=(P("dp", None, "expert"), P("expert", None), P(("dp", "expert"), None)),
        check_vma=False,
    )
```

profile of v0, /device:TPU:1, one launch (start us, length us, event | category | flops | bytes accessed | tf_op | source)
XLA Modules:
  0.0 256.7 jit_solution(10256356855558854937)
XLA Ops:
  7.2 0.0 copy-start
  7.2 0.0 all-gather.2.cloned.1.call-start
  7.2 0.7 all-gather.2.cloned.1.call-update
  7.9 0.9 copy.14
  8.8 1.2 constant_dynamic-slice_fusion.1
  10.1 1.3 fusion.15
  12.7 0.9 dynamic-update-slice
  13.6 62.1 %all-reduce = bf16[256]{0:T(256)(128)(2,1)S(1)} all-reduce(bf16[256]{0:T(256)(128)(2,1)S(1)} %dynamic-update-slice), channel_id=1, replica_groups=mesh['dp'=16,'expert'=32] {'expert'}, use_global_device_ids=true, to_apply=%add | all-reduce | flops 256 | bytes 1024
  75.7 0.7 fusion.10
  76.4 1.2 gather_fusion.1
  77.6 0.7 iota_compare_fusion.2
  78.3 0.7 fusion.9
  79.0 0.7 select_convert_fusion.1
  79.7 20.2 %all-gather.2.cloned.1.call-done = bf16[256,7168]{1,0:T(8,128)(2,1)} async-done(((bf16[8,7168]{1,0:T(8,128)(2,1)}), bf16[256,7168]{1,0:T(8,128)(2,1)}) %all-gather.2.cloned.1.call-update) | async-done | bytes 3670032 | tf_op jit(solution)/shard_map/all_gather | solution.py:20
  99.8 7.1 %gather_fusion = bf16[128,7168]{1,0:T(8,128)(2,1)} fusion(bf16[256,7168]{1,0:T(8,128)(2,1)} %all-gather.2.cloned.1.call-done, s32[1024]{0:T(1024)S(1)} %pad_clamp_fusion), kind=kCustom, calls=%fused_computation | custom fusion | bytes 3670528 | tf_op jit(solution)/shard_map/jit(_take)/gather | solution.py:23
  106.9 4.2 %fusion.5 = f32[128,7168]{1,0:T(8,128)} fusion(bf16[1,128,128]{1,2,0:T(8,128)(2,1)S(1)} %copy.14, f32[128]{0:T(128)S(1)} %fusion.9, f32[128]{0:T(128)S(1)} %get-tuple-element.12, bf16[128,7168]{1,0:T(8,128)(2,1)} %gather_fusion, pred[128]{0:T(512)(128)(4,1)S(1)} %get-tuple-element.13, pred[128]{0:T(512)(128)(4,1)S(1)} %iota_compare_fusion.2), kind=kOutput, calls=%fused_computation.12 | convolution fusion | flops 239517696 | bytes 5539072 | tf_op jit(solution)/shard_map/dot_general | solution.py:32
  111.1 0.0 copy-done
  111.1 0.9 fusion.2
  112.0 0.2 fusion
  112.2 0.1 broadcast_multiply_fusion
  112.3 56.9 %all-reduce.1 = f32[256,2]{0,1:T(2,128)S(1)} all-reduce(f32[256,2]{0,1:T(2,128)S(1)} %broadcast_multiply_fusion), channel_id=2, replica_groups=mesh['dp'=16,'expert'=32] {'expert'}, use_global_device_ids=true, to_apply=%region_2.3.clone | all-reduce | flops 512 | bytes 4096
  169.2 0.7 copy.15
  169.9 79.3 %all-reduce.3 = bf16[128,7168]{1,0:T(8,128)(2,1)} all-reduce(f32[128,7168]{1,0:T(8,128)} %fusion.5), channel_id=1, replica_groups=mesh['dp'=16,'expert'=32] {'dp'}, use_global_device_ids=true, to_apply=%region_0.1 | all-reduce | flops 917504 | bytes 5505024 | tf_op jit(solution)/shard_map/psum | solution.py:35
  249.2 0.6 constant_dynamic-slice_fusion.3
  (5 shorter events, 0.0 us)
Async XLA Ops:
  7.2 104.0 %copy-start = (bf16[128,7168]{1,0:T(8,128)(2,1)S(1)}, bf16[128,7168]{1,0:T(8,128)(2,1)}, u32[]{:S(2)}) copy-start(bf16[128,7168]{1,0:T(8,128)(2,1)} %param.10) | copy-start | bytes 5505028
  7.2 92.6 %all-gather.2.cloned.1.call-start = ((), (), s32[]{:S(2)}) async-start(), calls=%async_computation | async-start | bytes 3784704 | tf_op jit(solution)/shard_map/all_gather | solution.py:20
  106.9 4.2 %copy-start.1 = (bf16[128,7168]{1,0:T(8,128)(2,1)S(1)}, bf16[128,7168]{1,0:T(8,128)(2,1)}, u32[]{:S(2)}) copy-start(bf16[128,7168]{1,0:T(8,128)(2,1)} %gather_fusion) | copy-start | bytes 5505028
Sparse Core Ops, SparseCore 0:
  11.2 88.5 all-gather.1
where the time goes:
time: 257 us
  blocking collectives  198 us (77%)
  waiting for transfers between devices  20.8 us (8%)
  between operations  15.4 us (6%)
  local copies, waits for them, and re-layouts  14.7 us (6%)
  matrix products  5.27 us (2%)
    unnamed x2, blocking collectives  119 us
    psum x1, blocking collectives, on_device(): weight_grad = lax.psum(weight_part, 'dp').astype(jnp.bfloat16)  79.3 us
    all_gather x1, waiting for transfers between devices, on_device(): lax.all_gather(grad_values, 'expert', axis=0, tiled=True)  20.2 us
    gather x1, local copies, waits for them, and re-layouts, on_device(): picked = jnp.take(values_all, slot_tok, axis=0).astype(jnp.float32)  7.1 us
  transfers between devices with their start and end apart: 1, of which 1 were waited for; matrix products, arithmetic and copies ran while one was open for 3% of the time, Pallas kernels for 0%

commit v1 on v0

v1 whole, which is shorter than its diff:
```python
import jax
import jax.numpy as jnp
from jax import lax
from jax.sharding import PartitionSpec as P

BF, F32 = jnp.bfloat16, jnp.float32


def on_device(grad_values, grad_scales, hidden_act, down_weight, slot_token, slot_count, slot_gate):
    nz, nc, ny, nx = (lax.axis_size(a) for a in "zcyx")
    experts = slot_token.shape[1]
    owner = lax.axis_index("y") // (ny // experts)
    rows, width = grad_values.shape
    group = rows * ny * nx
    pick = lambda a: lax.dynamic_index_in_dim(a[0], owner, 0, keepdims=False)
    tok, num, gate = pick(slot_token), pick(slot_count), pick(slot_gate)
    slots = tok.shape[0]
    live = jnp.arange(slots, dtype=jnp.int32) < num
    tok = jnp.where(live, tok, group)
    hidden = hidden_act[0]
    units = hidden.shape[1]

    scaled = (grad_values.astype(F32) * grad_scales.astype(F32)[:, None]).astype(BF)
    everything = lax.all_gather(scaled, ("y", "x"), axis=0, tiled=True)

    parts = nc * nx
    cols = width // parts
    send = scaled.reshape(rows, parts, cols).transpose(1, 0, 2)
    mine = lax.all_to_all(send, ("c", "x"), 0, 0)
    mine = mine.reshape(nc, nx * rows, cols)
    mine = lax.all_gather(mine, "y", axis=1, tiled=True)
    weighted = (gate[:, None] * hidden.astype(F32)).astype(BF)
    tok_row = jnp.broadcast_to(tok.astype(BF)[None, :], (16, slots))
    pack = jnp.concatenate([weighted, tok_row], axis=0)
    packs = lax.all_gather(pack, ("c", "x"), axis=0, tiled=False)
    packs = packs.reshape(nc, nx, slots + 16, units)
    toks = packs[:, 0, slots, :].astype(jnp.int32)
    pick_all = (toks[:, :, None] == jnp.arange(group, dtype=jnp.int32)).astype(BF)
    routed = jnp.einsum("gst,gtd->gsd", pick_all, mine, preferred_element_type=F32).astype(BF)
    part = jnp.einsum("gxsj,gsd->xjd", packs[:, :, :slots], routed, preferred_element_type=F32)
    per = units // nz
    part = part.astype(BF).reshape(nx, nz, per, cols).transpose(1, 0, 2, 3)
    got = lax.all_to_all(part.reshape(nz * nx, per, cols), ("z", "x"), 0, 0)
    total = jnp.sum(got.reshape(nz, nx, per, cols).astype(F32), axis=0).astype(BF)
    half = total.transpose(1, 0, 2).reshape(per, nx * cols)
    half = lax.all_gather(half, "z", axis=0, tiled=True)
    other = lax.ppermute(half, "c", [(i, nc - 1 - i) for i in range(nc)])
    first = lax.axis_index("c") == 0
    weight_grad = jnp.concatenate(
        [jnp.where(first, half, other), jnp.where(first, other, half)], axis=1
    )

    everything, half = lax.optimization_barrier((everything, half))
    dims = (((1,), (1,)), ((), ()))
    by_token = lax.dot_general(everything, down_weight, dims, preferred_element_type=F32)
    onehot = (tok[:, None] == jnp.arange(group, dtype=jnp.int32)).astype(F32)
    project = jnp.dot(onehot, by_token, precision=lax.Precision.HIGHEST)
    hidden_grad = (gate[:, None] * project).astype(BF)[None]
    partial = jnp.sum(hidden.astype(F32) * project, axis=1)
    per_token = jnp.dot(partial, onehot, precision=lax.Precision.HIGHEST)
    spread = lax.all_to_all(per_token.reshape(ny * nx, rows), ("y", "x"), 0, 0)
    gate_grad = spread.reshape(experts, -1, rows).sum(axis=1).T
    return hidden_grad, weight_grad, gate_grad


def solution(mesh):
    fine = jax.sharding.Mesh(mesh.devices.reshape(8, 2, 8, 4), ("z", "c", "y", "x"))
    dp, expert = ("z", "c"), ("y", "x")
    return jax.shard_map(
        on_device,
        mesh=fine,
        in_specs=(
            P(dp + expert, None),
            P(dp + expert),
            P(dp, None, expert),
            P(expert, None),
            P(dp, None, None),
            P(dp, None),
            P(dp, None, None),
        ),
        out_specs=(P(dp, None, expert), P(expert, None), P(dp + expert, None)),
        check_vma=False,
    )
```

time: 257 us -> 172 us (0.67)
  blocking collectives: 198 us -> 97.9 us
  starting transfers between devices: 0.04 us -> 31.6 us
  waiting for transfers between devices: 20.8 us -> 7.34 us
  local copies, waits for them, and re-layouts: 14.7 us -> 3.8 us
  other arithmetic: 2.11 us -> 9.54 us
    unnamed x2 -> x0, blocking collectives: 119 us -> none
    psum x1 -> x0, blocking collectives: 79.3 us -> none  [on_device(): weight_grad = lax.psum(weight_part, 'dp').astype(jnp.bfloat16)]
    all_gather x0 -> x3, blocking collectives: none -> 67.6 us  [the longest x1 23.3 us: on_device(): mine = lax.all_gather(mine, 'y', axis=1, tiled=True)]
    all_to_all x0 -> x1, blocking collectives: none -> 30.2 us  [on_device(): got = lax.all_to_all(part.reshape(nz * nx, per, cols), ('z', 'x'), 0, 0)]
    all_gather x1, waiting for transfers between devices: 20.2 us -> 0.01 us  [on_device(): everything = lax.all_gather(scaled, ('y', 'x'), axis=0, tiled=True)]
    all_to_all x0 -> x2, starting transfers between devices: none -> 17.7 us  [the longest x1 10.2 us: on_device(): mine = lax.all_to_all(send, ('c', 'x'), 0, 0)]
    ppermute x0 -> x1, starting transfers between devices: none -> 13.9 us  [on_device(): other = lax.ppermute(half, 'c', [(i, nc - 1 - i) for i in range(nc)])]
    gather x2 -> x0, local copies, waits for them, and re-layouts: 8.33 us -> none  [the longest x1 7.1 us: on_device(): picked = jnp.take(values_all, slot_tok, axis=0).astype(jnp.float32)]
  transfers between devices with their start and end apart: 1 -> 4, of which waited for: 1 -> 2; matrix products, arithmetic and copies ran while one was open for 3% -> 7% of each run, Pallas kernels for 0% -> 0%
where the time goes in v1:
time: 172 us; the launch traced here: 171 us
  blocking collectives  97.9 us (57%)
  starting transfers between devices  31.6 us (18%)
  between operations  14.2 us (8%)
  other arithmetic  9.54 us (6%)
  waiting for transfers between devices  7.34 us (4%)
  matrix products  7.03 us (4%)
  local copies, waits for them, and re-layouts  3.8 us (2%)
    all_to_all x1, blocking collectives, on_device(): got = lax.all_to_all(part.reshape(nz * nx, per, cols), ('z', 'x'), 0, 0)  30.2 us
    all_gather x1, blocking collectives, on_device(): mine = lax.all_gather(mine, 'y', axis=1, tiled=True)  23.3 us
    all_gather x1, blocking collectives, on_device(): packs = lax.all_gather(pack, ('c', 'x'), axis=0, tiled=False)  22.8 us
    all_gather x1, blocking collectives, on_device(): half = lax.all_gather(half, 'z', axis=0, tiled=True)  21.5 us
    ppermute x1, starting transfers between devices, on_device(): other = lax.ppermute(half, 'c', [(i, nc - 1 - i) for i in range(nc)])  13.9 us
    all_to_all x1, starting transfers between devices, on_device(): mine = lax.all_to_all(send, ('c', 'x'), 0, 0)  10.2 us
    all_to_all x1, starting transfers between devices, on_device(): spread = lax.all_to_all(per_token.reshape(ny * nx, rows), ('y', 'x'), 0, 0)  7.49 us
    all_to_all x1, waiting for transfers between devices, on_device(): spread = lax.all_to_all(per_token.reshape(ny * nx, rows), ('y', 'x'), 0, 0)  5.14 us
  transfers between devices with their start and end apart: 4, of which 2 were waited for; matrix products, arithmetic and copies ran while one was open for 7% of the time, Pallas kernels for 0%

profile of v1, /device:TPU:1, one launch (start us, length us, event | category | flops | bytes accessed | tf_op | source)
XLA Modules:
  0.0 171.3 jit_solution(6518803708008005702)
XLA Ops:
  7.2 0.8 convert_element_type.50
  8.0 1.6 multiply_convert_fusion
  9.7 10.2 %all-to-all-start = ((bf16[8,8,896]{2,1,0:T(8,128)(2,1)}), bf16[8,8,896]{2,1,0:T(8,128)(2,1)S(1)}, u32[]{:S(2)}, u32[]{:S(2)}) async-start(bf16[8,8,896]{2,1,0:T(8,128)(2,1)} %bitcast.59), calls=%async_computation | async-start | bytes 229376 | tf_op jit(solution)/shard_map/all_to_all | solution.py:29
  19.8 0.9 copy.22
  20.7 1.2 constant_dynamic-slice_fusion.1
  22.0 0.7 fusion.12
  22.6 1.3 fusion.15
  24.2 22.8 %all-gather = bf16[1152,128]{1,0:T(8,128)(2,1)S(1)} all-gather(bf16[144,128]{1,0:T(8,128)(2,1)S(1)} %copy.23), channel_id=2, replica_groups=mesh['z'=8,'c'=2,'y'=8,'x'=4] {'c','x'}, dimensions={0}, use_global_device_ids=true | all-gather | bytes 331776 | tf_op jit(solution)/shard_map/all_gather | solution.py:35
  47.1 23.3 %all_gather.18 = bf16[2,256,896]{2,1,0:T(8,128)(2,1)} all-gather(bf16[2,32,896]{2,1,0:T(8,128)(2,1)S(1)} %bitcast.61), channel_id=1, replica_groups=mesh['z'=8,'c'=2,'y'=8,'x'=4] {'y'}, dimensions={1}, use_global_device_ids=true | all-gather | bytes 1032192 | tf_op jit(solution)/shard_map/all_gather | solution.py:31
  70.4 1.9 %bitcast_convert_fusion = bf16[4,128,896]{2,1,0:T(8,128)(2,1)S(1)} fusion(bf16[2,256,896]{2,1,0:T(8,128)(2,1)} %all_gather.18, bf16[2,4,144,128]{3,2,1,0:T(8,128)(2,1)S(1)} %bitcast.58, s32[2,128]{1,0:T(2,128)S(1)} %bitcast.64), kind=kOutput, calls=%fused_computation | convolution fusion | flops 353075200 | bytes 2098176 | tf_op jit(solution)/shard_map/gxsj,gsd->xjd/dot_general | solution.py:40
  72.4 30.2 %all_to_all.19 = bf16[32,16,896]{2,1,0:T(8,128)(2,1)S(1)} all-to-all(bf16[32,16,896]{2,1,0:T(8,128)(2,1)S(1)} %bitcast.55), channel_id=1, replica_groups=mesh['z'=8,'c'=2,'y'=8,'x'=4] {'z','x'}, dimensions={0} | all-to-all | bytes 1835008 | tf_op jit(solution)/shard_map/all_to_all | solution.py:43
  102.6 0.1 reduce_sum.30
  102.8 21.5 %all_gather.19 = bf16[128,3584]{1,0:T(8,128)(2,1)S(1)} all-gather(bf16[16,3584]{1,0:T(8,128)(2,1)S(1)} %bitcast.62), channel_id=1, replica_groups=mesh['z'=8,'c'=2,'y'=8,'x'=4] {'z'}, dimensions={0}, use_global_device_ids=true | all-gather | bytes 1032192 | tf_op jit(solution)/shard_map/all_gather | solution.py:46
  124.2 13.9 %collective-permute-start = (bf16[128,3584]{1,0:T(8,128)(2,1)S(1)}, bf16[128,3584]{1,0:T(8,128)(2,1)}, u32[]{:S(2)}, u32[]{:S(2)}) collective-permute-start(bf16[128,3584]{1,0:T(8,128)(2,1)S(1)} %all_gather.19), channel_id=1, source_target_pairs={{0,32},{32,0},{1,33},{33,1},{2,34},{34,2},{3,35},{35,3},{4,36},{36... | collective-permute-start | bytes 2752520 | tf_op jit(solution)/shard_map/ppermute | solution.py:47
  138.1 2.2 %collective-permute-done = bf16[128,3584]{1,0:T(8,128)(2,1)} collective-permute-done((bf16[128,3584]{1,0:T(8,128)(2,1)S(1)}, bf16[128,3584]{1,0:T(8,128)(2,1)}, u32[]{:S(2)}, u32[]{:S(2)}) %collective-permute-start) | collective-permute-done | bytes 917536 | tf_op jit(solution)/shard_map/ppermute | solution.py:47
  140.3 2.5 %broadcast_select_fusion.1 = (bf16[128,3584]{1,0:T(8,128)(2,1)S(1)}, bf16[128,3584]{1,0:T(8,128)(2,1)}) fusion(bf16[128,3584]{1,0:T(8,128)(2,1)} %copy-done.1, bf16[128,3584]{1,0:T(8,128)(2,1)} %collective-permute-done, pred[]{:T(512)S(6)} %eq.53), kind=kLoop, calls=%fused_computation.6 | loop fusion | flops 917504 | bytes 3670017 | tf_op jit(solution)/shard_map/jit(_where)/select_n | solution.py:50
  142.8 3.1 %fusion.16 = f32[256,128]{1,0:T(8,128)S(1)} fusion(bf16[256,7168]{1,0:T(8,128)(2,1)} %all-gather.3.cloned.1.call-done, bf16[128,7168]{1,0:T(8,128)(2,1)S(1)} %copy-done), kind=kOutput, calls=%fused_computation.35 | convolution fusion | flops 469762048 | bytes 5636096 | tf_op jit(solution)/shard_map/dot_general | solution.py:55
  146.0 0.3 fusion.7
  146.3 1.6 convolution_bitcast_fusion
  147.9 7.5 %all-to-all-start.2 = ((f32[32,1,8]{2,1,0:T(1,128)}), f32[32,1,8]{2,1,0:T(1,128)S(1)}, u32[]{:S(2)}, u32[]{:S(2)}) async-start(f32[32,1,8]{2,1,0:T(1,128)} %convolution_bitcast_fusion), calls=%async_computation.2 | async-start | bytes 32768 | tf_op jit(solution)/shard_map/all_to_all | solution.py:61
  155.4 2.6 %pad_maximum_fusion = bf16[128,7168]{1,0:T(8,128)(2,1)} fusion(bf16[128,3584]{1,0:T(8,128)(2,1)} %get-tuple-element.20, bf16[128,3584]{1,0:T(8,128)(2,1)S(1)} %get-tuple-element.19), kind=kLoop, calls=%fused_computation.1 | loop fusion | flops 3670016 | bytes 3670016 | tf_op jit(solution)/shard_map/concatenate | solution.py:49
  158.0 0.7 copy.27
  158.7 5.1 %all-to-all-done.2 = f32[32,1,8]{2,1,0:T(1,128)S(1)} async-done(((f32[32,1,8]{2,1,0:T(1,128)}), f32[32,1,8]{2,1,0:T(1,128)S(1)}, u32[]{:S(2)}, u32[]{:S(2)}) %all-to-all-start.2) | async-done | bytes 1056 | tf_op jit(solution)/shard_map/all_to_all | solution.py:61
  163.9 0.6 bitcast_reduce_fusion
  (16 shorter events, 0.4 us)
Async XLA Ops:
  7.2 135.6 %copy-start = (bf16[128,7168]{1,0:T(8,128)(2,1)S(1)}, bf16[128,7168]{1,0:T(8,128)(2,1)}, u32[]{:S(2)}) copy-start(bf16[128,7168]{1,0:T(8,128)(2,1)} %param.10) | copy-start | bytes 5505028
  7.2 135.6 %all-gather.3.cloned.1.call-start = ((), (), s32[]{:S(2)}) async-start(), calls=%async_computation.3 | async-start | bytes 3784704 | tf_op jit(solution)/shard_map/all_gather | solution.py:24
  9.7 37.4 %all-to-all-start = ((bf16[8,8,896]{2,1,0:T(8,128)(2,1)}), bf16[8,8,896]{2,1,0:T(8,128)(2,1)S(1)}, u32[]{:S(2)}, u32[]{:S(2)}) async-start(bf16[8,8,896]{2,1,0:T(8,128)(2,1)} %bitcast.59), calls=%async_computation | async-start | bytes 229376 | tf_op jit(solution)/shard_map/all_to_all | solution.py:29
  124.2 13.9 %copy-start.1 = (bf16[128,3584]{1,0:T(8,128)(2,1)}, bf16[128,3584]{1,0:T(8,128)(2,1)S(1)}, u32[]{:S(2)}) copy-start(bf16[128,3584]{1,0:T(8,128)(2,1)S(1)} %all_gather.19) | copy-start | bytes 2752516
  124.2 16.1 %collective-permute-start = (bf16[128,3584]{1,0:T(8,128)(2,1)S(1)}, bf16[128,3584]{1,0:T(8,128)(2,1)}, u32[]{:S(2)}, u32[]{:S(2)}) collective-permute-start(bf16[128,3584]{1,0:T(8,128)(2,1)S(1)} %all_gather.19), channel_id=1, source_target_pairs={{0,32},{32,0},{1,33},{33,1},{2,34},{34,2},{3,35},{35,3},{4,36},{36... | collective-permute-start | bytes 2752520 | tf_op jit(solution)/shard_map/ppermute | solution.py:47
  147.9 15.9 %all-to-all-start.2 = ((f32[32,1,8]{2,1,0:T(1,128)}), f32[32,1,8]{2,1,0:T(1,128)S(1)}, u32[]{:S(2)}, u32[]{:S(2)}) async-start(f32[32,1,8]{2,1,0:T(1,128)} %convolution_bitcast_fusion), calls=%async_computation.2 | async-start | bytes 32768 | tf_op jit(solution)/shard_map/all_to_all | solution.py:61
Sparse Core Ops, SparseCore 0:
  11.2 88.5 all-gather.2

commit v2 on v1

v2 whole, which is shorter than its diff:
```python
import jax
import jax.numpy as jnp
from jax import lax
from jax.sharding import PartitionSpec as P

BF, F32 = jnp.bfloat16, jnp.float32
DP, EXPERT = ("z", "c"), ("e", "q", "x")


def on_device(grad_values, grad_scales, hidden_act, down_weight, slot_token, slot_count, slot_gate):
    nz, nc, ne, nq, nx = (lax.axis_size(a) for a in "zceqx")
    core, owner = lax.axis_index("c"), lax.axis_index("e")
    rows, width = grad_values.shape
    ny = ne * nq
    group = rows * ny * nx
    pick = lambda a: lax.dynamic_index_in_dim(a[0], owner, 0, keepdims=False)
    tok, num, gate = pick(slot_token), pick(slot_count), pick(slot_gate)
    slots = tok.shape[0]
    live = jnp.arange(slots, dtype=jnp.int32) < num
    tok = jnp.where(live, tok, group)
    hidden = hidden_act[0]
    units = hidden.shape[1]
    cols = width // (nc * nq)

    scaled = (grad_values.astype(F32) * grad_scales.astype(F32)[:, None]).astype(BF)
    send = scaled.reshape(rows, nc, 1, nq, cols).transpose(1, 2, 3, 0, 4)
    send = jnp.broadcast_to(send, (nc, ne, nq, rows, cols)).reshape(-1, rows, cols)
    mine = lax.all_to_all(send, ("c", "e", "q"), 0, 0)

    weighted = (gate[:, None] * hidden.astype(F32)).astype(BF)
    tok_row = jnp.broadcast_to(tok.astype(BF)[None, :], (16, slots))
    pack = jnp.concatenate([weighted, tok_row], axis=0)
    packs = jnp.broadcast_to(pack[None], (nc * nq,) + pack.shape)
    packs = lax.all_to_all(packs, ("c", "q"), 0, 0)

    own_cols = lax.dynamic_slice_in_dim(down_weight, core * (nq * cols), nq * cols, 1)
    own_cols = own_cols.reshape(units, nq, cols).transpose(1, 0, 2)
    own_cols, mine = lax.optimization_barrier((own_cols, mine))
    w_cols = lax.all_to_all(own_cols, "q", 0, 0)

    mine = mine.reshape(nc, ny * rows, cols)
    mine = lax.all_gather(mine, "x", axis=1, tiled=True)
    ids = jnp.arange(group, dtype=jnp.int32).reshape(ny, nx, rows)
    ids = ids.transpose(1, 0, 2).reshape(-1)

    packs = packs.reshape(nc, nq, slots + 16, units)
    toks = packs[:, 0, slots, :].astype(jnp.int32)
    pick_all = (toks[:, :, None] == ids).astype(BF)
    routed = jnp.einsum("gst,gtd->gsd", pick_all, mine, preferred_element_type=F32).astype(BF)
    part = jnp.einsum("gqsj,gsd->qjd", packs[:, :, :slots], routed, preferred_element_type=F32)
    per = units // nz
    part = part.astype(BF).reshape(nq, nz, per, cols).transpose(1, 0, 2, 3)
    got = lax.all_to_all(part, "z", 0, 0)

    proj = jnp.einsum("gsd,qjd->gqsj", routed, w_cols, preferred_element_type=F32).astype(BF)
    proj = lax.all_to_all(proj.reshape(nc * nq, slots, units), ("c", "q"), 0, 0)

    total = jnp.sum(got.astype(F32), axis=0).astype(BF)
    total = lax.all_to_all(total, "q", 0, 0)
    half = total.transpose(1, 0, 2).reshape(per, nq * cols)

    project = jnp.sum(proj.astype(F32), axis=0)
    hidden_grad = (gate[:, None] * project).astype(BF)[None]
    partial = jnp.sum(hidden.astype(F32) * project, axis=1)
    onehot = (tok[:, None] == jnp.arange(group, dtype=jnp.int32)).astype(F32)
    per_token = jnp.dot(partial, onehot, precision=lax.Precision.HIGHEST)
    spread = lax.all_to_all(per_token.reshape(ny * nx, rows), EXPERT, 0, 0)
    gate_grad = spread.reshape(ne, -1, rows).sum(axis=1).T

    half = lax.all_gather(half, "z", axis=0, tiled=True)
    cut = units // 2
    weight_grad = jnp.concatenate(
        [lax.all_gather(half[i : i + cut], "c", axis=1, tiled=True) for i in (0, cut)], axis=0
    )
    return hidden_grad, weight_grad, gate_grad


def solution(mesh):
    fine = jax.sharding.Mesh(mesh.devices.reshape(8, 2, 2, 4, 4), DP + EXPERT)
    return jax.shard_map(
        on_device,
        mesh=fine,
        in_specs=(
            P(DP + EXPERT, None),
            P(DP + EXPERT),
            P(DP, None, EXPERT),
            P(EXPERT, None),
            P(DP, None, None),
            P(DP, None),
            P(DP, None, None),
        ),
        out_specs=(P(DP, None, EXPERT), P(EXPERT, None), P(DP + EXPERT, None)),
        check_vma=False,
    )
```

time: 172 us -> 175 us (1.017)
  waiting for transfers between devices: 7.34 us -> 64.3 us
  blocking collectives: 97.9 us -> 46.2 us
  between operations: 14.2 us -> 0.78 us
  starting transfers between devices: 31.6 us -> 41.8 us
  local copies, waits for them, and re-layouts: 3.8 us -> 9.21 us
  matrix products: 7.03 us -> 4.11 us
  other arithmetic: 9.54 us -> 7.53 us
    all_to_all x2 -> x7, waiting for transfers between devices: 5.14 us -> 64.3 us  [the longest x1 24.5 us: on_device(): got = lax.all_to_all(part, 'z', 0, 0)]
    all_to_all x1 -> x0, blocking collectives: 30.2 us -> none  [on_device(): got = lax.all_to_all(part.reshape(nz * nx, per, cols), ('z', 'x'), 0, 0)]
    all_to_all x2 -> x7, starting transfers between devices: 17.7 us -> 41.8 us  [the longest x1 10.2 us: on_device(): mine = lax.all_to_all(send, ('c', 'e', 'q'), 0, 0)]
    all_gather x2 -> x3, blocking collectives: 46.2 us -> 25 us  [the longest x2 12.7 us: on_device(): lax.all_gather(half[i:i + cut], 'c', axis=1, tiled=True)]
    ppermute x1 -> x0, starting transfers between devices: 13.9 us -> none  [on_device(): other = lax.ppermute(half, 'c', [(i, nc - 1 - i) for i in range(nc)])]
    dot_general x3, matrix products: 5.38 us -> 2.45 us  [the longest x1 1.65 us: on_device(): jnp.einsum('gsd,qjd->gqsj', routed, w_cols, preferred_element_type=F32)]
    select_n x1 -> x0, other arithmetic: 2.49 us -> none  [on_device(): jnp.where(first, half, other)]
    reshape x2 -> x4, local copies, waits for them, and re-layouts: 0.1 us -> 2.38 us  [the longest x1 1.28 us: on_device(): own_cols = own_cols.reshape(units, nq, cols).transpose(1, 0, 2)]
  transfers between devices with their start and end apart: 4 -> 7, of which waited for: 2 -> 7; matrix products, arithmetic and copies ran while one was open for 7% -> 8% of each run, Pallas kernels for 0% -> 0%
where the time goes in v2:
time: 175 us; the launch traced here: 174 us
  waiting for transfers between devices  64.3 us (37%)
  blocking collectives  46.2 us (26%)
  starting transfers between devices  41.8 us (24%)
  local copies, waits for them, and re-layouts  9.21 us (5%)
  other arithmetic  7.53 us (4%)
  matrix products  4.11 us (2%)
    all_to_all x1, waiting for transfers between devices, on_device(): got = lax.all_to_all(part, 'z', 0, 0)  24.5 us
    all_gather x1, blocking collectives, on_device(): half = lax.all_gather(half, 'z', axis=0, tiled=True)  21.2 us
    all_gather x2, blocking collectives, on_device(): lax.all_gather(half[i:i + cut], 'c', axis=1, tiled=True)  12.7 us
    all_gather x1, blocking collectives, on_device(): mine = lax.all_gather(mine, 'x', axis=1, tiled=True)  12.2 us
    all_to_all x1, starting transfers between devices, on_device(): mine = lax.all_to_all(send, ('c', 'e', 'q'), 0, 0)  10.2 us
    all_to_all x1, waiting for transfers between devices, on_device(): w_cols = lax.all_to_all(own_cols, 'q', 0, 0)  10.1 us
    all_to_all x1, starting transfers between devices, on_device(): got = lax.all_to_all(part, 'z', 0, 0)  8.41 us
    all_to_all x1, waiting for transfers between devices, on_device(): spread = lax.all_to_all(per_token.reshape(ny * nx, rows), EXPERT, 0, 0)  7.73 us
  transfers between devices with their start and end apart: 7, of which 7 were waited for; matrix products, arithmetic and copies ran while one was open for 8% of the time, Pallas kernels for 0%

profile of v2, /device:TPU:1, one launch (start us, length us, event | category | flops | bytes accessed | tf_op | source)
XLA Modules:
  0.0 173.9 jit_solution(14228976102330441567)
XLA Ops:
  3.1 10.2 %all-to-all-start = ((bf16[16,8,896]{2,1,0:T(8,128)(2,1)}), bf16[16,8,896]{2,1,0:T(8,128)(2,1)S(1)}, u32[]{:S(2)}, u32[]{:S(2)}) async-start(bf16[16,8,896]{2,1,0:T(8,128)(2,1)} %bitcast.6), calls=%async_computation | async-start | bytes 458752 | tf_op jit(solution)/shard_map/all_to_all | solution.py:28
  14.6 1.3 fusion.17
  17.5 5.0 %all-to-all-done = bf16[16,8,896]{2,1,0:T(8,128)(2,1)S(1)} async-done(((bf16[16,8,896]{2,1,0:T(8,128)(2,1)}), bf16[16,8,896]{2,1,0:T(8,128)(2,1)S(1)}, u32[]{:S(2)}, u32[]{:S(2)}) %all-to-all-start) | async-done | bytes 229408 | tf_op jit(solution)/shard_map/all_to_all | solution.py:28
  23.2 4.8 %all-to-all-start.2 = ((bf16[8,144,128]{2,1,0:T(8,128)(2,1)}), bf16[8,144,128]{2,1,0:T(8,128)(2,1)S(1)}, u32[]{:S(2)}, u32[]{:S(2)}) async-start(bf16[8,144,128]{2,1,0:T(8,128)(2,1)} %broadcast_in_dim.16), calls=%async_computation.2 | async-start | bytes 589824 | tf_op jit(solution)/shard_map/all_to_all | solution.py:34
  29.0 1.5 copy.31
  30.5 1.3 copy.21
  31.8 5.9 %all-to-all-done.2 = bf16[8,144,128]{2,1,0:T(8,128)(2,1)S(1)} async-done(((bf16[8,144,128]{2,1,0:T(8,128)(2,1)}), bf16[8,144,128]{2,1,0:T(8,128)(2,1)S(1)}, u32[]{:S(2)}, u32[]{:S(2)}) %all-to-all-start.2) | async-done | bytes 294944 | tf_op jit(solution)/shard_map/all_to_all | solution.py:34
  37.8 4.2 %all-to-all-start.1 = ((bf16[4,128,896]{2,1,0:T(8,128)(2,1)}), bf16[4,128,896]{2,1,0:T(8,128)(2,1)}, u32[]{:S(2)}, u32[]{:S(2)}) async-start(bf16[4,128,896]{2,1,0:T(8,128)(2,1)} %bitcast.2), calls=%async_computation.1 | async-start | bytes 1835008 | tf_op jit(solution)/shard_map/all_to_all | solution.py:39
  42.1 12.2 %all_gather.12 = bf16[2,256,896]{2,1,0:T(8,128)(2,1)S(1)} all-gather(bf16[2,64,896]{2,1,0:T(8,128)(2,1)S(1)} %bitcast.71), channel_id=1, replica_groups=mesh['z'=8,'c'=2,'e'=2,'q'=4,'x'=4] {'x'}, dimensions={1}, use_global_device_ids=true | all-gather | bytes 1146880 | tf_op jit(solution)/shard_map/all_gather | solution.py:42
  54.7 10.1 %all-to-all-done.1 = bf16[4,128,896]{2,1,0:T(8,128)(2,1)} async-done(((bf16[4,128,896]{2,1,0:T(8,128)(2,1)}), bf16[4,128,896]{2,1,0:T(8,128)(2,1)}, u32[]{:S(2)}, u32[]{:S(2)}) %all-to-all-start.1) | async-done | bytes 917536 | tf_op jit(solution)/shard_map/all_to_all | solution.py:39
  64.8 1.6 fusion
  67.3 4.4 %all-to-all-start.3 = ((bf16[8,128,128]{2,1,0:T(8,128)(2,1)}), bf16[8,128,128]{2,1,0:T(8,128)(2,1)S(1)}, u32[]{:S(2)}, u32[]{:S(2)}) async-start(bf16[8,128,128]{2,1,0:T(8,128)(2,1)} %bitcast.17), calls=%async_computation.3 | async-start | bytes 524288 | tf_op jit(solution)/shard_map/all_to_all | solution.py:56
  73.2 7.6 %all-to-all-done.3 = bf16[8,128,128]{2,1,0:T(8,128)(2,1)S(1)} async-done(((bf16[8,128,128]{2,1,0:T(8,128)(2,1)}), bf16[8,128,128]{2,1,0:T(8,128)(2,1)S(1)}, u32[]{:S(2)}, u32[]{:S(2)}) %all-to-all-start.3) | async-done | bytes 262176 | tf_op jit(solution)/shard_map/all_to_all | solution.py:56
  80.8 8.4 %all-to-all-start.4 = ((bf16[8,4,16,896]{3,2,1,0:T(8,128)(2,1)}), bf16[8,4,16,896]{3,2,1,0:T(8,128)(2,1)S(1)}, u32[]{:S(2)}, u32[]{:S(2)}) async-start(bf16[8,4,16,896]{3,2,1,0:T(8,128)(2,1)} %bitcast.66), calls=%async_computation.4 | async-start | bytes 1835008 | tf_op jit(solution)/shard_map/all_to_all | solution.py:53
  89.4 1.7 convolution_bitcast_fusion
  91.0 24.5 %all-to-all-done.4 = bf16[8,4,16,896]{3,2,1,0:T(8,128)(2,1)S(1)} async-done(((bf16[8,4,16,896]{3,2,1,0:T(8,128)(2,1)}), bf16[8,4,16,896]{3,2,1,0:T(8,128)(2,1)S(1)}, u32[]{:S(2)}, u32[]{:S(2)}) %all-to-all-start.4) | async-done | bytes 917536 | tf_op jit(solution)/shard_map/all_to_all | solution.py:53
  115.6 6.4 %all-to-all-start.6 = ((f32[32,1,8]{2,1,0:T(1,128)}), f32[32,1,8]{2,1,0:T(1,128)S(1)}, u32[]{:S(2)}, u32[]{:S(2)}) async-start(f32[32,1,8]{2,1,0:T(1,128)} %convolution_bitcast_fusion), calls=%async_computation.6 | async-start | bytes 32768 | tf_op jit(solution)/shard_map/all_to_all | solution.py:67
  122.8 7.7 %all-to-all-done.6 = f32[32,1,8]{2,1,0:T(1,128)S(1)} async-done(((f32[32,1,8]{2,1,0:T(1,128)}), f32[32,1,8]{2,1,0:T(1,128)S(1)}, u32[]{:S(2)}, u32[]{:S(2)}) %all-to-all-start.6) | async-done | bytes 1056 | tf_op jit(solution)/shard_map/all_to_all | solution.py:67
  130.5 3.3 %all-to-all-start.5 = ((bf16[4,16,896]{2,1,0:T(8,128)(2,1)}), bf16[4,16,896]{2,1,0:T(8,128)(2,1)S(1)}, u32[]{:S(2)}, u32[]{:S(2)}) async-start(bf16[4,16,896]{2,1,0:T(8,128)(2,1)} %reduce_sum.43), calls=%async_computation.5 | async-start | bytes 229376 | tf_op jit(solution)/shard_map/all_to_all | solution.py:59
  135.1 3.4 %all-to-all-done.5 = bf16[4,16,896]{2,1,0:T(8,128)(2,1)S(1)} async-done(((bf16[4,16,896]{2,1,0:T(8,128)(2,1)}), bf16[4,16,896]{2,1,0:T(8,128)(2,1)S(1)}, u32[]{:S(2)}, u32[]{:S(2)}) %all-to-all-start.5) | async-done | bytes 114720 | tf_op jit(solution)/shard_map/all_to_all | solution.py:59
  138.5 21.2 %all_gather.13 = bf16[128,3584]{1,0:T(8,128)(2,1)S(1)} all-gather(bf16[16,3584]{1,0:T(8,128)(2,1)S(1)} %bitcast.74), channel_id=1, replica_groups=mesh['z'=8,'c'=2,'e'=2,'q'=4,'x'=4] {'z'}, dimensions={0}, use_global_device_ids=true | all-gather | bytes 1032192 | tf_op jit(solution)/shard_map/all_gather | solution.py:70
  159.8 10.3 %all_gather.14 = bf16[64,7168]{1,0:T(8,128)(2,1)S(1)} all-gather(bf16[64,3584]{1,0:T(8,128)(2,1)S(1)} %get-tuple-element.9), channel_id=1, replica_groups=mesh['z'=8,'c'=2,'e'=2,'q'=4,'x'=4] {'c'}, dimensions={1}, use_global_device_ids=true | all-gather | bytes 1376256 | tf_op jit(solution)/shard_map/all_gather | solution.py:73
  170.1 2.5 %all_gather.15 = bf16[64,7168]{1,0:T(8,128)(2,1)S(1)} all-gather(bf16[64,3584]{1,0:T(8,128)(2,1)S(1)} %get-tuple-element.10), channel_id=1, replica_groups=mesh['z'=8,'c'=2,'e'=2,'q'=4,'x'=4] {'c'}, dimensions={1}, use_global_device_ids=true | all-gather | bytes 1376256 | tf_op jit(solution)/shard_map/all_gather | solution.py:73
  172.5 1.4 pad_maximum_fusion
  (29 shorter events, 12.0 us)
Async XLA Ops:
  0.6 27.4 %copy-start = (bf16[128,7168]{1,0:T(8,128)(2,1)S(1)}, bf16[128,7168]{1,0:T(8,128)(2,1)}, u32[]{:S(2)}) copy-start(bf16[128,7168]{1,0:T(8,128)(2,1)} %param.10) | copy-start | bytes 5505028
  3.1 19.3 %all-to-all-start = ((bf16[16,8,896]{2,1,0:T(8,128)(2,1)}), bf16[16,8,896]{2,1,0:T(8,128)(2,1)S(1)}, u32[]{:S(2)}, u32[]{:S(2)}) async-start(bf16[16,8,896]{2,1,0:T(8,128)(2,1)} %bitcast.6), calls=%async_computation | async-start | bytes 458752 | tf_op jit(solution)/shard_map/all_to_all | solution.py:28
  23.2 14.6 %all-to-all-start.2 = ((bf16[8,144,128]{2,1,0:T(8,128)(2,1)}), bf16[8,144,128]{2,1,0:T(8,128)(2,1)S(1)}, u32[]{:S(2)}, u32[]{:S(2)}) async-start(bf16[8,144,128]{2,1,0:T(8,128)(2,1)} %broadcast_in_dim.16), calls=%async_computation.2 | async-start | bytes 589824 | tf_op jit(solution)/shard_map/all_to_all | solution.py:34
  37.8 27.0 %all-to-all-start.1 = ((bf16[4,128,896]{2,1,0:T(8,128)(2,1)}), bf16[4,128,896]{2,1,0:T(8,128)(2,1)}, u32[]{:S(2)}, u32[]{:S(2)}) async-start(bf16[4,128,896]{2,1,0:T(8,128)(2,1)} %bitcast.2), calls=%async_computation.1 | async-start | bytes 1835008 | tf_op jit(solution)/shard_map/all_to_all | solution.py:39
  67.3 13.5 %all-to-all-start.3 = ((bf16[8,128,128]{2,1,0:T(8,128)(2,1)}), bf16[8,128,128]{2,1,0:T(8,128)(2,1)S(1)}, u32[]{:S(2)}, u32[]{:S(2)}) async-start(bf16[8,128,128]{2,1,0:T(8,128)(2,1)} %bitcast.17), calls=%async_computation.3 | async-start | bytes 524288 | tf_op jit(solution)/shard_map/all_to_all | solution.py:56
  72.2 17.1 %copy-start.1 = (bf16[1,128,128]{2,1,0:T(8,128)(2,1)S(1)}, bf16[1,128,128]{2,1,0:T(8,128)(2,1)}, u32[]{:S(2)}) copy-start(bf16[1,128,128]{2,1,0:T(8,128)(2,1)} %param.9) | copy-start | bytes 98308
  80.8 34.8 %all-to-all-start.4 = ((bf16[8,4,16,896]{3,2,1,0:T(8,128)(2,1)}), bf16[8,4,16,896]{3,2,1,0:T(8,128)(2,1)S(1)}, u32[]{:S(2)}, u32[]{:S(2)}) async-start(bf16[8,4,16,896]{3,2,1,0:T(8,128)(2,1)} %bitcast.66), calls=%async_computation.4 | async-start | bytes 1835008 | tf_op jit(solution)/shard_map/all_to_all | solution.py:53
  115.6 14.9 %all-to-all-start.6 = ((f32[32,1,8]{2,1,0:T(1,128)}), f32[32,1,8]{2,1,0:T(1,128)S(1)}, u32[]{:S(2)}, u32[]{:S(2)}) async-start(f32[32,1,8]{2,1,0:T(1,128)} %convolution_bitcast_fusion), calls=%async_computation.6 | async-start | bytes 32768 | tf_op jit(solution)/shard_map/all_to_all | solution.py:67
  130.5 8.0 %all-to-all-start.5 = ((bf16[4,16,896]{2,1,0:T(8,128)(2,1)}), bf16[4,16,896]{2,1,0:T(8,128)(2,1)S(1)}, u32[]{:S(2)}, u32[]{:S(2)}) async-start(bf16[4,16,896]{2,1,0:T(8,128)(2,1)} %reduce_sum.43), calls=%async_computation.5 | async-start | bytes 229376 | tf_op jit(solution)/shard_map/all_to_all | solution.py:59

commit v3 on v2

v3 whole, which is shorter than its diff:
```python
import jax
import jax.numpy as jnp
from jax import lax
from jax.sharding import PartitionSpec as P

BF, F32 = jnp.bfloat16, jnp.float32
DP, EXPERT = ("h", "l", "c"), ("e", "q", "x")
SIZES = (4, 2, 2, 2, 4, 4)
SPLIT = ("l", "c", "x")
LANES, TILES = 128, 4
EXTRA = 16


def tiles(a):
    *lead, rows, cols = a.shape
    a = jnp.pad(a, [(0, 0)] * (a.ndim - 1) + [(0, TILES * LANES - cols)])
    a = jnp.swapaxes(a.reshape(*lead, rows, TILES, LANES), -3, -2)
    return a.reshape(*lead, TILES * rows, LANES)


def untiled(a, cols):
    *lead, rows, _ = a.shape
    a = jnp.swapaxes(a.reshape(*lead, TILES, rows // TILES, LANES), -3, -2)
    return a.reshape(*lead, rows // TILES, TILES * LANES)[..., :cols]


def slices(a):
    rows, width = a.shape
    a = a.reshape(rows, 8, 2, width // 16)
    return tiles(a.transpose(2, 1, 0, 3).reshape(16, rows, width // 16))


def on_device(grad_values, grad_scales, hidden_act, down_weight, slot_token, slot_count, slot_gate):
    nh, nl, nc, ne, nq, nx = (lax.axis_size(a) for a in "hlceqx")
    low, core, owner = (lax.axis_index(a) for a in "lce")
    rows, width = grad_values.shape
    ny, quarters = ne * nq, nl * nc
    group = rows * ny * nx
    pick = lambda a: lax.dynamic_index_in_dim(a[0], owner, 0, keepdims=False)
    tok, num, gate = pick(slot_token), pick(slot_count), pick(slot_gate)
    slots = tok.shape[0]
    live = jnp.arange(slots, dtype=jnp.int32) < num
    tok = jnp.where(live, tok, group)
    hidden = hidden_act[0]
    units = hidden.shape[1]
    dests = quarters * nx

    scaled = (grad_values.astype(F32) * grad_scales.astype(F32)[:, None]).astype(BF)
    weighted = (gate[:, None] * hidden.astype(F32)).astype(BF)
    tok_row = jnp.broadcast_to(tok.astype(BF)[None, :], (EXTRA, slots))
    pack = jnp.concatenate([weighted, tok_row], axis=0)
    share = units // quarters
    w_rows = lax.dynamic_slice_in_dim(down_weight, (low * nc + core) * share, share, 0)
    send = jnp.concatenate(
        [
            slices(scaled),
            jnp.broadcast_to(pack[None], (dests,) + pack.shape),
            slices(w_rows),
        ],
        axis=1,
    )
    got = lax.all_to_all(send, SPLIT, 0, 0)
    a, b, cols = TILES * rows, TILES * rows + slots + EXTRA, width // dests
    mine = untiled(got[:, :a], cols).reshape(quarters, nx * rows, cols)
    mine = lax.all_gather(mine, ("e", "q"), axis=0)
    packs = got[:, a:b].reshape(quarters, nx, slots + EXTRA, units)
    w_cols = untiled(got[:, b:], cols).reshape(quarters, nx, share, cols)

    toks = packs[:, 0, slots, :].astype(jnp.int32)
    ids = jnp.arange(group, dtype=jnp.int32)
    pick_all = (toks[:, :, None] == ids).astype(BF)
    mine = mine.transpose(1, 0, 2, 3).reshape(quarters, group, cols)
    routed = jnp.einsum("gst,gtd->gsd", pick_all, mine, preferred_element_type=F32).astype(BF)
    part = jnp.einsum("gxsj,gsd->xjd", packs[:, :, :slots], routed, preferred_element_type=F32)
    part = part.astype(BF).reshape(nx, nh, units // nh, cols).transpose(1, 0, 2, 3)
    sums = lax.all_to_all(part, "h", 0, 0)
    w_cols = w_cols.transpose(1, 0, 2, 3).reshape(nx, units, cols)
    proj = jnp.einsum("gsd,xjd->gxsj", routed, w_cols, preferred_element_type=F32).astype(BF)

    sums = jnp.sum(sums.astype(F32), axis=0).astype(BF)
    per = units // nh // quarters
    sums = sums.reshape(nx, quarters, per, cols).transpose(1, 0, 2, 3)
    send = jnp.concatenate(
        [tiles(sums).reshape(dests, TILES * per, LANES), proj.reshape(dests, slots, units)], axis=1
    )
    got = lax.all_to_all(send, SPLIT, 0, 0)
    a = TILES * per
    block = untiled(got[:, :a], cols).reshape(nl, nc * nx, per, cols)
    block = block.transpose(2, 1, 0, 3).reshape(per, width)
    project = jnp.sum(got[:, a:].astype(F32), axis=0)
    hidden_grad = (gate[:, None] * project).astype(BF)[None]
    partial = jnp.sum(hidden.astype(F32) * project, axis=1)
    onehot = (tok[:, None] == ids).astype(F32)
    per_token = jnp.dot(partial, onehot, precision=lax.Precision.HIGHEST)
    spread = lax.all_to_all(per_token.reshape(ny * nx, rows), EXPERT, 0, 0)
    gate_grad = spread.reshape(ne, -1, rows).sum(axis=1).T

    block = lax.all_gather(block, ("h", "l"), axis=0)
    cut = nh * nl // 2
    halves = [lax.all_gather(block[i : i + cut], "c", axis=1, tiled=True) for i in (0, cut)]
    weight_grad = jnp.concatenate([a.reshape(-1, width) for a in halves], axis=0)
    return hidden_grad, weight_grad, gate_grad


def solution(mesh):
    fine = jax.sharding.Mesh(mesh.devices.reshape(SIZES), DP + EXPERT)
    return jax.shard_map(
        on_device,
        mesh=fine,
        in_specs=(
            P(DP + EXPERT, None),
            P(DP + EXPERT),
            P(DP, None, EXPERT),
            P(EXPERT, None),
            P(DP, None, None),
            P(DP, None),
            P(DP, None, None),
        ),
        out_specs=(P(DP, None, EXPERT), P(EXPERT, None), P(DP + EXPERT, None)),
        check_vma=False,
    )
```

time: 175 us -> 149 us (0.85)
  waiting for transfers between devices: 64.3 us -> 20.6 us
  blocking collectives: 46.2 us -> 79.7 us
  starting transfers between devices: 41.8 us -> 26.3 us
    all_to_all x6 -> x2, waiting for transfers between devices: 56.5 us -> 20.6 us  [the longest x1 11.6 us: on_device(): got = lax.all_to_all(send, SPLIT, 0, 0)]
    all_to_all x0 -> x1, blocking collectives: none -> 27.5 us  [on_device(): got = lax.all_to_all(send, SPLIT, 0, 0)]
    all_to_all x6 -> x2, starting transfers between devices: 35.4 us -> 20.9 us  [the longest x1 11.4 us: on_device(): got = lax.all_to_all(send, SPLIT, 0, 0)]
    all_to_all x1, waiting for transfers between devices: 7.73 us -> 0.01 us  [on_device(): spread = lax.all_to_all(per_token.reshape(ny * nx, rows), EXPERT, 0, 0)]
    all_gather x4, blocking collectives: 46.2 us -> 52.3 us  [the longest x1 21.3 us: on_device(): block = lax.all_gather(block, ('h', 'l'), axis=0)]
    transpose x0 -> x7, local copies, waits for them, and re-layouts: none -> 2.65 us  [the longest x1 1.9 us: on_device(): part.astype(BF).reshape(nx, nh, units // nh, cols).transpose(1, 0, 2, 3)]
  transfers between devices with their start and end apart: 7 -> 3, of which waited for: 7 -> 2; matrix products, arithmetic and copies ran while one was open for 8% -> 2% of each run, Pallas kernels for 0% -> 0%
where the time goes in v3:
time: 149 us; the launch traced here: 148 us
  blocking collectives  79.7 us (53%)
  starting transfers between devices  26.3 us (18%)
  waiting for transfers between devices  20.6 us (14%)
  local copies, waits for them, and re-layouts  9.17 us (6%)
  other arithmetic  7.3 us (5%)
  matrix products  3.92 us (3%)
    all_to_all x1, blocking collectives, on_device(): got = lax.all_to_all(send, SPLIT, 0, 0)  27.5 us
    all_gather x1, blocking collectives, on_device(): block = lax.all_gather(block, ('h', 'l'), axis=0)  21.3 us
    all_gather x1, blocking collectives, on_device(): mine = lax.all_gather(mine, ('e', 'q'), axis=0)  21.1 us
    all_to_all x1, waiting for transfers between devices, on_device(): got = lax.all_to_all(send, SPLIT, 0, 0)  11.6 us
    all_to_all x1, starting transfers between devices, on_device(): got = lax.all_to_all(send, SPLIT, 0, 0)  11.4 us
    all_gather x2, blocking collectives, on_device(): lax.all_gather(block[i:i + cut], 'c', axis=1, tiled=True)  9.82 us
    all_to_all x1, starting transfers between devices, on_device(): sums = lax.all_to_all(part, 'h', 0, 0)  9.58 us
    all_to_all x1, waiting for transfers between devices, on_device(): sums = lax.all_to_all(part, 'h', 0, 0)  9.04 us
  transfers between devices with their start and end apart: 3, of which 2 were waited for; matrix products, arithmetic and copies ran while one was open for 2% of the time, Pallas kernels for 0%

profile of v3, /device:TPU:1, one launch (start us, length us, event | category | flops | bytes accessed | tf_op | source)
XLA Modules:
  0.0 148.0 jit_solution(545853620599407260)
XLA Ops:
  0.7 1.4 constant_dynamic-slice_fusion.2
  2.0 0.7 fusion.12
  2.7 0.7 convert_element_type.72
  3.4 1.0 multiply_convert_fusion
  4.7 0.7 reshape.182
  6.4 0.7 fusion.15
  7.4 27.5 %all_to_all.24 = bf16[16,304,128]{2,1,0:T(8,128)(2,1)S(1)} all-to-all(bf16[16,304,128]{2,1,0:T(8,128)(2,1)S(1)} %pad_maximum_fusion.1), channel_id=1, replica_groups=mesh['h'=4,'l'=2,'c'=2,'e'=2,'q'=4,'x'=4] {'l','c','x'}, dimensions={0} | all-to-all | bytes 2490368 | tf_op jit(solution)/shard_map/all_to_all | solution.py:62
  34.9 21.1 %all_gather.12 = bf16[8,4,32,448]{3,2,1,0:T(8,128)(2,1)S(1)} all-gather(bf16[1,4,32,448]{3,2,1,0:T(8,128)(2,1)S(1)} %bitcast.123), channel_id=1, replica_groups=mesh['h'=4,'l'=2,'c'=2,'e'=2,'q'=4,'x'=4] {'e','q'}, dimensions={0}, use_global_device_ids=true | all-gather | bytes 1032192 | tf_op jit(solution)/shard_map/all_gather | solution.py:65
  56.8 1.2 fusion
  57.9 2.0 %copy.49 = bf16[4,128,448]{2,1,0:T(8,128)(2,1)} copy(bf16[4,128,448]{1,2,0:T(8,128)(2,1)} %fusion) | data formatting | bytes 917504 | tf_op jit(solution)/shard_map/convert_element_type | solution.py:75
  59.9 1.9 %copy.50 = bf16[4,4,32,448]{3,2,1,0:T(8,128)(2,1)} copy(bf16[4,4,32,448]{3,2,0,1:T(8,128)(2,1)} %bitcast.116) | data formatting | bytes 917504 | tf_op jit(solution)/shard_map/transpose | solution.py:75
  61.8 9.6 %all-to-all-start.1 = ((bf16[4,4,32,448]{3,2,1,0:T(8,128)(2,1)}), bf16[4,4,32,448]{3,2,1,0:T(8,128)(2,1)}, u32[]{:S(2)}, u32[]{:S(2)}) async-start(bf16[4,4,32,448]{3,2,1,0:T(8,128)(2,1)} %copy.50), calls=%async_computation.1 | async-start | bytes 1048576 | tf_op jit(solution)/shard_map/all_to_all | solution.py:76
  72.5 9.0 %all-to-all-done.1 = bf16[4,4,32,448]{3,2,1,0:T(8,128)(2,1)} async-done(((bf16[4,4,32,448]{3,2,1,0:T(8,128)(2,1)}), bf16[4,4,32,448]{3,2,1,0:T(8,128)(2,1)}, u32[]{:S(2)}, u32[]{:S(2)}) %all-to-all-start.1) | async-done | bytes 458784 | tf_op jit(solution)/shard_map/all_to_all | solution.py:76
  81.6 1.1 reduce_sum.41
  82.8 0.9 pad_maximum_fusion.2
  83.7 11.4 %all-to-all-start.2 = ((bf16[16,160,128]{2,1,0:T(8,128)(2,1)}), bf16[16,160,128]{2,1,0:T(8,128)(2,1)S(1)}, u32[]{:S(2)}, u32[]{:S(2)}) async-start(bf16[16,160,128]{2,1,0:T(8,128)(2,1)} %pad_maximum_fusion.2), calls=%async_computation.2 | async-start | bytes 1310720 | tf_op jit(solution)/shard_map/all_to_all | solution.py:86
  95.0 11.6 %all-to-all-done.2 = bf16[16,160,128]{2,1,0:T(8,128)(2,1)S(1)} async-done(((bf16[16,160,128]{2,1,0:T(8,128)(2,1)}), bf16[16,160,128]{2,1,0:T(8,128)(2,1)S(1)}, u32[]{:S(2)}, u32[]{:S(2)}) %all-to-all-start.2) | async-done | bytes 655392 | tf_op jit(solution)/shard_map/all_to_all | solution.py:86
  107.1 1.7 %convolution_bitcast_fusion.1 = f32[32,1,8]{2,1,0:T(1,128)} fusion(s32[32,8]{1,0:T(8,128)S(1)} %multiply_add_fusion, s32[128]{0:T(128)S(1)} %get-tuple-element.4, f32[128]{0:T(128)S(1)} %fusion.8), kind=kOutput, calls=%fused_computation.7 | convolution fusion | flops 425984 | bytes 3072 | tf_op jit(solution)/shard_map/dot_general | solution.py:94
  108.8 5.4 %all-to-all-start.3 = ((f32[32,1,8]{2,1,0:T(1,128)}), f32[32,1,8]{2,1,0:T(1,128)S(1)}, u32[]{:S(2)}, u32[]{:S(2)}) async-start(f32[32,1,8]{2,1,0:T(1,128)} %convolution_bitcast_fusion.1), calls=%async_computation.3 | async-start | bytes 32768 | tf_op jit(solution)/shard_map/all_to_all | solution.py:95
  114.2 21.3 %all_gather.13 = bf16[8,8,7168]{2,1,0:T(8,128)(2,1)S(1)} all-gather(bf16[1,8,7168]{2,1,0:T(8,128)(2,1)S(1)} %all_gather_reshape.7), channel_id=1, replica_groups=mesh['h'=4,'l'=2,'c'=2,'e'=2,'q'=4,'x'=4] {'h','l'}, dimensions={0}, use_global_device_ids=true | all-gather | bytes 1032192 | tf_op jit(solution)/shard_map/all_gather | solution.py:98
  135.5 7.4 %all_gather.14 = bf16[4,16,7168]{2,1,0:T(8,128)(2,1)S(1)} all-gather(bf16[4,8,7168]{2,1,0:T(8,128)(2,1)S(1)} %get-tuple-element.5), channel_id=1, replica_groups=mesh['h'=4,'l'=2,'c'=2,'e'=2,'q'=4,'x'=4] {'c'}, dimensions={1}, use_global_device_ids=true | all-gather | bytes 1376256 | tf_op jit(solution)/shard_map/all_gather | solution.py:100
  142.9 2.5 %all_gather.15 = bf16[4,16,7168]{2,1,0:T(8,128)(2,1)S(1)} all-gather(bf16[4,8,7168]{2,1,0:T(8,128)(2,1)S(1)} %get-tuple-element.6), channel_id=1, replica_groups=mesh['h'=4,'l'=2,'c'=2,'e'=2,'q'=4,'x'=4] {'c'}, dimensions={1}, use_global_device_ids=true | all-gather | bytes 1376256 | tf_op jit(solution)/shard_map/all_gather | solution.py:100
  145.4 1.4 pad_maximum_fusion
  146.7 0.7 fusion.9
  (43 shorter events, 4.5 us)
Async XLA Ops:
  0.6 4.0 %copy-start = (bf16[128,7168]{1,0:T(8,128)(2,1)S(1)}, bf16[128,7168]{1,0:T(8,128)(2,1)}, u32[]{:S(2)}) copy-start(bf16[128,7168]{1,0:T(8,128)(2,1)} %param.10) | copy-start | bytes 5505028
  5.7 0.7 copy-start.3
  5.7 1.3 copy-start.1
  61.8 19.7 %all-to-all-start.1 = ((bf16[4,4,32,448]{3,2,1,0:T(8,128)(2,1)}), bf16[4,4,32,448]{3,2,1,0:T(8,128)(2,1)}, u32[]{:S(2)}, u32[]{:S(2)}) async-start(bf16[4,4,32,448]{3,2,1,0:T(8,128)(2,1)} %copy.50), calls=%async_computation.1 | async-start | bytes 1048576 | tf_op jit(solution)/shard_map/all_to_all | solution.py:76
  82.8 24.2 %copy-start.2 = (bf16[1,128,128]{2,1,0:T(8,128)(2,1)S(1)}, bf16[1,128,128]{2,1,0:T(8,128)(2,1)}, u32[]{:S(2)}) copy-start(bf16[1,128,128]{2,1,0:T(8,128)(2,1)} %param.9) | copy-start | bytes 98308
  83.7 22.9 %all-to-all-start.2 = ((bf16[16,160,128]{2,1,0:T(8,128)(2,1)}), bf16[16,160,128]{2,1,0:T(8,128)(2,1)S(1)}, u32[]{:S(2)}, u32[]{:S(2)}) async-start(bf16[16,160,128]{2,1,0:T(8,128)(2,1)} %pad_maximum_fusion.2), calls=%async_computation.2 | async-start | bytes 1310720 | tf_op jit(solution)/shard_map/all_to_all | solution.py:86
  108.8 38.6 %all-to-all-start.3 = ((f32[32,1,8]{2,1,0:T(1,128)}), f32[32,1,8]{2,1,0:T(1,128)S(1)}, u32[]{:S(2)}, u32[]{:S(2)}) async-start(f32[32,1,8]{2,1,0:T(1,128)} %convolution_bitcast_fusion.1), calls=%async_computation.3 | async-start | bytes 32768 | tf_op jit(solution)/shard_map/all_to_all | solution.py:95

commit v4 on v3

--- a/solution.py
+++ b/solution.py
@@ -46,24 +46,23 @@
     dests = quarters * nx
 
     scaled = (grad_values.astype(F32) * grad_scales.astype(F32)[:, None]).astype(BF)
+    cols = width // dests
+    mine = lax.all_to_all(slices(scaled), SPLIT, 0, 0)
+
     weighted = (gate[:, None] * hidden.astype(F32)).astype(BF)
     tok_row = jnp.broadcast_to(tok.astype(BF)[None, :], (EXTRA, slots))
     pack = jnp.concatenate([weighted, tok_row], axis=0)
     share = units // quarters
     w_rows = lax.dynamic_slice_in_dim(down_weight, (low * nc + core) * share, share, 0)
     send = jnp.concatenate(
-        [
-            slices(scaled),
-            jnp.broadcast_to(pack[None], (dests,) + pack.shape),
-            slices(w_rows),
-        ],
-        axis=1,
+        [jnp.broadcast_to(pack[None], (dests,) + pack.shape), slices(w_rows)], axis=1
     )
+    send, mine = lax.optimization_barrier((send, mine))
     got = lax.all_to_all(send, SPLIT, 0, 0)
-    a, b, cols = TILES * rows, TILES * rows + slots + EXTRA, width // dests
-    mine = untiled(got[:, :a], cols).reshape(quarters, nx * rows, cols)
+    mine = untiled(mine, cols).reshape(quarters, nx * rows, cols)
     mine = lax.all_gather(mine, ("e", "q"), axis=0)
-    packs = got[:, a:b].reshape(quarters, nx, slots + EXTRA, units)
+    b = slots + EXTRA
+    packs = got[:, :b].reshape(quarters, nx, slots + EXTRA, units)
     w_cols = untiled(got[:, b:], cols).reshape(quarters, nx, share, cols)
 
     toks = packs[:, 0, slots, :].astype(jnp.int32)
@@ -77,8 +76,8 @@
     w_cols = w_cols.transpose(1, 0, 2, 3).reshape(nx, units, cols)
     proj = jnp.einsum("gsd,xjd->gxsj", routed, w_cols, preferred_element_type=F32).astype(BF)
 
+    per = units // nh // quarters
     sums = jnp.sum(sums.astype(F32), axis=0).astype(BF)
-    per = units // nh // quarters
     sums = sums.reshape(nx, quarters, per, cols).transpose(1, 0, 2, 3)
     send = jnp.concatenate(
         [tiles(sums).reshape(dests, TILES * per, LANES), proj.reshape(dests, slots, units)], axis=1
@@ -87,7 +86,8 @@
     a = TILES * per
     block = untiled(got[:, :a], cols).reshape(nl, nc * nx, per, cols)
     block = block.transpose(2, 1, 0, 3).reshape(per, width)
-    project = jnp.sum(got[:, a:].astype(F32), axis=0)
+    proj = got[:, a:]
+    project = jnp.sum(proj.astype(F32), axis=0)
     hidden_grad = (gate[:, None] * project).astype(BF)[None]
     partial = jnp.sum(hidden.astype(F32) * project, axis=1)
     onehot = (tok[:, None] == ids).astype(F32)

time: 149 us -> 141 us (0.946)
  blocking collectives: 79.7 us -> 54.2 us
  starting transfers between devices: 26.3 us -> 40.8 us
  matrix products: 3.92 us -> 6.16 us
    all_to_all x1 -> x0, blocking collectives: 27.5 us -> none  [on_device(): got = lax.all_to_all(send, SPLIT, 0, 0)]
    all_to_all x0 -> x1, starting transfers between devices: none -> 10.2 us  [on_device(): mine = lax.all_to_all(slices(scaled), SPLIT, 0, 0)]
    all_to_all x1 -> x2, starting transfers between devices: 11.4 us -> 16.2 us  [on_device(): got = lax.all_to_all(send, SPLIT, 0, 0)]
    all_to_all x1 -> x2, waiting for transfers between devices: 11.6 us -> 11.5 us  [on_device(): got = lax.all_to_all(send, SPLIT, 0, 0)]
  transfers between devices with their start and end apart: 3 -> 5, of which waited for: 2 -> 3; matrix products, arithmetic and copies ran while one was open for 2% -> 7% of each run, Pallas kernels for 0% -> 0%
where the time goes in v4:
time: 141 us; the launch traced here: 140 us
  blocking collectives  54.2 us (38%)
  starting transfers between devices  40.8 us (29%)
  waiting for transfers between devices  20.8 us (15%)
  local copies, waits for them, and re-layouts  9.5 us (7%)
  other arithmetic  7.38 us (5%)
  matrix products  6.16 us (4%)
    all_gather x1, blocking collectives, on_device(): mine = lax.all_gather(mine, ('e', 'q'), axis=0)  22.4 us
    all_gather x1, blocking collectives, on_device(): block = lax.all_gather(block, ('h', 'l'), axis=0)  22.3 us
    all_to_all x2, starting transfers between devices, on_device(): got = lax.all_to_all(send, SPLIT, 0, 0)  16.2 us
    all_to_all x2, waiting for transfers between devices, on_device(): got = lax.all_to_all(send, SPLIT, 0, 0)  11.5 us
    all_to_all x1, starting transfers between devices, on_device(): mine = lax.all_to_all(slices(scaled), SPLIT, 0, 0)  10.2 us
    all_gather x2, blocking collectives, on_device(): lax.all_gather(block[i:i + cut], 'c', axis=1, tiled=True)  9.48 us
    all_to_all x1, waiting for transfers between devices, on_device(): sums = lax.all_to_all(part, 'h', 0, 0)  8.68 us
    all_to_all x1, starting transfers between devices, on_device(): sums = lax.all_to_all(part, 'h', 0, 0)  8.15 us
  transfers between devices with their start and end apart: 5, of which 3 were waited for; matrix products, arithmetic and copies ran while one was open for 7% of the time, Pallas kernels for 0%

profile of v4, /device:TPU:1, one launch (start us, length us, event | category | flops | bytes accessed | tf_op | source)
XLA Modules:
  0.0 139.8 jit_solution(9511796171368844035)
XLA Ops:
  0.6 0.8 convert_element_type.76
  1.4 1.0 multiply_convert_fusion
  3.4 10.2 %all-to-all-start = ((bf16[16,32,128]{2,1,0:T(8,128)(2,1)}), bf16[16,32,128]{2,1,0:T(8,128)(2,1)S(1)}, u32[]{:S(2)}, u32[]{:S(2)}) async-start(bf16[16,32,128]{2,1,0:T(8,128)(2,1)} %pad_bitcast_fusion), calls=%async_computation | async-start | bytes 262144 | tf_op jit(solution)/shard_map/all_to_all | solution.py:50
  13.6 1.2 constant_dynamic-slice_fusion.2
  18.1 1.1 pad_maximum_fusion.1
  19.8 5.1 %all-to-all-start.1 = ((bf16[16,272,128]{2,1,0:T(8,128)(2,1)}), bf16[16,272,128]{2,1,0:T(8,128)(2,1)S(1)}, u32[]{:S(2)}, u32[]{:S(2)}) async-start(bf16[16,272,128]{2,1,0:T(8,128)(2,1)} %pad_maximum_fusion.1), calls=%async_computation.1 | async-start | bytes 2228224 | tf_op jit(solution)/shard_map/all_to_all | solution.py:61
  24.9 22.4 %all_gather.12 = bf16[8,4,32,448]{3,2,1,0:T(8,128)(2,1)S(1)} all-gather(bf16[1,4,32,448]{3,2,1,0:T(8,128)(2,1)S(1)} %bitcast.121), channel_id=1, replica_groups=mesh['h'=4,'l'=2,'c'=2,'e'=2,'q'=4,'x'=4] {'e','q'}, dimensions={0}, use_global_device_ids=true | all-gather | bytes 1032192 | tf_op jit(solution)/shard_map/all_gather | solution.py:63
  47.3 1.0 copy.47
  48.4 1.8 %convolution_convert_fusion.1 = bf16[4,128,448]{1,2,0:T(8,128)(2,1)S(1)} fusion(bf16[4,256,448]{2,1,0:T(8,128)(2,1)} %bitcast.105, s32[4,128]{1,0:T(4,128)S(1)} %bitcast.128), kind=kOutput, calls=%fused_computation.3 | convolution fusion | flops 117800960 | bytes 1378304 | tf_op jit(solution)/shard_map/gst,gtd->gsd/dot_general | solution.py:72
  51.0 1.2 fusion
  52.2 1.2 copy.49
  53.4 0.8 copy.50
  54.3 8.2 %all-to-all-start.2 = ((bf16[4,4,32,448]{3,2,1,0:T(8,128)(2,1)}), bf16[4,4,32,448]{3,2,1,0:T(8,128)(2,1)S(1)}, u32[]{:S(2)}, u32[]{:S(2)}) async-start(bf16[4,4,32,448]{3,2,1,0:T(8,128)(2,1)} %copy.50), calls=%async_computation.2 | async-start | bytes 1048576 | tf_op jit(solution)/shard_map/all_to_all | solution.py:75
  63.0 1.5 %fusion.1 = bf16[4,4,128,128]{3,2,0,1:T(8,128)(2,1)S(1)} fusion(bf16[4,128,448,1]{2,1,3,0:T(8,128)(2,1)S(1)} %bitcast.110, bf16[4,128,448]{1,2,0:T(8,128)(2,1)} %copy-done.1), kind=kOutput, calls=%fused_computation.5 | convolution fusion | flops 235143168 | bytes 1441792 | tf_op jit(solution)/shard_map/gsd,xjd->gxsj/dot_general | solution.py:77
  64.6 8.7 %all-to-all-done.2 = bf16[4,4,32,448]{3,2,1,0:T(8,128)(2,1)S(1)} async-done(((bf16[4,4,32,448]{3,2,1,0:T(8,128)(2,1)}), bf16[4,4,32,448]{3,2,1,0:T(8,128)(2,1)S(1)}, u32[]{:S(2)}, u32[]{:S(2)}) %all-to-all-start.2) | async-done | bytes 458784 | tf_op jit(solution)/shard_map/all_to_all | solution.py:75
  73.4 0.9 pad_maximum_fusion.2
  74.3 11.1 %all-to-all-start.3 = ((bf16[16,160,128]{2,1,0:T(8,128)(2,1)}), bf16[16,160,128]{2,1,0:T(8,128)(2,1)S(1)}, u32[]{:S(2)}, u32[]{:S(2)}) async-start(bf16[16,160,128]{2,1,0:T(8,128)(2,1)} %pad_maximum_fusion.2), calls=%async_computation.3 | async-start | bytes 1310720 | tf_op jit(solution)/shard_map/all_to_all | solution.py:85
  85.4 11.5 %all-to-all-done.3 = bf16[16,160,128]{2,1,0:T(8,128)(2,1)S(1)} async-done(((bf16[16,160,128]{2,1,0:T(8,128)(2,1)}), bf16[16,160,128]{2,1,0:T(8,128)(2,1)S(1)}, u32[]{:S(2)}, u32[]{:S(2)}) %all-to-all-start.3) | async-done | bytes 655392 | tf_op jit(solution)/shard_map/all_to_all | solution.py:85
  97.4 1.7 %convolution_bitcast_fusion.1 = f32[32,1,8]{2,1,0:T(1,128)} fusion(s32[32,8]{1,0:T(8,128)S(1)} %multiply_add_fusion, s32[128]{0:T(128)S(1)} %get-tuple-element.8, f32[128]{0:T(128)S(1)} %fusion.8), kind=kOutput, calls=%fused_computation.7 | convolution fusion | flops 425984 | bytes 3072 | tf_op jit(solution)/shard_map/dot_general | solution.py:94
  99.1 6.2 %all-to-all-start.4 = ((f32[32,1,8]{2,1,0:T(1,128)}), f32[32,1,8]{2,1,0:T(1,128)S(1)}, u32[]{:S(2)}, u32[]{:S(2)}) async-start(f32[32,1,8]{2,1,0:T(1,128)} %convolution_bitcast_fusion.1), calls=%async_computation.4 | async-start | bytes 32768 | tf_op jit(solution)/shard_map/all_to_all | solution.py:95
  105.3 22.3 %all_gather.13 = bf16[8,8,7168]{2,1,0:T(8,128)(2,1)S(1)} all-gather(bf16[1,8,7168]{2,1,0:T(8,128)(2,1)S(1)} %all_gather_reshape.7), channel_id=1, replica_groups=mesh['h'=4,'l'=2,'c'=2,'e'=2,'q'=4,'x'=4] {'h','l'}, dimensions={0}, use_global_device_ids=true | all-gather | bytes 1032192 | tf_op jit(solution)/shard_map/all_gather | solution.py:98
  127.6 7.0 %all_gather.14 = bf16[4,16,7168]{2,1,0:T(8,128)(2,1)S(1)} all-gather(bf16[4,8,7168]{2,1,0:T(8,128)(2,1)S(1)} %get-tuple-element.9), channel_id=1, replica_groups=mesh['h'=4,'l'=2,'c'=2,'e'=2,'q'=4,'x'=4] {'c'}, dimensions={1}, use_global_device_ids=true | all-gather | bytes 1376256 | tf_op jit(solution)/shard_map/all_gather | solution.py:100
  134.7 2.5 %all_gather.15 = bf16[4,16,7168]{2,1,0:T(8,128)(2,1)S(1)} all-gather(bf16[4,8,7168]{2,1,0:T(8,128)(2,1)S(1)} %get-tuple-element.10), channel_id=1, replica_groups=mesh['h'=4,'l'=2,'c'=2,'e'=2,'q'=4,'x'=4] {'c'}, dimensions={1}, use_global_device_ids=true | all-gather | bytes 1376256 | tf_op jit(solution)/shard_map/all_gather | solution.py:100
  137.1 1.4 pad_maximum_fusion
  (45 shorter events, 8.1 us)
Async XLA Ops:
  0.6 14.9 %copy-start = (bf16[128,7168]{1,0:T(8,128)(2,1)S(1)}, bf16[128,7168]{1,0:T(8,128)(2,1)}, u32[]{:S(2)}) copy-start(bf16[128,7168]{1,0:T(8,128)(2,1)} %param.10) | copy-start | bytes 5505028
  3.4 16.4 %all-to-all-start = ((bf16[16,32,128]{2,1,0:T(8,128)(2,1)}), bf16[16,32,128]{2,1,0:T(8,128)(2,1)S(1)}, u32[]{:S(2)}, u32[]{:S(2)}) async-start(bf16[16,32,128]{2,1,0:T(8,128)(2,1)} %pad_bitcast_fusion), calls=%async_computation | async-start | bytes 262144 | tf_op jit(solution)/shard_map/all_to_all | solution.py:50
  16.5 0.7 copy-start.3
  16.5 1.3 copy-start.2
  19.8 28.6 %all-to-all-start.1 = ((bf16[16,272,128]{2,1,0:T(8,128)(2,1)}), bf16[16,272,128]{2,1,0:T(8,128)(2,1)S(1)}, u32[]{:S(2)}, u32[]{:S(2)}) async-start(bf16[16,272,128]{2,1,0:T(8,128)(2,1)} %pad_maximum_fusion.1), calls=%async_computation.1 | async-start | bytes 2228224 | tf_op jit(solution)/shard_map/all_to_all | solution.py:61
  50.3 0.8 copy-start.1
  54.3 19.0 %all-to-all-start.2 = ((bf16[4,4,32,448]{3,2,1,0:T(8,128)(2,1)}), bf16[4,4,32,448]{3,2,1,0:T(8,128)(2,1)S(1)}, u32[]{:S(2)}, u32[]{:S(2)}) async-start(bf16[4,4,32,448]{3,2,1,0:T(8,128)(2,1)} %copy.50), calls=%async_computation.2 | async-start | bytes 1048576 | tf_op jit(solution)/shard_map/all_to_all | solution.py:75
  74.3 22.6 %all-to-all-start.3 = ((bf16[16,160,128]{2,1,0:T(8,128)(2,1)}), bf16[16,160,128]{2,1,0:T(8,128)(2,1)S(1)}, u32[]{:S(2)}, u32[]{:S(2)}) async-start(bf16[16,160,128]{2,1,0:T(8,128)(2,1)} %pad_maximum_fusion.2), calls=%async_computation.3 | async-start | bytes 1310720 | tf_op jit(solution)/shard_map/all_to_all | solution.py:85
  99.1 40.1 %all-to-all-start.4 = ((f32[32,1,8]{2,1,0:T(1,128)}), f32[32,1,8]{2,1,0:T(1,128)S(1)}, u32[]{:S(2)}, u32[]{:S(2)}) async-start(f32[32,1,8]{2,1,0:T(1,128)} %convolution_bitcast_fusion.1), calls=%async_computation.4 | async-start | bytes 32768 | tf_op jit(solution)/shard_map/all_to_all | solution.py:95

commit v5 on v0

v5 whole, which is shorter than its diff:
```python
import jax
import jax.numpy as jnp
from jax import lax
from jax.experimental import pallas as pl
from jax.experimental.pallas import tpu as pltpu
from jax.sharding import PartitionSpec as P

BF, F32, I32 = jnp.bfloat16, jnp.float32, jnp.int32
DP, EXPERT = ("h", "l", "c"), ("e", "q", "x")
H, L, C, E, Q, X = SIZES = (4, 2, 2, 2, 4, 4)
SPLIT = ("l", "c", "x")
QUARTERS, PARTS = L * C, L * C * X
LANES, TILES = 128, 4
WIDTH, SLOTS, UNITS, ROWS = 7168, 128, 128, 8
GROUP = E * Q * X * ROWS
COLS, WIDE = WIDTH // PARTS, TILES * LANES
PAIR = 2 * COLS
SHARE = UNITS // QUARTERS
CHUNK = UNITS // H
PER = CHUNK // QUARTERS
EXTRA = 16
PACK = SLOTS + EXTRA
BACK = TILES * PER


def lanes(shape):
    return lax.broadcasted_iota(I32, shape, len(shape) - 1)


def column(row):
    n = row.shape[1]
    across, down = lanes((n, n)), lax.broadcasted_iota(I32, (n, n), 0)
    return jnp.sum(jnp.where(across == down, row, jnp.zeros_like(row)), axis=1, keepdims=True)


def slice_of(a, n, l):
    start = n * PAIR
    if l == 0:
        a = a[:, start : start + WIDE]
    else:
        a = pltpu.roll(a[:, start + PAIR - WIDE : start + PAIR], COLS, 1)
    return jnp.where(lanes(a.shape) < COLS, a, 0.0)


def tokens_kernel(values_ref, scales_ref, out_ref):
    scaled = values_ref[...].astype(F32) * column(scales_ref[...].astype(F32))
    for l in range(L):
        for n in range(C * X):
            out_ref[l * C * X + n] = slice_of(scaled, n, l)[:, :COLS].astype(BF)


def own_slots(where_ref, tok_ref, count_ref):
    owner = where_ref[0]
    tok = jnp.where(owner == 0, tok_ref[0:1, :], tok_ref[1:2, :])
    return jnp.where(lanes((1, SLOTS)) < count_ref[0, owner], tok, GROUP)


def own_gate(where_ref, gate_ref):
    return column(jnp.where(where_ref[0] == 0, gate_ref[0:1, :], gate_ref[1:2, :]))


def pack_kernel(where_ref, count_ref, tok_ref, gate_ref, hidden_ref, w_ref, out_ref):
    weighted = (own_gate(where_ref, gate_ref) * hidden_ref[...].astype(F32)).astype(BF)
    tok = own_slots(where_ref, tok_ref, count_ref).astype(F32)
    tok = jnp.broadcast_to(tok, (EXTRA, SLOTS)).astype(BF)
    w = w_ref[...].astype(F32)
    for l in range(L):
        for n in range(C * X):
            at = l * C * X + n
            out_ref[at, 0:SLOTS, :] = weighted
            out_ref[at, SLOTS:PACK, :] = tok
            part = slice_of(w, n, l).astype(BF)
            for t in range(TILES):
                low = PACK + t * SHARE
                out_ref[at, low : low + SHARE, :] = part[:, t * LANES : (t + 1) * LANES]


def weight_kernel(mine_ref, pack_ref, part_ref, routed_ref):
    routed_ref[:, COLS:] = jnp.zeros((QUARTERS * SLOTS, WIDE - COLS), BF)
    ids = lax.broadcasted_iota(I32, (GROUP, SLOTS), 0)
    first = (((0,), (0,)), ((), ()))
    for g in range(QUARTERS):
        tok = pack_ref[g * X, SLOTS:PACK, :].astype(F32)[0:1, :].astype(I32)
        picks = jnp.where(ids == tok, 1.0, 0.0).astype(BF)
        rows = mine_ref[:, g].reshape(GROUP, COLS)
        routed = lax.dot_general(picks, rows, first, preferred_element_type=F32)
        routed_ref[g * SLOTS : (g + 1) * SLOTS, :COLS] = routed.astype(BF)
    routed = routed_ref[:, :COLS]
    for x in range(X):
        weighted = jnp.concatenate([pack_ref[g * X + x, :SLOTS, :] for g in range(QUARTERS)], axis=0)
        part = lax.dot_general(weighted, routed, first, preferred_element_type=F32).astype(BF)
        for h in range(H):
            part_ref[h, x] = part[h * CHUNK : (h + 1) * CHUNK]


def project_kernel(routed_ref, pack_ref, out_ref):
    routed = routed_ref[...]
    for x in range(X):
        w = [
            jnp.concatenate(
                [pack_ref[q * X + x, PACK + t * SHARE : PACK + (t + 1) * SHARE, :] for q in range(QUARTERS)],
                axis=0,
            )
            for t in range(TILES)
        ]
        w = jnp.concatenate(w, axis=1)
        proj = lax.dot_general(routed, w, (((1,), (1,)), ((), ())), preferred_element_type=F32)
        for g in range(QUARTERS):
            out_ref[g * X + x] = proj[g * SLOTS : (g + 1) * SLOTS].astype(BF)


def back_kernel(sums_ref, proj_ref, out_ref):
    for x in range(X):
        total = sums_ref[0, x].astype(F32)
        for h in range(1, H):
            total = total + sums_ref[h, x].astype(F32)
        total = jnp.concatenate([total, jnp.zeros((CHUNK, WIDE - COLS), F32)], axis=1)
        for g in range(QUARTERS):
            rows = total[g * PER : (g + 1) * PER]
            rows = [rows[:, t * LANES : (t + 1) * LANES] for t in range(TILES)]
            out_ref[g * X + x, 0:BACK, :] = jnp.concatenate(rows, axis=0).astype(BF)
            out_ref[g * X + x, BACK:, :] = proj_ref[g * X + x]


def finish_kernel(
    where_ref, count_ref, tok_ref, gate_ref, hidden_ref, got_ref, grad_ref, spread_ref, block_ref
):
    project = got_ref[0, BACK:, :].astype(F32)
    for n in range(1, PARTS):
        project = project + got_ref[n, BACK:, :].astype(F32)
    grad_ref[...] = (own_gate(where_ref, gate_ref) * project).astype(BF)
    partial = jnp.sum(hidden_ref[...].astype(F32) * project, axis=1, keepdims=True)
    tok = column(own_slots(where_ref, tok_ref, count_ref))
    device = jnp.where(lanes((SLOTS, E * Q * X)) == tok // ROWS, 1.0, 0.0)
    row = jnp.where(lanes((SLOTS, ROWS)) == tok % ROWS, partial, 0.0)
    spread_ref[...] = lax.dot_general(
        device, row, (((0,), (0,)), ((), ())), precision=lax.Precision.HIGHEST, preferred_element_type=F32
    )
    low = lanes((PER, LANES)) < COLS % LANES
    for n in range(C * X):
        a, b = (got_ref[l * C * X + n, 0:BACK, :].astype(F32) for l in range(L))
        a, b = ([p[t * PER : (t + 1) * PER] for t in range(TILES)] for p in (a, b))
        b = [pltpu.roll(p, COLS % LANES, 1) for p in b]
        tiles = a[:-1] + [jnp.where(low, p, r) for p, r in zip([a[-1]] + b[:-1], b)]
        block_ref[:, n * PAIR : (n + 1) * PAIR] = jnp.concatenate(tiles, axis=1).astype(BF)


VM, SM = pl.BlockSpec(memory_space=pltpu.VMEM), pl.BlockSpec(memory_space=pltpu.SMEM)


def call(kernel, outs, *args, scalars=0, flops=0):
    outs = [jax.ShapeDtypeStruct(s, d) for s, d in outs]
    nbytes = sum(a.size * a.dtype.itemsize for a in list(args) + outs)
    return pl.pallas_call(
        kernel,
        out_shape=outs,
        in_specs=[SM] * scalars + [VM] * (len(args) - scalars),
        out_specs=[VM] * len(outs),
        cost_estimate=pl.CostEstimate(flops=flops, bytes_accessed=nbytes, transcendentals=0),
        compiler_params=pltpu.CompilerParams(vmem_limit_bytes=32 * 1024 * 1024),
    )(*args)


def on_device(grad_values, grad_scales, hidden_act, down_weight, slot_token, slot_count, slot_gate):
    low, core, owner = (lax.axis_index(a) for a in "lce")
    hidden, tok, gate = hidden_act[0], slot_token[0], slot_gate[0]
    where = owner[None].astype(I32)

    (send,) = call(
        tokens_kernel, [((PARTS, ROWS, COLS), BF)], grad_values, grad_scales.reshape(1, ROWS)
    )
    mine = lax.all_to_all(send, SPLIT, 0, 0)

    w_rows = lax.dynamic_slice_in_dim(down_weight, (low * C + core) * SHARE, SHARE, 0)
    (pack,) = call(
        pack_kernel,
        [((PARTS, PACK + TILES * SHARE, LANES), BF)],
        where, slot_count, tok, gate, hidden, w_rows,
        scalars=2,
    )
    pack, mine = lax.optimization_barrier((pack, mine))
    pack = lax.all_to_all(pack, SPLIT, 0, 0)
    mine = lax.all_gather(mine.reshape(QUARTERS, X * ROWS, COLS), ("e", "q"), axis=0)

    part, routed = call(
        weight_kernel,
        [((H, X, CHUNK, COLS), BF), ((QUARTERS * SLOTS, WIDE), BF)],
        mine, pack,
        flops=2 * QUARTERS * SLOTS * COLS * (GROUP + X * UNITS),
    )
    sums = lax.all_to_all(part, "h", 0, 0)
    (proj,) = call(
        project_kernel,
        [((PARTS, SLOTS, UNITS), BF)],
        routed, pack,
        flops=2 * QUARTERS * SLOTS * WIDE * X * UNITS,
    )

    (send,) = call(back_kernel, [((PARTS, BACK + SLOTS, LANES), BF)], sums, proj)
    got = lax.all_to_all(send, SPLIT, 0, 0)
    hidden_grad, spread, block = call(
        finish_kernel,
        [((SLOTS, UNITS), BF), ((E * Q * X, ROWS), F32), ((PER, WIDTH), BF)],
        where, slot_count, tok, gate, hidden, got,
        scalars=2,
    )
    spread = lax.all_to_all(spread, EXPERT, 0, 0)
    gate_grad = spread.reshape(E, Q * X, ROWS).sum(axis=1).T

    block = lax.all_gather(block, ("h", "l"), axis=0)
    cut = H * L // 2
    halves = [lax.all_gather(block[i : i + cut], "c", axis=1, tiled=True) for i in (0, cut)]
    weight_grad = jnp.concatenate([a.reshape(-1, WIDTH) for a in halves], axis=0)
    return hidden_grad[None], weight_grad, gate_grad


def solution(mesh):
    fine = jax.sharding.Mesh(mesh.devices.reshape(SIZES), DP + EXPERT)
    return jax.shard_map(
        on_device,
        mesh=fine,
        in_specs=(
            P(DP + EXPERT, None),
            P(DP + EXPERT),
            P(DP, None, EXPERT),
            P(EXPERT, None),
            P(DP, None, None),
            P(DP, None),
            P(DP, None, None),
        ),
        out_specs=(P(DP, None, EXPERT), P(EXPERT, None), P(DP + EXPERT, None)),
        check_vma=False,
    )
```

time: 257 us -> 137 us (0.53)
  blocking collectives: 198 us -> 79.6 us
  starting transfers between devices: 0.04 us -> 29.1 us
  between operations: 15.4 us -> 0.77 us
  waiting for transfers between devices: 20.8 us -> 9.55 us
  matrix products: 5.27 us -> 0 us
  Pallas kernels: 0 us -> 4.58 us
  local copies, waits for them, and re-layouts: 14.7 us -> 11.2 us
    unnamed x2 -> x0, blocking collectives: 119 us -> none
    psum x1 -> x0, blocking collectives: 79.3 us -> none  [on_device(): weight_grad = lax.psum(weight_part, 'dp').astype(jnp.bfloat16)]
    all_gather x0 -> x4, blocking collectives: none -> 55.6 us  [the longest x1 23.9 us: on_device(): lax.all_gather(mine.reshape(QUARTERS, X * ROWS, COLS), ('e', 'q'), axis=0)]
    all_to_all x0 -> x4, starting transfers between devices: none -> 29.1 us  [the longest x1 10.2 us: on_device(): mine = lax.all_to_all(send, SPLIT, 0, 0)]
    all_to_all x0 -> x1, blocking collectives: none -> 24 us  [on_device(): got = lax.all_to_all(send, SPLIT, 0, 0)]
    all_gather x1 -> x0, waiting for transfers between devices: 20.2 us -> none  [on_device(): lax.all_gather(grad_values, 'expert', axis=0, tiled=True)]
    all_to_all x0 -> x4, waiting for transfers between devices: none -> 9.55 us  [the longest x1 7.88 us: on_device(): sums = lax.all_to_all(part, 'h', 0, 0)]
    gather x2 -> x0, local copies, waits for them, and re-layouts: 8.33 us -> none  [the longest x1 7.1 us: on_device(): picked = jnp.take(values_all, slot_tok, axis=0).astype(jnp.float32)]
  transfers between devices with their start and end apart: 1 -> 4, of which waited for: 1 -> 2; matrix products, arithmetic and copies ran while one was open for 3% -> 1% of each run, Pallas kernels for 0% -> 1%
where the time goes in v5:
time: 137 us
  blocking collectives  79.6 us (58%)
  starting transfers between devices  29.1 us (21%)
  local copies, waits for them, and re-layouts  11.2 us (8%)
  waiting for transfers between devices  9.55 us (7%)
  Pallas kernels  4.58 us (3%)
  other arithmetic  1.93 us (1%)
    all_to_all x1, blocking collectives, on_device(): got = lax.all_to_all(send, SPLIT, 0, 0)  24 us
    all_gather x1, blocking collectives, on_device(): lax.all_gather(mine.reshape(QUARTERS, X * ROWS, COLS), ('e', 'q'), axis=0)  23.9 us
    all_gather x1, blocking collectives, on_device(): block = lax.all_gather(block, ('h', 'l'), axis=0)  21.7 us
    unnamed x36, local copies, waits for them, and re-layouts  11.1 us
    all_to_all x1, starting transfers between devices, on_device(): mine = lax.all_to_all(send, SPLIT, 0, 0)  10.2 us
    all_gather x2, blocking collectives, on_device(): lax.all_gather(block[i:i + cut], 'c', axis=1, tiled=True)  9.98 us
    all_to_all x1, starting transfers between devices, on_device(): sums = lax.all_to_all(part, 'h', 0, 0)  8.51 us
    all_to_all x1, waiting for transfers between devices, on_device(): sums = lax.all_to_all(part, 'h', 0, 0)  7.88 us
  transfers between devices with their start and end apart: 4, of which 2 were waited for; matrix products, arithmetic and copies ran while one was open for 1% of the time, Pallas kernels for 1%

profile of v5, /device:TPU:1, one launch (start us, length us, event | category | flops | bytes accessed | tf_op | source)
XLA Modules:
  0.0 136.7 jit_solution(14761747800551250941)
XLA Ops:
  0.7 1.0 copy-done.10
  2.3 0.8 shard_map.95
  3.2 10.2 %all-to-all-start = ((bf16[16,8,448]{2,1,0:T(8,128)(2,1)}), bf16[16,8,448]{2,1,0:T(8,128)(2,1)S(1)}, u32[]{:S(2)}, u32[]{:S(2)}) async-start(bf16[16,8,448]{2,1,0:T(8,128)(2,1)} %shard_map.95), calls=%async_computation | async-start | bytes 262144 | tf_op jit(solution)/shard_map/all_to_all | solution.py:172
  13.4 0.7 copy-done.8
  16.9 1.0 copy-done.1
  17.9 1.7 %all-to-all-done = bf16[16,8,448]{2,1,0:T(8,128)(2,1)S(1)} async-done(((bf16[16,8,448]{2,1,0:T(8,128)(2,1)}), bf16[16,8,448]{2,1,0:T(8,128)(2,1)S(1)}, u32[]{:S(2)}, u32[]{:S(2)}) %all-to-all-start) | async-done | bytes 114720 | tf_op jit(solution)/shard_map/all_to_all | solution.py:172
  19.6 4.1 %all-to-all-start.1 = ((bf16[16,272,128]{2,1,0:T(8,128)(2,1)}), bf16[16,272,128]{2,1,0:T(8,128)(2,1)S(1)}, u32[]{:S(2)}, u32[]{:S(2)}) async-start(bf16[16,272,128]{2,1,0:T(8,128)(2,1)} %copy-done.1), calls=%async_computation.1 | async-start | bytes 2228224 | tf_op jit(solution)/shard_map/all_to_all | solution.py:182
  23.7 23.9 %all_gather.15.mine_ref = bf16[8,4,32,448]{3,2,1,0:T(8,128)(2,1)} all-gather(bf16[1,4,32,448]{3,2,1,0:T(8,128)(2,1)S(1)} %bitcast.29), channel_id=1, replica_groups=mesh['h'=4,'l'=2,'c'=2,'e'=2,'q'=4,'x'=4] {'e','q'}, dimensions={0}, use_global_device_ids=true | all-gather | bytes 1032192 | tf_op jit(solution)/shard_map/all_gather | solution.py:183
  47.6 1.2 copy-done.2
  48.8 0.8 shard_map.96
  49.6 0.8 copy-done.5
  50.4 0.8 copy-done.6
  51.2 8.5 %all-to-all-start.2 = ((bf16[4,4,32,448]{3,2,1,0:T(8,128)(2,1)}), bf16[4,4,32,448]{3,2,1,0:T(8,128)(2,1)S(1)}, u32[]{:S(2)}, u32[]{:S(2)}) async-start(bf16[4,4,32,448]{3,2,1,0:T(8,128)(2,1)} %copy-done.5), calls=%async_computation.2 | async-start | bytes 1048576 | tf_op jit(solution)/shard_map/all_to_all | solution.py:191
  59.7 1.0 copy-done.7
  61.5 0.8 copy-done.3
  62.2 7.9 %all-to-all-done.2.sums_ref = bf16[4,4,32,448]{3,2,1,0:T(8,128)(2,1)S(1)} async-done(((bf16[4,4,32,448]{3,2,1,0:T(8,128)(2,1)}), bf16[4,4,32,448]{3,2,1,0:T(8,128)(2,1)S(1)}, u32[]{:S(2)}, u32[]{:S(2)}) %all-to-all-start.2) | async-done | bytes 458784 | tf_op jit(solution)/shard_map/all_to_all | solution.py:191
  70.1 1.0 copy-done.4
  71.3 24.0 %all_to_all.29.got_ref = bf16[16,160,128]{2,1,0:T(8,128)(2,1)S(1)} all-to-all(bf16[16,160,128]{2,1,0:T(8,128)(2,1)S(1)} %shard_map.98), channel_id=1, replica_groups=mesh['h'=4,'l'=2,'c'=2,'e'=2,'q'=4,'x'=4] {'l','c','x'}, dimensions={0} | all-to-all | bytes 1310720 | tf_op jit(solution)/shard_map/all_to_all | solution.py:200
  95.3 1.5 %shard_map.99 = (bf16[128,128]{1,0:T(8,128)(2,1)}, f32[32,8]{1,0:T(8,128)}, bf16[8,7168]{1,0:T(8,128)(2,1)S(1)}) custom-call(s32[1]{0:T(128)} %bitcast.where_ref, s32[1,2]{1,0:T(1,128)S(1)} %copy-done.16, s32[2,128]{1,0:T(2,128)S(1)} %bitcast.23, f32[2,128]{1,0:T(2,128)S(1)} %bitcast.25, bf16[128,128]{1,0:T(8,128)(2,1)S(1)} %bitcast.21, ...), custom_call_target="tpu_custom_call" | custom-call | bytes 838668 | tf_op jit(solution)/shard_map/pallas_call | solution.py:154
  96.8 6.3 %all-to-all-start.4 = ((f32[32,1,8]{2,1,0:T(1,128)}), f32[32,1,8]{2,1,0:T(1,128)S(1)}, u32[]{:S(2)}, u32[]{:S(2)}) async-start(f32[32,1,8]{2,1,0:T(1,128)} %bitcast.12), calls=%async_computation.4 | async-start | bytes 32768 | tf_op jit(solution)/shard_map/all_to_all | solution.py:207
  103.1 21.7 %all-gather = bf16[64,7168]{1,0:T(8,128)(2,1)S(1)} all-gather(bf16[8,7168]{1,0:T(8,128)(2,1)S(1)} %get-tuple-element.15), channel_id=2, replica_groups=mesh['h'=4,'l'=2,'c'=2,'e'=2,'q'=4,'x'=4] {'h','l'}, dimensions={0}, use_global_device_ids=true | all-gather | bytes 1032192 | tf_op jit(solution)/shard_map/all_gather | solution.py:210
  124.8 7.5 %all_gather.18 = bf16[4,16,7168]{2,1,0:T(8,128)(2,1)S(1)} all-gather(bf16[4,8,7168]{2,1,0:T(8,128)(2,1)S(1)} %get-tuple-element.17), channel_id=1, replica_groups=mesh['h'=4,'l'=2,'c'=2,'e'=2,'q'=4,'x'=4] {'c'}, dimensions={1}, use_global_device_ids=true | all-gather | bytes 1376256 | tf_op jit(solution)/shard_map/all_gather | solution.py:212
  132.3 2.5 %all_gather.19 = bf16[4,16,7168]{2,1,0:T(8,128)(2,1)S(1)} all-gather(bf16[4,8,7168]{2,1,0:T(8,128)(2,1)S(1)} %get-tuple-element.18), channel_id=1, replica_groups=mesh['h'=4,'l'=2,'c'=2,'e'=2,'q'=4,'x'=4] {'c'}, dimensions={1}, use_global_device_ids=true | all-gather | bytes 1376256 | tf_op jit(solution)/shard_map/all_gather | solution.py:212
  134.8 1.4 pad_maximum_fusion
  (35 shorter events, 4.9 us)
Async XLA Ops:
  0.6 12.7 %copy-start = (bf16[128,7168]{1,0:T(8,128)(2,1)S(1)}, bf16[128,7168]{1,0:T(8,128)(2,1)}, u32[]{:S(2)}) copy-start(bf16[128,7168]{1,0:T(8,128)(2,1)} %param.10) | copy-start | bytes 5505028
  0.6 1.0 copy-start.10
  1.7 0.7 copy-start.17
  3.2 16.4 %all-to-all-start = ((bf16[16,8,448]{2,1,0:T(8,128)(2,1)}), bf16[16,8,448]{2,1,0:T(8,128)(2,1)S(1)}, u32[]{:S(2)}, u32[]{:S(2)}) async-start(bf16[16,8,448]{2,1,0:T(8,128)(2,1)} %shard_map.95), calls=%async_computation | async-start | bytes 262144 | tf_op jit(solution)/shard_map/all_to_all | solution.py:172
  13.4 0.8 copy-start.8
  14.2 0.7 copy-start.11
  14.9 0.7 copy-start.13
  15.5 0.7 copy-start.15
  16.9 1.0 copy-start.1
  19.6 28.0 %all-to-all-start.1 = ((bf16[16,272,128]{2,1,0:T(8,128)(2,1)}), bf16[16,272,128]{2,1,0:T(8,128)(2,1)S(1)}, u32[]{:S(2)}, u32[]{:S(2)}) async-start(bf16[16,272,128]{2,1,0:T(8,128)(2,1)} %copy-done.1), calls=%async_computation.1 | async-start | bytes 2228224 | tf_op jit(solution)/shard_map/all_to_all | solution.py:182
  47.6 1.2 copy-start.2
  49.6 0.8 copy-start.5
  50.4 0.8 copy-start.6
  51.2 18.9 %all-to-all-start.2 = ((bf16[4,4,32,448]{3,2,1,0:T(8,128)(2,1)}), bf16[4,4,32,448]{3,2,1,0:T(8,128)(2,1)S(1)}, u32[]{:S(2)}, u32[]{:S(2)}) async-start(bf16[4,4,32,448]{3,2,1,0:T(8,128)(2,1)} %copy-done.5), calls=%async_computation.2 | async-start | bytes 1048576 | tf_op jit(solution)/shard_map/all_to_all | solution.py:191
  59.7 1.0 copy-start.7
  61.4 0.8 copy-start.3
  70.1 1.0 copy-start.4
  71.2 24.1 %copy-start.9 = (bf16[1,128,128]{2,1,0:T(8,128)(2,1)S(1)}, bf16[1,128,128]{2,1,0:T(8,128)(2,1)}, u32[]{:S(2)}) copy-start(bf16[1,128,128]{2,1,0:T(8,128)(2,1)} %param.9) | copy-start | bytes 98308
  71.2 24.1 %copy-start.12 = (s32[1,2,128]{2,1,0:T(2,128)S(1)}, s32[1,2,128]{2,1,0:T(2,128)}, u32[]{:S(2)}) copy-start(s32[1,2,128]{2,1,0:T(2,128)} %param.11) | copy-start | bytes 3076
  71.2 24.1 %copy-start.14 = (f32[1,2,128]{2,1,0:T(2,128)S(1)}, f32[1,2,128]{2,1,0:T(2,128)}, u32[]{:S(2)}) copy-start(f32[1,2,128]{2,1,0:T(2,128)} %param.13) | copy-start | bytes 3076
  71.2 24.1 %copy-start.16 = (s32[1,2]{1,0:T(1,128)S(1)}, s32[1,2]{1,0:T(1,128)}, u32[]{:S(2)}) copy-start(s32[1,2]{1,0:T(1,128)} %count_ref.3) | copy-start | bytes 28
  96.8 39.4 %all-to-all-start.4 = ((f32[32,1,8]{2,1,0:T(1,128)}), f32[32,1,8]{2,1,0:T(1,128)S(1)}, u32[]{:S(2)}, u32[]{:S(2)}) async-start(f32[32,1,8]{2,1,0:T(1,128)} %bitcast.12), calls=%async_computation.4 | async-start | bytes 32768 | tf_op jit(solution)/shard_map/all_to_all | solution.py:207

commit v6 on v5

--- a/solution.py
+++ b/solution.py
@@ -6,18 +6,18 @@
 from jax.sharding import PartitionSpec as P
 
 BF, F32, I32 = jnp.bfloat16, jnp.float32, jnp.int32
-DP, EXPERT = ("h", "l", "c"), ("e", "q", "x")
-H, L, C, E, Q, X = SIZES = (4, 2, 2, 2, 4, 4)
+DP, EXPERT = ("h", "l", "c"), ("e", "m", "n", "x")
+H, L, C, E, M, N, X = SIZES = (4, 2, 2, 2, 2, 2, 4)
 SPLIT = ("l", "c", "x")
 QUARTERS, PARTS = L * C, L * C * X
 LANES, TILES = 128, 4
 WIDTH, SLOTS, UNITS, ROWS = 7168, 128, 128, 8
-GROUP = E * Q * X * ROWS
+GROUP = E * M * N * X * ROWS
 COLS, WIDE = WIDTH // PARTS, TILES * LANES
 PAIR = 2 * COLS
 SHARE = UNITS // QUARTERS
 CHUNK = UNITS // H
-PER = CHUNK // QUARTERS
+PER = CHUNK // C
 EXTRA = 16
 PACK = SLOTS + EXTRA
 BACK = TILES * PER
@@ -46,7 +46,9 @@
     scaled = values_ref[...].astype(F32) * column(scales_ref[...].astype(F32))
     for l in range(L):
         for n in range(C * X):
-            out_ref[l * C * X + n] = slice_of(scaled, n, l)[:, :COLS].astype(BF)
+            part = slice_of(scaled, n, l)[:, :COLS].astype(BF)
+            for i in range(N):
+                out_ref[((l * C + n // X) * N + i) * X + n % X] = part
 
 
 def own_slots(where_ref, tok_ref, count_ref):
@@ -116,7 +118,8 @@
             total = total + sums_ref[h, x].astype(F32)
         total = jnp.concatenate([total, jnp.zeros((CHUNK, WIDE - COLS), F32)], axis=1)
         for g in range(QUARTERS):
-            rows = total[g * PER : (g + 1) * PER]
+            c = g % C
+            rows = total[c * PER : (c + 1) * PER]
             rows = [rows[:, t * LANES : (t + 1) * LANES] for t in range(TILES)]
             out_ref[g * X + x, 0:BACK, :] = jnp.concatenate(rows, axis=0).astype(BF)
             out_ref[g * X + x, BACK:, :] = proj_ref[g * X + x]
@@ -131,7 +134,7 @@
     grad_ref[...] = (own_gate(where_ref, gate_ref) * project).astype(BF)
     partial = jnp.sum(hidden_ref[...].astype(F32) * project, axis=1, keepdims=True)
     tok = column(own_slots(where_ref, tok_ref, count_ref))
-    device = jnp.where(lanes((SLOTS, E * Q * X)) == tok // ROWS, 1.0, 0.0)
+    device = jnp.where(lanes((SLOTS, E * M * N * X)) == tok // ROWS, 1.0, 0.0)
     row = jnp.where(lanes((SLOTS, ROWS)) == tok % ROWS, partial, 0.0)
     spread_ref[...] = lax.dot_general(
         device, row, (((0,), (0,)), ((), ())), precision=lax.Precision.HIGHEST, preferred_element_type=F32
@@ -167,9 +170,9 @@
     where = owner[None].astype(I32)
 
     (send,) = call(
-        tokens_kernel, [((PARTS, ROWS, COLS), BF)], grad_values, grad_scales.reshape(1, ROWS)
-    )
-    mine = lax.all_to_all(send, SPLIT, 0, 0)
+        tokens_kernel, [((N * PARTS, ROWS, COLS), BF)], grad_values, grad_scales.reshape(1, ROWS)
+    )
+    mine = lax.all_to_all(send, ("l", "c", "n", "x"), 0, 0)
 
     w_rows = lax.dynamic_slice_in_dim(down_weight, (low * C + core) * SHARE, SHARE, 0)
     (pack,) = call(
@@ -180,7 +183,7 @@
     )
     pack, mine = lax.optimization_barrier((pack, mine))
     pack = lax.all_to_all(pack, SPLIT, 0, 0)
-    mine = lax.all_gather(mine.reshape(QUARTERS, X * ROWS, COLS), ("e", "q"), axis=0)
+    mine = lax.all_gather(mine.reshape(QUARTERS, N * X * ROWS, COLS), ("e", "m"), axis=0)
 
     part, routed = call(
         weight_kernel,
@@ -200,15 +203,15 @@
     got = lax.all_to_all(send, SPLIT, 0, 0)
     hidden_grad, spread, block = call(
         finish_kernel,
-        [((SLOTS, UNITS), BF), ((E * Q * X, ROWS), F32), ((PER, WIDTH), BF)],
+        [((SLOTS, UNITS), BF), ((E * M * N * X, ROWS), F32), ((PER, WIDTH), BF)],
         where, slot_count, tok, gate, hidden, got,
         scalars=2,
     )
     spread = lax.all_to_all(spread, EXPERT, 0, 0)
-    gate_grad = spread.reshape(E, Q * X, ROWS).sum(axis=1).T
-
-    block = lax.all_gather(block, ("h", "l"), axis=0)
-    cut = H * L // 2
+    gate_grad = spread.reshape(E, M * N * X, ROWS).sum(axis=1).T
+
+    block = lax.all_gather(block, "h", axis=0)
+    cut = H // 2
     halves = [lax.all_gather(block[i : i + cut], "c", axis=1, tiled=True) for i in (0, cut)]
     weight_grad = jnp.concatenate([a.reshape(-1, WIDTH) for a in halves], axis=0)
     return hidden_grad[None], weight_grad, gate_grad

time: 137 us -> 132 us (0.964)
  blocking collectives: 79.6 us -> 73.2 us
  waiting for transfers between devices: 9.55 us -> 13.5 us
  local copies, waits for them, and re-layouts: 11.2 us -> 8.49 us
    all_to_all x1, waiting for transfers between devices: 1.66 us -> 6.51 us  [on_device(): mine = lax.all_to_all(send, ('l', 'c', 'n', 'x'), 0, 0)]
    all_gather x2, blocking collectives: 45.6 us -> 41 us  [the longest x1 21.4 us: on_device(): lax.all_gather(mine.reshape(QUARTERS, N * X * ROWS, COLS), ('e', 'm'), ax...]
    all_gather x2, blocking collectives: 9.98 us -> 6.19 us  [on_device(): lax.all_gather(block[i:i + cut], 'c', axis=1, tiled=True)]
    unnamed x36 -> x28, local copies, waits for them, and re-layouts: 11.1 us -> 8.39 us
    all_to_all x1, blocking collectives: 24 us -> 26.1 us  [on_device(): got = lax.all_to_all(send, SPLIT, 0, 0)]
where the time goes in v6:
time: 132 us; the launch traced here: 131 us
  blocking collectives  73.2 us (55%)
  starting transfers between devices  28.8 us (22%)
  waiting for transfers between devices  13.5 us (10%)
  local copies, waits for them, and re-layouts  8.49 us (6%)
  Pallas kernels  4.63 us (4%)
  other arithmetic  1.93 us (1%)
    all_to_all x1, blocking collectives, on_device(): got = lax.all_to_all(send, SPLIT, 0, 0)  26.1 us
    all_gather x1, blocking collectives, on_device(): lax.all_gather(mine.reshape(QUARTERS, N * X * ROWS, COLS), ('e', 'm'), ax...  21.4 us
    all_gather x1, blocking collectives, on_device(): block = lax.all_gather(block, 'h', axis=0)  19.6 us
    all_to_all x1, starting transfers between devices, on_device(): mine = lax.all_to_all(send, ('l', 'c', 'n', 'x'), 0, 0)  10.4 us
    all_to_all x1, starting transfers between devices, on_device(): sums = lax.all_to_all(part, 'h', 0, 0)  9.01 us
    unnamed x28, local copies, waits for them, and re-layouts  8.39 us
    all_to_all x1, waiting for transfers between devices, on_device(): sums = lax.all_to_all(part, 'h', 0, 0)  6.98 us
    all_to_all x1, waiting for transfers between devices, on_device(): mine = lax.all_to_all(send, ('l', 'c', 'n', 'x'), 0, 0)  6.51 us
  transfers between devices with their start and end apart: 4, of which 2 were waited for; matrix products, arithmetic and copies ran while one was open for 1% of the time, Pallas kernels for 1%

profile of v6, /device:TPU:1, one launch (start us, length us, event | category | flops | bytes accessed | tf_op | source)
XLA Modules:
  0.0 131.4 jit_solution(7119828342900863993)
XLA Ops:
  0.7 1.0 copy-done.9
  2.4 0.9 shard_map.95
  3.2 10.4 %all-to-all-start = ((bf16[32,8,448]{2,1,0:T(8,128)(2,1)}), bf16[32,8,448]{2,1,0:T(8,128)(2,1)S(1)}, u32[]{:S(2)}, u32[]{:S(2)}) async-start(bf16[32,8,448]{2,1,0:T(8,128)(2,1)} %shard_map.95), calls=%async_computation | async-start | bytes 524288 | tf_op jit(solution)/shard_map/all_to_all | solution.py:175
  13.8 0.7 shard_map.94
  14.5 1.0 copy-done.1
  15.5 6.5 %all-to-all-done = bf16[32,8,448]{2,1,0:T(8,128)(2,1)S(1)} async-done(((bf16[32,8,448]{2,1,0:T(8,128)(2,1)}), bf16[32,8,448]{2,1,0:T(8,128)(2,1)S(1)}, u32[]{:S(2)}, u32[]{:S(2)}) %all-to-all-start) | async-done | bytes 229408 | tf_op jit(solution)/shard_map/all_to_all | solution.py:175
  22.0 3.9 %all-to-all-start.1 = ((bf16[16,272,128]{2,1,0:T(8,128)(2,1)}), bf16[16,272,128]{2,1,0:T(8,128)(2,1)S(1)}, u32[]{:S(2)}, u32[]{:S(2)}) async-start(bf16[16,272,128]{2,1,0:T(8,128)(2,1)} %copy-done.1), calls=%async_computation.1 | async-start | bytes 2228224 | tf_op jit(solution)/shard_map/all_to_all | solution.py:185
  25.9 21.4 %all_gather.15.mine_ref = bf16[4,4,64,448]{3,2,1,0:T(8,128)(2,1)} all-gather(bf16[1,4,64,448]{3,2,1,0:T(8,128)(2,1)S(1)} %bitcast.29), channel_id=1, replica_groups=mesh['h'=4,'l'=2,'c'=2,'e'=2,'m'=2,'n'=2,'x'=4] {'e','m'}, dimensions={0}, use_global_device_ids=true | all-gather | bytes 1146880 | tf_op jit(solution)/shard_map/all_gather | solution.py:186
  47.3 1.2 copy-done.2
  48.6 0.8 shard_map.96
  49.4 0.8 copy-done.5
  50.2 0.8 copy-done.6
  51.0 9.0 %all-to-all-start.2 = ((bf16[4,4,32,448]{3,2,1,0:T(8,128)(2,1)}), bf16[4,4,32,448]{3,2,1,0:T(8,128)(2,1)S(1)}, u32[]{:S(2)}, u32[]{:S(2)}) async-start(bf16[4,4,32,448]{3,2,1,0:T(8,128)(2,1)} %copy-done.5), calls=%async_computation.2 | async-start | bytes 1048576 | tf_op jit(solution)/shard_map/all_to_all | solution.py:194
  60.0 1.0 copy-done.7
  61.7 0.8 copy-done.3
  62.5 7.0 %all-to-all-done.2.sums_ref = bf16[4,4,32,448]{3,2,1,0:T(8,128)(2,1)S(1)} async-done(((bf16[4,4,32,448]{3,2,1,0:T(8,128)(2,1)}), bf16[4,4,32,448]{3,2,1,0:T(8,128)(2,1)S(1)}, u32[]{:S(2)}, u32[]{:S(2)}) %all-to-all-start.2) | async-done | bytes 458784 | tf_op jit(solution)/shard_map/all_to_all | solution.py:194
  69.5 1.0 copy-done.4
  70.6 26.1 %all_to_all.29.got_ref = bf16[16,192,128]{2,1,0:T(8,128)(2,1)S(1)} all-to-all(bf16[16,192,128]{2,1,0:T(8,128)(2,1)S(1)} %shard_map.98), channel_id=1, replica_groups=mesh['h'=4,'l'=2,'c'=2,'e'=2,'m'=2,'n'=2,'x'=4] {'l','c','x'}, dimensions={0} | all-to-all | bytes 1572864 | tf_op jit(solution)/shard_map/all_to_all | solution.py:203
  96.7 1.5 %shard_map.99 = (bf16[128,128]{1,0:T(8,128)(2,1)}, f32[32,8]{1,0:T(8,128)}, bf16[16,7168]{1,0:T(8,128)(2,1)S(1)}) custom-call(s32[1]{0:T(128)} %bitcast.where_ref, s32[1,2]{1,0:T(1,128)S(1)} %copy-done.12, s32[2,128]{1,0:T(2,128)S(1)} %bitcast.21, f32[2,128]{1,0:T(2,128)S(1)} %bitcast.23, bf16[128,128]{1,0:T(8,128)(2,1)S(1)} %bitcast.19, ...), custom_call_target="tpu_custom_call" | custom-call | bytes 1084428 | tf_op jit(solution)/shard_map/pallas_call | solution.py:157
  98.2 5.4 %all-to-all-start.4 = ((f32[32,1,8]{2,1,0:T(1,128)}), f32[32,1,8]{2,1,0:T(1,128)S(1)}, u32[]{:S(2)}, u32[]{:S(2)}) async-start(f32[32,1,8]{2,1,0:T(1,128)} %bitcast.12), calls=%async_computation.4 | async-start | bytes 32768 | tf_op jit(solution)/shard_map/all_to_all | solution.py:210
  103.6 19.6 %all-gather = bf16[64,7168]{1,0:T(8,128)(2,1)S(1)} all-gather(bf16[16,7168]{1,0:T(8,128)(2,1)S(1)} %get-tuple-element.15), channel_id=2, replica_groups=mesh['h'=4,'l'=2,'c'=2,'e'=2,'m'=2,'n'=2,'x'=4] {'h'}, dimensions={0}, use_global_device_ids=true | all-gather | bytes 1146880 | tf_op jit(solution)/shard_map/all_gather | solution.py:213
  123.2 3.7 %all_gather.19 = bf16[2,32,7168]{2,1,0:T(8,128)(2,1)S(1)} all-gather(bf16[2,16,7168]{2,1,0:T(8,128)(2,1)S(1)} %bitcast.28), channel_id=1, replica_groups=mesh['h'=4,'l'=2,'c'=2,'e'=2,'m'=2,'n'=2,'x'=4] {'c'}, dimensions={1}, use_global_device_ids=true | all-gather | bytes 1376256 | tf_op jit(solution)/shard_map/all_gather | solution.py:215
  127.0 2.5 %all_gather.18 = bf16[2,32,7168]{2,1,0:T(8,128)(2,1)S(1)} all-gather(bf16[2,16,7168]{2,1,0:T(8,128)(2,1)S(1)} %bitcast.27), channel_id=1, replica_groups=mesh['h'=4,'l'=2,'c'=2,'e'=2,'m'=2,'n'=2,'x'=4] {'c'}, dimensions={1}, use_global_device_ids=true | all-gather | bytes 1376256 | tf_op jit(solution)/shard_map/all_gather | solution.py:215
  129.4 1.4 %pad_maximum_fusion = bf16[128,7168]{1,0:T(8,128)(2,1)} fusion(bf16[64,7168]{1,0:T(8,128)(2,1)S(1)} %bitcast.25, bf16[64,7168]{1,0:T(8,128)(2,1)S(1)} %bitcast.26), kind=kLoop, calls=%fused_computation | loop fusion | flops 3670016 | bytes 3670016 | tf_op jit(solution)/shard_map/concatenate | solution.py:216
  (27 shorter events, 2.2 us)
Async XLA Ops:
  0.6 13.1 %copy-start = (bf16[128,7168]{1,0:T(8,128)(2,1)S(1)}, bf16[128,7168]{1,0:T(8,128)(2,1)}, u32[]{:S(2)}) copy-start(bf16[128,7168]{1,0:T(8,128)(2,1)} %param.10) | copy-start | bytes 5505028
  0.6 13.1 %copy-start.8 = (bf16[1,128,128]{2,1,0:T(8,128)(2,1)S(1)}, bf16[1,128,128]{2,1,0:T(8,128)(2,1)}, u32[]{:S(2)}) copy-start(bf16[1,128,128]{2,1,0:T(8,128)(2,1)} %param.9) | copy-start | bytes 98308
  0.7 1.0 copy-start.9
  1.7 0.7 copy-start.13
  2.3 11.4 %copy-start.10 = (s32[1,2,128]{2,1,0:T(2,128)S(1)}, s32[1,2,128]{2,1,0:T(2,128)}, u32[]{:S(2)}) copy-start(s32[1,2,128]{2,1,0:T(2,128)} %param.11) | copy-start | bytes 3076
  2.3 11.4 %copy-start.11 = (f32[1,2,128]{2,1,0:T(2,128)S(1)}, f32[1,2,128]{2,1,0:T(2,128)}, u32[]{:S(2)}) copy-start(f32[1,2,128]{2,1,0:T(2,128)} %param.13) | copy-start | bytes 3076
  2.3 11.4 %copy-start.12 = (s32[1,2]{1,0:T(1,128)S(1)}, s32[1,2]{1,0:T(1,128)}, u32[]{:S(2)}) copy-start(s32[1,2]{1,0:T(1,128)} %count_ref.3) | copy-start | bytes 28
  3.2 18.8 %all-to-all-start = ((bf16[32,8,448]{2,1,0:T(8,128)(2,1)}), bf16[32,8,448]{2,1,0:T(8,128)(2,1)S(1)}, u32[]{:S(2)}, u32[]{:S(2)}) async-start(bf16[32,8,448]{2,1,0:T(8,128)(2,1)} %shard_map.95), calls=%async_computation | async-start | bytes 524288 | tf_op jit(solution)/shard_map/all_to_all | solution.py:175
  14.5 1.0 copy-start.1
  22.0 25.3 %all-to-all-start.1 = ((bf16[16,272,128]{2,1,0:T(8,128)(2,1)}), bf16[16,272,128]{2,1,0:T(8,128)(2,1)S(1)}, u32[]{:S(2)}, u32[]{:S(2)}) async-start(bf16[16,272,128]{2,1,0:T(8,128)(2,1)} %copy-done.1), calls=%async_computation.1 | async-start | bytes 2228224 | tf_op jit(solution)/shard_map/all_to_all | solution.py:185
  47.3 1.2 copy-start.2
  49.4 0.8 copy-start.5
  50.1 0.8 copy-start.6
  51.0 18.6 %all-to-all-start.2 = ((bf16[4,4,32,448]{3,2,1,0:T(8,128)(2,1)}), bf16[4,4,32,448]{3,2,1,0:T(8,128)(2,1)S(1)}, u32[]{:S(2)}, u32[]{:S(2)}) async-start(bf16[4,4,32,448]{3,2,1,0:T(8,128)(2,1)} %copy-done.5), calls=%async_computation.2 | async-start | bytes 1048576 | tf_op jit(solution)/shard_map/all_to_all | solution.py:194
  60.0 1.0 copy-start.7
  61.7 0.8 copy-start.3
  69.5 1.0 copy-start.4
  98.2 32.6 %all-to-all-start.4 = ((f32[32,1,8]{2,1,0:T(1,128)}), f32[32,1,8]{2,1,0:T(1,128)S(1)}, u32[]{:S(2)}, u32[]{:S(2)}) async-start(f32[32,1,8]{2,1,0:T(1,128)} %bitcast.12), calls=%async_computation.4 | async-start | bytes 32768 | tf_op jit(solution)/shard_map/all_to_all | solution.py:210

commit v7 on v6

--- a/solution.py
+++ b/solution.py
@@ -21,6 +21,7 @@
 EXTRA = 16
 PACK = SLOTS + EXTRA
 BACK = TILES * PER
+OWNED = E * M * N * ROWS
 
 
 def lanes(shape):
@@ -61,16 +62,31 @@
     return column(jnp.where(where_ref[0] == 0, gate_ref[0:1, :], gate_ref[1:2, :]))
 
 
+def split3(a):
+    high = a.astype(BF)
+    rest = a - high.astype(F32)
+    mid = rest.astype(BF)
+    return high.astype(F32), mid.astype(F32), rest - mid.astype(F32)
+
+
+def stack_rows(rows):
+    shape = (EXTRA, rows[0].shape[1])
+    at, out = lax.broadcasted_iota(I32, shape, 0), jnp.zeros(shape, F32)
+    for i, row in enumerate(rows):
+        out = jnp.where(at == i, row, out)
+    return out.astype(BF)
+
+
 def pack_kernel(where_ref, count_ref, tok_ref, gate_ref, hidden_ref, w_ref, out_ref):
-    weighted = (own_gate(where_ref, gate_ref) * hidden_ref[...].astype(F32)).astype(BF)
+    gate = jnp.where(where_ref[0] == 0, gate_ref[0:1, :], gate_ref[1:2, :])
     tok = own_slots(where_ref, tok_ref, count_ref).astype(F32)
-    tok = jnp.broadcast_to(tok, (EXTRA, SLOTS)).astype(BF)
+    extra = stack_rows((tok,) + split3(gate))
     w = w_ref[...].astype(F32)
     for l in range(L):
         for n in range(C * X):
             at = l * C * X + n
-            out_ref[at, 0:SLOTS, :] = weighted
-            out_ref[at, SLOTS:PACK, :] = tok
+            out_ref[at, 0:SLOTS, :] = hidden_ref[...]
+            out_ref[at, SLOTS:PACK, :] = extra
             part = slice_of(w, n, l).astype(BF)
             for t in range(TILES):
                 low = PACK + t * SHARE
@@ -81,22 +97,37 @@
     routed_ref[:, COLS:] = jnp.zeros((QUARTERS * SLOTS, WIDE - COLS), BF)
     ids = lax.broadcasted_iota(I32, (GROUP, SLOTS), 0)
     first = (((0,), (0,)), ((), ()))
+    gates = []
     for g in range(QUARTERS):
-        tok = pack_ref[g * X, SLOTS:PACK, :].astype(F32)[0:1, :].astype(I32)
-        picks = jnp.where(ids == tok, 1.0, 0.0).astype(BF)
+        extra = pack_ref[g * X, SLOTS:PACK, :].astype(F32)
+        gates.append(column(extra[1:2] + extra[2:3] + extra[3:4]))
+        picks = jnp.where(ids == extra[0:1].astype(I32), 1.0, 0.0).astype(BF)
         rows = mine_ref[:, g].reshape(GROUP, COLS)
-        routed = lax.dot_general(picks, rows, first, preferred_element_type=F32)
-        routed_ref[g * SLOTS : (g + 1) * SLOTS, :COLS] = routed.astype(BF)
-    routed = routed_ref[:, :COLS]
+        rows = lax.dot_general(picks, rows, first, preferred_element_type=F32)
+        routed_ref[g * SLOTS : (g + 1) * SLOTS, :COLS] = rows.astype(BF)
+    rows = routed_ref[:, :COLS]
     for x in range(X):
-        weighted = jnp.concatenate([pack_ref[g * X + x, :SLOTS, :] for g in range(QUARTERS)], axis=0)
-        part = lax.dot_general(weighted, routed, first, preferred_element_type=F32).astype(BF)
+        weighted = [
+            (gates[g] * pack_ref[g * X + x, :SLOTS, :].astype(F32)).astype(BF) for g in range(QUARTERS)
+        ]
+        weighted = jnp.concatenate(weighted, axis=0)
+        part = lax.dot_general(weighted, rows, first, preferred_element_type=F32).astype(BF)
         for h in range(H):
             part_ref[h, x] = part[h * CHUNK : (h + 1) * CHUNK]
 
 
-def project_kernel(routed_ref, pack_ref, out_ref):
+def back_kernel(sums_ref, routed_ref, pack_ref, out_ref):
+    for x in range(X):
+        total = sums_ref[0, x].astype(F32)
+        for h in range(1, H):
+            total = total + sums_ref[h, x].astype(F32)
+        total = jnp.concatenate([total, jnp.zeros((CHUNK, WIDE - COLS), F32)], axis=1).astype(BF)
+        for g in range(QUARTERS):
+            rows = total[g % C * PER : (g % C + 1) * PER]
+            for t in range(TILES):
+                out_ref[g * X + x, t * PER : (t + 1) * PER, :] = rows[:, t * LANES : (t + 1) * LANES]
     routed = routed_ref[...]
+    gates = [jnp.zeros((SLOTS, 1), F32)] * QUARTERS
     for x in range(X):
         w = [
             jnp.concatenate(
@@ -108,36 +139,36 @@
         w = jnp.concatenate(w, axis=1)
         proj = lax.dot_general(routed, w, (((1,), (1,)), ((), ())), preferred_element_type=F32)
         for g in range(QUARTERS):
-            out_ref[g * X + x] = proj[g * SLOTS : (g + 1) * SLOTS].astype(BF)
-
-
-def back_kernel(sums_ref, proj_ref, out_ref):
-    for x in range(X):
-        total = sums_ref[0, x].astype(F32)
-        for h in range(1, H):
-            total = total + sums_ref[h, x].astype(F32)
-        total = jnp.concatenate([total, jnp.zeros((CHUNK, WIDE - COLS), F32)], axis=1)
-        for g in range(QUARTERS):
-            c = g % C
-            rows = total[c * PER : (c + 1) * PER]
-            rows = [rows[:, t * LANES : (t + 1) * LANES] for t in range(TILES)]
-            out_ref[g * X + x, 0:BACK, :] = jnp.concatenate(rows, axis=0).astype(BF)
-            out_ref[g * X + x, BACK:, :] = proj_ref[g * X + x]
-
-
-def finish_kernel(
-    where_ref, count_ref, tok_ref, gate_ref, hidden_ref, got_ref, grad_ref, spread_ref, block_ref
-):
-    project = got_ref[0, BACK:, :].astype(F32)
+            rows = proj[g * SLOTS : (g + 1) * SLOTS]
+            out_ref[g * X + x, BACK : BACK + SLOTS, :] = rows.astype(BF)
+            hidden = pack_ref[g * X + x, :SLOTS, :].astype(F32)
+            gates[g] = gates[g] + jnp.sum(hidden * rows, axis=1, keepdims=True)
+    at = lanes((SLOTS, LANES))
+    for g in range(QUARTERS):
+        tok = column(pack_ref[g * X, SLOTS:PACK, :].astype(F32)[0:1]).astype(I32)
+        device, spot = tok // ROWS, tok % ROWS
+        spot = jnp.where(tok < GROUP, device // X * ROWS + spot, LANES)
+        for x in range(X):
+            here = (at == spot) & (device % X == x)
+            row = jnp.sum(jnp.where(here, gates[g], 0.0), axis=0, keepdims=True)
+            high, mid, low = split3(row)
+            out_ref[g * X + x, BACK + SLOTS :, :] = stack_rows((high + pltpu.roll(mid, OWNED, 1), low))
+
+
+def finish_kernel(where_ref, gate_ref, got_ref, grad_ref, spread_ref, block_ref):
+    project = got_ref[0, BACK : BACK + SLOTS, :].astype(F32)
+    gates = got_ref[0, BACK + SLOTS :, :].astype(F32)
     for n in range(1, PARTS):
-        project = project + got_ref[n, BACK:, :].astype(F32)
+        project = project + got_ref[n, BACK : BACK + SLOTS, :].astype(F32)
+        gates = gates + got_ref[n, BACK + SLOTS :, :].astype(F32)
     grad_ref[...] = (own_gate(where_ref, gate_ref) * project).astype(BF)
-    partial = jnp.sum(hidden_ref[...].astype(F32) * project, axis=1, keepdims=True)
-    tok = column(own_slots(where_ref, tok_ref, count_ref))
-    device = jnp.where(lanes((SLOTS, E * M * N * X)) == tok // ROWS, 1.0, 0.0)
-    row = jnp.where(lanes((SLOTS, ROWS)) == tok % ROWS, partial, 0.0)
-    spread_ref[...] = lax.dot_general(
-        device, row, (((0,), (0,)), ((), ())), precision=lax.Precision.HIGHEST, preferred_element_type=F32
+    row = gates[0:1] + (pltpu.roll(gates[0:1], OWNED, 1) + gates[1:2])
+    shape = (E * M * N, LANES)
+    row = jnp.where(lanes(shape) // ROWS == lax.broadcasted_iota(I32, shape, 0), row, 0.0)
+    shape = (LANES, ROWS)
+    fold = jnp.where(lax.broadcasted_iota(I32, shape, 0) % ROWS == lanes(shape), 1.0, 0.0)
+    spread_ref[...] = jnp.dot(
+        row, fold, precision=lax.Precision.HIGHEST, preferred_element_type=F32
     )
     low = lanes((PER, LANES)) < COLS % LANES
     for n in range(C * X):
@@ -151,13 +182,13 @@
 VM, SM = pl.BlockSpec(memory_space=pltpu.VMEM), pl.BlockSpec(memory_space=pltpu.SMEM)
 
 
-def call(kernel, outs, *args, scalars=0, flops=0):
+def call(kernel, places, outs, *args, flops=0):
     outs = [jax.ShapeDtypeStruct(s, d) for s, d in outs]
     nbytes = sum(a.size * a.dtype.itemsize for a in list(args) + outs)
     return pl.pallas_call(
         kernel,
         out_shape=outs,
-        in_specs=[SM] * scalars + [VM] * (len(args) - scalars),
+        in_specs=places,
         out_specs=[VM] * len(outs),
         cost_estimate=pl.CostEstimate(flops=flops, bytes_accessed=nbytes, transcendentals=0),
         compiler_params=pltpu.CompilerParams(vmem_limit_bytes=32 * 1024 * 1024),
@@ -170,16 +201,19 @@
     where = owner[None].astype(I32)
 
     (send,) = call(
-        tokens_kernel, [((N * PARTS, ROWS, COLS), BF)], grad_values, grad_scales.reshape(1, ROWS)
+        tokens_kernel,
+        [VM, VM],
+        [((N * PARTS, ROWS, COLS), BF)],
+        grad_values, grad_scales.reshape(1, ROWS),
     )
     mine = lax.all_to_all(send, ("l", "c", "n", "x"), 0, 0)
 
     w_rows = lax.dynamic_slice_in_dim(down_weight, (low * C + core) * SHARE, SHARE, 0)
     (pack,) = call(
         pack_kernel,
+        [SM, SM, VM, VM, VM, VM],
         [((PARTS, PACK + TILES * SHARE, LANES), BF)],
         where, slot_count, tok, gate, hidden, w_rows,
-        scalars=2,
     )
     pack, mine = lax.optimization_barrier((pack, mine))
     pack = lax.all_to_all(pack, SPLIT, 0, 0)
@@ -187,28 +221,29 @@
 
     part, routed = call(
         weight_kernel,
+        [VM, VM],
         [((H, X, CHUNK, COLS), BF), ((QUARTERS * SLOTS, WIDE), BF)],
         mine, pack,
         flops=2 * QUARTERS * SLOTS * COLS * (GROUP + X * UNITS),
     )
     sums = lax.all_to_all(part, "h", 0, 0)
-    (proj,) = call(
-        project_kernel,
-        [((PARTS, SLOTS, UNITS), BF)],
-        routed, pack,
+
+    (send,) = call(
+        back_kernel,
+        [VM, VM, VM],
+        [((PARTS, BACK + PACK, LANES), BF)],
+        sums, routed, pack,
         flops=2 * QUARTERS * SLOTS * WIDE * X * UNITS,
     )
-
-    (send,) = call(back_kernel, [((PARTS, BACK + SLOTS, LANES), BF)], sums, proj)
     got = lax.all_to_all(send, SPLIT, 0, 0)
     hidden_grad, spread, block = call(
         finish_kernel,
-        [((SLOTS, UNITS), BF), ((E * M * N * X, ROWS), F32), ((PER, WIDTH), BF)],
-        where, slot_count, tok, gate, hidden, got,
-        scalars=2,
-    )
-    spread = lax.all_to_all(spread, EXPERT, 0, 0)
-    gate_grad = spread.reshape(E, M * N * X, ROWS).sum(axis=1).T
+        [SM, VM, VM],
+        [((SLOTS, UNITS), BF), ((E * M * N, ROWS), F32), ((PER, WIDTH), BF)],
+        where, gate, got,
+    )
+    spread = lax.all_to_all(spread, ("e", "m", "n"), 0, 0, tiled=True)
+    gate_grad = spread.reshape(E, M * N, ROWS).sum(axis=1).T
 
     block = lax.all_gather(block, "h", axis=0)
     cut = H // 2

time: 132 us -> 129 us (0.977)
  blocking collectives: 73.2 us -> 92.5 us
  starting transfers between devices: 28.8 us -> 18.6 us
  waiting for transfers between devices: 13.5 us -> 6.52 us
  local copies, waits for them, and re-layouts: 8.49 us -> 4.01 us
    all_to_all x0 -> x1, blocking collectives: none -> 20.3 us  [on_device(): sums = lax.all_to_all(part, 'h', 0, 0)]
    all_to_all x2 -> x1, starting transfers between devices: 14.4 us -> 4.26 us  [on_device(): spread = lax.all_to_all(spread, ('e', 'm', 'n'), 0, 0, tiled=True)]
    all_to_all x2 -> x1, waiting for transfers between devices: 6.99 us -> 0.01 us  [on_device(): spread = lax.all_to_all(spread, ('e', 'm', 'n'), 0, 0, tiled=True)]
    unnamed x28 -> x18, local copies, waits for them, and re-layouts: 8.39 us -> 3.91 us
    all_gather x2, blocking collectives: 6.19 us -> 8.61 us  [on_device(): lax.all_gather(block[i:i + cut], 'c', axis=1, tiled=True)]
    all_gather x1, blocking collectives: 19.6 us -> 17.4 us  [on_device(): block = lax.all_gather(block, 'h', axis=0)]
    pallas_call x6 -> x5, Pallas kernels: 4.63 us -> 4.34 us  [call(): pl.pallas_call(kernel, out_shape=outs, in_specs=places, out_specs=[VM] *...]
  transfers between devices with their start and end apart: 4 -> 3, of which waited for: 2 -> 1; matrix products, arithmetic and copies ran while one was open for 1% -> 1% of each run, Pallas kernels for 1% -> 1%
where the time goes in v7:
time: 129 us
  blocking collectives  92.5 us (72%)
  starting transfers between devices  18.6 us (14%)
  waiting for transfers between devices  6.52 us (5%)
  Pallas kernels  4.34 us (3%)
  local copies, waits for them, and re-layouts  4.01 us (3%)
  other arithmetic  1.93 us (1%)
    all_to_all x1, blocking collectives, on_device(): got = lax.all_to_all(send, SPLIT, 0, 0)  24.8 us
    all_gather x1, blocking collectives, on_device(): lax.all_gather(mine.reshape(QUARTERS, N * X * ROWS, COLS), ('e', 'm'), ax...  21.4 us
    all_to_all x1, blocking collectives, on_device(): sums = lax.all_to_all(part, 'h', 0, 0)  20.3 us
    all_gather x1, blocking collectives, on_device(): block = lax.all_gather(block, 'h', axis=0)  17.4 us
    all_to_all x1, starting transfers between devices, on_device(): mine = lax.all_to_all(send, ('l', 'c', 'n', 'x'), 0, 0)  10.4 us
    all_gather x2, blocking collectives, on_device(): lax.all_gather(block[i:i + cut], 'c', axis=1, tiled=True)  8.61 us
    all_to_all x1, waiting for transfers between devices, on_device(): mine = lax.all_to_all(send, ('l', 'c', 'n', 'x'), 0, 0)  6.52 us
    pallas_call x5, Pallas kernels, call(): pl.pallas_call(kernel, out_shape=outs, in_specs=places, out_specs=[VM] *...  4.34 us
  transfers between devices with their start and end apart: 3, of which 1 were waited for; matrix products, arithmetic and copies ran while one was open for 1% of the time, Pallas kernels for 1%

profile of v7, /device:TPU:1, one launch (start us, length us, event | category | flops | bytes accessed | tf_op | source)
XLA Modules:
  0.0 128.7 jit_solution(10279874415176906351)
XLA Ops:
  0.6 0.0 copy-start
  0.7 1.0 copy-done.3
  1.7 0.7 copy-done.7
  2.4 0.9 shard_map.95
  3.2 10.4 %all-to-all-start = ((bf16[32,8,448]{2,1,0:T(8,128)(2,1)}), bf16[32,8,448]{2,1,0:T(8,128)(2,1)S(1)}, u32[]{:S(2)}, u32[]{:S(2)}) async-start(bf16[32,8,448]{2,1,0:T(8,128)(2,1)} %shard_map.95), calls=%async_computation | async-start | bytes 524288 | tf_op jit(solution)/shard_map/all_to_all | solution.py:209
  13.8 0.7 shard_map.94
  14.5 0.0 copy-start.1
  14.5 1.0 copy-done.1
  15.5 6.5 %all-to-all-done = bf16[32,8,448]{2,1,0:T(8,128)(2,1)S(1)} async-done(((bf16[32,8,448]{2,1,0:T(8,128)(2,1)}), bf16[32,8,448]{2,1,0:T(8,128)(2,1)S(1)}, u32[]{:S(2)}, u32[]{:S(2)}) %all-to-all-start) | async-done | bytes 229408 | tf_op jit(solution)/shard_map/all_to_all | solution.py:209
  22.0 3.9 %all-to-all-start.1 = ((bf16[16,272,128]{2,1,0:T(8,128)(2,1)}), bf16[16,272,128]{2,1,0:T(8,128)(2,1)S(1)}, u32[]{:S(2)}, u32[]{:S(2)}) async-start(bf16[16,272,128]{2,1,0:T(8,128)(2,1)} %copy-done.1), calls=%async_computation.1 | async-start | bytes 2228224 | tf_op jit(solution)/shard_map/all_to_all | solution.py:219
  25.9 21.4 %all_gather.15.mine_ref = bf16[4,4,64,448]{3,2,1,0:T(8,128)(2,1)} all-gather(bf16[1,4,64,448]{3,2,1,0:T(8,128)(2,1)S(1)} %bitcast.25), channel_id=1, replica_groups=mesh['h'=4,'l'=2,'c'=2,'e'=2,'m'=2,'n'=2,'x'=4] {'e','m'}, dimensions={0}, use_global_device_ids=true | all-gather | bytes 1146880 | tf_op jit(solution)/shard_map/all_gather | solution.py:220
  47.4 1.2 copy-done.2
  48.6 0.8 shard_map.96
  49.4 20.3 %all_to_all.29.sums_ref = bf16[4,4,32,448]{3,2,1,0:T(8,128)(2,1)S(1)} all-to-all(bf16[4,4,32,448]{3,2,1,0:T(8,128)(2,1)S(1)} %get-tuple-element.12), channel_id=1, replica_groups=mesh['h'=4,'l'=2,'c'=2,'e'=2,'m'=2,'n'=2,'x'=4] {'h'}, dimensions={0} | all-to-all | bytes 917504 | tf_op jit(solution)/shard_map/all_to_all | solution.py:229
  69.7 1.1 shard_map.97
  70.8 24.8 %all_to_all.30.got_ref = bf16[16,208,128]{2,1,0:T(8,128)(2,1)S(1)} all-to-all(bf16[16,208,128]{2,1,0:T(8,128)(2,1)S(1)} %shard_map.97), channel_id=1, replica_groups=mesh['h'=4,'l'=2,'c'=2,'e'=2,'m'=2,'n'=2,'x'=4] {'l','c','x'}, dimensions={0} | all-to-all | bytes 1703936 | tf_op jit(solution)/shard_map/all_to_all | solution.py:238
  95.6 0.8 shard_map.98
  96.4 4.3 %all-to-all-start.4 = ((f32[8,1,8]{2,1,0:T(1,128)}), f32[8,1,8]{2,1,0:T(1,128)S(1)}, u32[]{:S(2)}, u32[]{:S(2)}) async-start(f32[8,1,8]{2,1,0:T(1,128)} %bitcast.12), calls=%async_computation.4 | async-start | bytes 8192 | tf_op jit(solution)/shard_map/all_to_all | solution.py:245
  100.7 17.4 %all-gather = bf16[64,7168]{1,0:T(8,128)(2,1)S(1)} all-gather(bf16[16,7168]{1,0:T(8,128)(2,1)S(1)} %get-tuple-element.15), channel_id=2, replica_groups=mesh['h'=4,'l'=2,'c'=2,'e'=2,'m'=2,'n'=2,'x'=4] {'h'}, dimensions={0}, use_global_device_ids=true | all-gather | bytes 1146880 | tf_op jit(solution)/shard_map/all_gather | solution.py:248
  118.1 0.1 fusion
  118.2 6.2 %all_gather.19 = bf16[2,32,7168]{2,1,0:T(8,128)(2,1)S(1)} all-gather(bf16[2,16,7168]{2,1,0:T(8,128)(2,1)S(1)} %bitcast.24), channel_id=1, replica_groups=mesh['h'=4,'l'=2,'c'=2,'e'=2,'m'=2,'n'=2,'x'=4] {'c'}, dimensions={1}, use_global_device_ids=true | all-gather | bytes 1376256 | tf_op jit(solution)/shard_map/all_gather | solution.py:250
  124.3 2.5 %all_gather.18 = bf16[2,32,7168]{2,1,0:T(8,128)(2,1)S(1)} all-gather(bf16[2,16,7168]{2,1,0:T(8,128)(2,1)S(1)} %bitcast.23), channel_id=1, replica_groups=mesh['h'=4,'l'=2,'c'=2,'e'=2,'m'=2,'n'=2,'x'=4] {'c'}, dimensions={1}, use_global_device_ids=true | all-gather | bytes 1376256 | tf_op jit(solution)/shard_map/all_gather | solution.py:250
  126.8 1.4 %pad_maximum_fusion = bf16[128,7168]{1,0:T(8,128)(2,1)} fusion(bf16[64,7168]{1,0:T(8,128)(2,1)S(1)} %bitcast.21, bf16[64,7168]{1,0:T(8,128)(2,1)S(1)} %bitcast.22), kind=kLoop, calls=%fused_computation | loop fusion | flops 3670016 | bytes 3670016 | tf_op jit(solution)/shard_map/concatenate | solution.py:251
  128.1 0.6 reduce_sum.9
  (15 shorter events, 0.1 us)
Async XLA Ops:
  0.6 13.1 %copy-start = (bf16[128,7168]{1,0:T(8,128)(2,1)S(1)}, bf16[128,7168]{1,0:T(8,128)(2,1)}, u32[]{:S(2)}) copy-start(bf16[128,7168]{1,0:T(8,128)(2,1)} %param.10) | copy-start | bytes 5505028
  0.6 13.1 %copy-start.5 = (f32[1,2,128]{2,1,0:T(2,128)S(1)}, f32[1,2,128]{2,1,0:T(2,128)}, u32[]{:S(2)}) copy-start(f32[1,2,128]{2,1,0:T(2,128)} %param.13) | copy-start | bytes 3076
  0.7 13.1 %copy-start.8 = (s32[1,2]{1,0:T(1,128)S(1)}, s32[1,2]{1,0:T(1,128)}, u32[]{:S(2)}) copy-start(s32[1,2]{1,0:T(1,128)} %count_ref.1) | copy-start | bytes 28
  0.7 1.0 copy-start.3
  1.7 0.7 copy-start.7
  2.4 11.4 %copy-start.4 = (bf16[1,128,128]{2,1,0:T(8,128)(2,1)S(1)}, bf16[1,128,128]{2,1,0:T(8,128)(2,1)}, u32[]{:S(2)}) copy-start(bf16[1,128,128]{2,1,0:T(8,128)(2,1)} %param.9) | copy-start | bytes 98308
  2.4 11.4 %copy-start.6 = (s32[1,2,128]{2,1,0:T(2,128)S(1)}, s32[1,2,128]{2,1,0:T(2,128)}, u32[]{:S(2)}) copy-start(s32[1,2,128]{2,1,0:T(2,128)} %param.11) | copy-start | bytes 3076
  3.2 18.8 %all-to-all-start = ((bf16[32,8,448]{2,1,0:T(8,128)(2,1)}), bf16[32,8,448]{2,1,0:T(8,128)(2,1)S(1)}, u32[]{:S(2)}, u32[]{:S(2)}) async-start(bf16[32,8,448]{2,1,0:T(8,128)(2,1)} %shard_map.95), calls=%async_computation | async-start | bytes 524288 | tf_op jit(solution)/shard_map/all_to_all | solution.py:209
  14.5 1.0 copy-start.1
  22.0 25.3 %all-to-all-start.1 = ((bf16[16,272,128]{2,1,0:T(8,128)(2,1)}), bf16[16,272,128]{2,1,0:T(8,128)(2,1)S(1)}, u32[]{:S(2)}, u32[]{:S(2)}) async-start(bf16[16,272,128]{2,1,0:T(8,128)(2,1)} %copy-done.1), calls=%async_computation.1 | async-start | bytes 2228224 | tf_op jit(solution)/shard_map/all_to_all | solution.py:219
  47.4 1.2 copy-start.2
  96.4 31.7 %all-to-all-start.4 = ((f32[8,1,8]{2,1,0:T(1,128)}), f32[8,1,8]{2,1,0:T(1,128)S(1)}, u32[]{:S(2)}, u32[]{:S(2)}) async-start(f32[8,1,8]{2,1,0:T(1,128)} %bitcast.12), calls=%async_computation.4 | async-start | bytes 8192 | tf_op jit(solution)/shard_map/all_to_all | solution.py:245

commit v8 on v7

--- a/solution.py
+++ b/solution.py
@@ -17,10 +17,11 @@
 PAIR = 2 * COLS
 SHARE = UNITS // QUARTERS
 CHUNK = UNITS // H
-PER = CHUNK // C
 EXTRA = 16
 PACK = SLOTS + EXTRA
-BACK = TILES * PER
+WHOLE, HALF = (TILES - 1) * CHUNK, CHUNK // 2
+BACK = WHOLE + HALF
+TAIL = COLS % LANES
 OWNED = E * M * N * ROWS
 
 
@@ -93,7 +94,7 @@
                 out_ref[at, low : low + SHARE, :] = part[:, t * LANES : (t + 1) * LANES]
 
 
-def weight_kernel(mine_ref, pack_ref, part_ref, routed_ref):
+def weight_kernel(core_ref, mine_ref, pack_ref, part_ref, keep_ref, send_ref, routed_ref):
     routed_ref[:, COLS:] = jnp.zeros((QUARTERS * SLOTS, WIDE - COLS), BF)
     ids = lax.broadcasted_iota(I32, (GROUP, SLOTS), 0)
     first = (((0,), (0,)), ((), ()))
@@ -105,29 +106,28 @@
         rows = mine_ref[:, g].reshape(GROUP, COLS)
         rows = lax.dot_general(picks, rows, first, preferred_element_type=F32)
         routed_ref[g * SLOTS : (g + 1) * SLOTS, :COLS] = rows.astype(BF)
-    rows = routed_ref[:, :COLS]
+    routed = routed_ref[...]
+
     for x in range(X):
         weighted = [
             (gates[g] * pack_ref[g * X + x, :SLOTS, :].astype(F32)).astype(BF) for g in range(QUARTERS)
         ]
         weighted = jnp.concatenate(weighted, axis=0)
-        part = lax.dot_general(weighted, rows, first, preferred_element_type=F32).astype(BF)
+        part = lax.dot_general(weighted, routed, first, preferred_element_type=F32)
         for h in range(H):
-            part_ref[h, x] = part[h * CHUNK : (h + 1) * CHUNK]
-
-
-def back_kernel(sums_ref, routed_ref, pack_ref, out_ref):
-    for x in range(X):
-        total = sums_ref[0, x].astype(F32)
-        for h in range(1, H):
-            total = total + sums_ref[h, x].astype(F32)
-        total = jnp.concatenate([total, jnp.zeros((CHUNK, WIDE - COLS), F32)], axis=1).astype(BF)
-        for g in range(QUARTERS):
-            rows = total[g % C * PER : (g % C + 1) * PER]
-            for t in range(TILES):
-                out_ref[g * X + x, t * PER : (t + 1) * PER, :] = rows[:, t * LANES : (t + 1) * LANES]
-    routed = routed_ref[...]
-    gates = [jnp.zeros((SLOTS, 1), F32)] * QUARTERS
+            rows = part[h * CHUNK : (h + 1) * CHUNK]
+            for t in range(TILES - 1):
+                part_ref[h, x, t * CHUNK : (t + 1) * CHUNK, :] = rows[:, t * LANES : (t + 1) * LANES].astype(BF)
+            rows = rows[:, WIDE - LANES :]
+            part_ref[h, x, WHOLE:, :] = (rows[:HALF] + pltpu.roll(rows[HALF:], TAIL, 1)).astype(BF)
+
+    core = core_ref[0]
+    groups = [l * C + c for c in (core, 1 - core) for l in range(L)]
+    outs = [(ref, l) for ref in (keep_ref, send_ref) for l in range(L)]
+    routed = jnp.concatenate(
+        [routed_ref[pl.ds(pl.multiple_of(g * SLOTS, SLOTS), SLOTS), :] for g in groups], axis=0
+    )
+    sums = [jnp.zeros((SLOTS, 1), F32)] * QUARTERS
     for x in range(X):
         w = [
             jnp.concatenate(
@@ -138,51 +138,74 @@
         ]
         w = jnp.concatenate(w, axis=1)
         proj = lax.dot_general(routed, w, (((1,), (1,)), ((), ())), preferred_element_type=F32)
-        for g in range(QUARTERS):
-            rows = proj[g * SLOTS : (g + 1) * SLOTS]
-            out_ref[g * X + x, BACK : BACK + SLOTS, :] = rows.astype(BF)
-            hidden = pack_ref[g * X + x, :SLOTS, :].astype(F32)
-            gates[g] = gates[g] + jnp.sum(hidden * rows, axis=1, keepdims=True)
+        for i, (ref, l) in enumerate(outs):
+            rows = proj[i * SLOTS : (i + 1) * SLOTS]
+            ref[l * X + x, 0:SLOTS, :] = rows.astype(BF)
+            hidden = pack_ref[groups[i] * X + x, :SLOTS, :].astype(F32)
+            sums[i] = sums[i] + jnp.sum(hidden * rows, axis=1, keepdims=True)
     at = lanes((SLOTS, LANES))
-    for g in range(QUARTERS):
-        tok = column(pack_ref[g * X, SLOTS:PACK, :].astype(F32)[0:1]).astype(I32)
+    for i, (ref, l) in enumerate(outs):
+        tok = column(pack_ref[groups[i] * X, SLOTS:PACK, :].astype(F32)[0:1]).astype(I32)
         device, spot = tok // ROWS, tok % ROWS
         spot = jnp.where(tok < GROUP, device // X * ROWS + spot, LANES)
         for x in range(X):
             here = (at == spot) & (device % X == x)
-            row = jnp.sum(jnp.where(here, gates[g], 0.0), axis=0, keepdims=True)
-            high, mid, low = split3(row)
-            out_ref[g * X + x, BACK + SLOTS :, :] = stack_rows((high + pltpu.roll(mid, OWNED, 1), low))
+            row = jnp.sum(jnp.where(here, sums[i], 0.0), axis=0, keepdims=True)
+            ref[l * X + x, SLOTS:PACK, :] = terms(row)
+
+
+def terms(row):
+    high, mid, low = split3(row)
+    return stack_rows((high + pltpu.roll(mid, OWNED, 1), low))
+
+
+def row_of(tile):
+    row = tile[0:1] + (pltpu.roll(tile[0:1], OWNED, 1) + tile[1:2])
+    return jnp.where(lanes(row.shape) < OWNED, row, 0.0)
+
+
+def back_kernel(sums_ref, keep_ref, other_ref, out_ref):
+    for x in range(X):
+        total = sums_ref[0, x].astype(F32)
+        for h in range(1, H):
+            total = total + sums_ref[h, x].astype(F32)
+        for l in range(L):
+            out_ref[l * X + x, 0:BACK, :] = total.astype(BF)
+    for n in range(L * X):
+        both = keep_ref[n].astype(F32) + other_ref[n].astype(F32)
+        out_ref[n, BACK : BACK + SLOTS, :] = both[:SLOTS].astype(BF)
+        out_ref[n, BACK + SLOTS :, :] = terms(row_of(both[SLOTS:]))
 
 
 def finish_kernel(where_ref, gate_ref, got_ref, grad_ref, spread_ref, block_ref):
-    project = got_ref[0, BACK : BACK + SLOTS, :].astype(F32)
-    gates = got_ref[0, BACK + SLOTS :, :].astype(F32)
-    for n in range(1, PARTS):
-        project = project + got_ref[n, BACK : BACK + SLOTS, :].astype(F32)
-        gates = gates + got_ref[n, BACK + SLOTS :, :].astype(F32)
-    grad_ref[...] = (own_gate(where_ref, gate_ref) * project).astype(BF)
-    row = gates[0:1] + (pltpu.roll(gates[0:1], OWNED, 1) + gates[1:2])
+    both = got_ref[0, BACK:, :].astype(F32)
+    for n in range(1, L * X):
+        both = both + got_ref[n, BACK:, :].astype(F32)
+    grad_ref[...] = (own_gate(where_ref, gate_ref) * both[:SLOTS]).astype(BF)
     shape = (E * M * N, LANES)
-    row = jnp.where(lanes(shape) // ROWS == lax.broadcasted_iota(I32, shape, 0), row, 0.0)
+    row = jnp.where(lanes(shape) // ROWS == lax.broadcasted_iota(I32, shape, 0), row_of(both[SLOTS:]), 0.0)
     shape = (LANES, ROWS)
     fold = jnp.where(lax.broadcasted_iota(I32, shape, 0) % ROWS == lanes(shape), 1.0, 0.0)
     spread_ref[...] = jnp.dot(
         row, fold, precision=lax.Precision.HIGHEST, preferred_element_type=F32
     )
-    low = lanes((PER, LANES)) < COLS % LANES
-    for n in range(C * X):
-        a, b = (got_ref[l * C * X + n, 0:BACK, :].astype(F32) for l in range(L))
-        a, b = ([p[t * PER : (t + 1) * PER] for t in range(TILES)] for p in (a, b))
-        b = [pltpu.roll(p, COLS % LANES, 1) for p in b]
+    low = lanes((CHUNK, LANES)) < TAIL
+    for x in range(X):
+        a, b = (got_ref[l * X + x, 0:BACK, :].astype(F32) for l in range(L))
+        a, b = (
+            [p[t * CHUNK : (t + 1) * CHUNK] for t in range(TILES - 1)]
+            + [jnp.concatenate([p[WHOLE:], pltpu.roll(p[WHOLE:], TAIL, 1)], axis=0)]
+            for p in (a, b)
+        )
+        b = [pltpu.roll(p, TAIL, 1) for p in b]
         tiles = a[:-1] + [jnp.where(low, p, r) for p, r in zip([a[-1]] + b[:-1], b)]
-        block_ref[:, n * PAIR : (n + 1) * PAIR] = jnp.concatenate(tiles, axis=1).astype(BF)
+        block_ref[:, x * PAIR : (x + 1) * PAIR] = jnp.concatenate(tiles, axis=1).astype(BF)
 
 
 VM, SM = pl.BlockSpec(memory_space=pltpu.VMEM), pl.BlockSpec(memory_space=pltpu.SMEM)
 
 
-def call(kernel, places, outs, *args, flops=0):
+def call(kernel, places, outs, *args, scratch=(), flops=0):
     outs = [jax.ShapeDtypeStruct(s, d) for s, d in outs]
     nbytes = sum(a.size * a.dtype.itemsize for a in list(args) + outs)
     return pl.pallas_call(
@@ -190,6 +213,7 @@
         out_shape=outs,
         in_specs=places,
         out_specs=[VM] * len(outs),
+        scratch_shapes=scratch,
         cost_estimate=pl.CostEstimate(flops=flops, bytes_accessed=nbytes, transcendentals=0),
         compiler_params=pltpu.CompilerParams(vmem_limit_bytes=32 * 1024 * 1024),
     )(*args)
@@ -219,37 +243,37 @@
     pack = lax.all_to_all(pack, SPLIT, 0, 0)
     mine = lax.all_gather(mine.reshape(QUARTERS, N * X * ROWS, COLS), ("e", "m"), axis=0)
 
-    part, routed = call(
+    part, keep, other = call(
         weight_kernel,
-        [VM, VM],
-        [((H, X, CHUNK, COLS), BF), ((QUARTERS * SLOTS, WIDE), BF)],
-        mine, pack,
-        flops=2 * QUARTERS * SLOTS * COLS * (GROUP + X * UNITS),
-    )
+        [SM, VM, VM],
+        [((H, X, BACK, LANES), BF), ((L * X, PACK, LANES), BF), ((L * X, PACK, LANES), BF)],
+        core[None].astype(I32), mine, pack,
+        scratch=[pltpu.VMEM((QUARTERS * SLOTS, WIDE), BF)],
+        flops=2 * QUARTERS * SLOTS * (COLS * GROUP + 2 * WIDE * X * UNITS),
+    )
+    other = lax.ppermute(other, "c", [(i, C - 1 - i) for i in range(C)])
     sums = lax.all_to_all(part, "h", 0, 0)
 
     (send,) = call(
         back_kernel,
         [VM, VM, VM],
-        [((PARTS, BACK + PACK, LANES), BF)],
-        sums, routed, pack,
-        flops=2 * QUARTERS * SLOTS * WIDE * X * UNITS,
-    )
-    got = lax.all_to_all(send, SPLIT, 0, 0)
+        [((L * X, BACK + PACK, LANES), BF)],
+        sums, keep, other,
+    )
+    got = lax.all_to_all(send, ("l", "x"), 0, 0)
     hidden_grad, spread, block = call(
         finish_kernel,
         [SM, VM, VM],
-        [((SLOTS, UNITS), BF), ((E * M * N, ROWS), F32), ((PER, WIDTH), BF)],
+        [((SLOTS, UNITS), BF), ((E * M * N, ROWS), F32), ((CHUNK, X * PAIR), BF)],
         where, gate, got,
     )
     spread = lax.all_to_all(spread, ("e", "m", "n"), 0, 0, tiled=True)
     gate_grad = spread.reshape(E, M * N, ROWS).sum(axis=1).T
 
-    block = lax.all_gather(block, "h", axis=0)
-    cut = H // 2
+    block = lax.all_gather(block, "h", axis=0, tiled=True)
+    cut = UNITS // 2
     halves = [lax.all_gather(block[i : i + cut], "c", axis=1, tiled=True) for i in (0, cut)]
-    weight_grad = jnp.concatenate([a.reshape(-1, WIDTH) for a in halves], axis=0)
-    return hidden_grad[None], weight_grad, gate_grad
+    return hidden_grad[None], jnp.concatenate(halves, axis=0), gate_grad
 
 
 def solution(mesh):

time: 129 us -> 123 us (0.953)
  blocking collectives: 92.5 us -> 67.8 us
  starting transfers between devices: 18.6 us -> 31.8 us
  waiting for transfers between devices: 6.52 us -> 11.4 us
  Pallas kernels: 4.34 us -> 6.06 us
    all_to_all x2 -> x1, blocking collectives: 45.1 us -> 18.3 us  [on_device(): got = lax.all_to_all(send, ('l', 'x'), 0, 0)]
    all_to_all x0 -> x1, starting transfers between devices: none -> 9.01 us  [on_device(): sums = lax.all_to_all(part, 'h', 0, 0)]
    ppermute x0 -> x1, starting transfers between devices: none -> 4.35 us  [on_device(): other = lax.ppermute(other, 'c', [(i, C - 1 - i) for i in range(C)])]
    all_to_all x0 -> x1, waiting for transfers between devices: none -> 3.65 us  [on_device(): sums = lax.all_to_all(part, 'h', 0, 0)]
    pallas_call x5, Pallas kernels: 4.34 us -> 6.06 us  [call(): pl.pallas_call(kernel, out_shape=outs, in_specs=places, out_specs=[VM] *...]
    all_gather x1, blocking collectives: 17.4 us -> 18.8 us  [on_device(): block = lax.all_gather(block, 'h', axis=0, tiled=True)]
    unnamed x18 -> x16, local copies, waits for them, and re-layouts: 3.91 us -> 2.93 us
  transfers between devices with their start and end apart: 3 -> 5, of which waited for: 1 -> 3; matrix products, arithmetic and copies ran while one was open for 1% -> 1% of each run, Pallas kernels for 1% -> 1%
where the time goes in v8:
time: 123 us
  blocking collectives  67.8 us (55%)
  starting transfers between devices  31.8 us (26%)
  waiting for transfers between devices  11.4 us (9%)
  Pallas kernels  6.06 us (5%)
  local copies, waits for them, and re-layouts  3.03 us (2%)
  other arithmetic  1.93 us (2%)
    all_gather x1, blocking collectives, on_device(): lax.all_gather(mine.reshape(QUARTERS, N * X * ROWS, COLS), ('e', 'm'), ax...  21.4 us
    all_gather x1, blocking collectives, on_device(): block = lax.all_gather(block, 'h', axis=0, tiled=True)  18.8 us
    all_to_all x1, blocking collectives, on_device(): got = lax.all_to_all(send, ('l', 'x'), 0, 0)  18.3 us
    all_to_all x1, starting transfers between devices, on_device(): mine = lax.all_to_all(send, ('l', 'c', 'n', 'x'), 0, 0)  10.4 us
    all_gather x2, blocking collectives, on_device(): lax.all_gather(block[i:i + cut], 'c', axis=1, tiled=True)  9.28 us
    all_to_all x1, starting transfers between devices, on_device(): sums = lax.all_to_all(part, 'h', 0, 0)  9.01 us
    all_to_all x1, waiting for transfers between devices, on_device(): mine = lax.all_to_all(send, ('l', 'c', 'n', 'x'), 0, 0)  6.52 us
    pallas_call x5, Pallas kernels, call(): pl.pallas_call(kernel, out_shape=outs, in_specs=places, out_specs=[VM] *...  6.06 us
  transfers between devices with their start and end apart: 5, of which 3 were waited for; matrix products, arithmetic and copies ran while one was open for 1% of the time, Pallas kernels for 1%

profile of v8, /device:TPU:1, one launch (start us, length us, event | category | flops | bytes accessed | tf_op | source)
XLA Modules:
  0.0 122.8 jit_solution(12657127659827370616)
XLA Ops:
  0.7 1.0 copy-done.2
  1.7 0.7 copy-done.6
  2.4 0.9 shard_map.95
  3.2 10.4 %all-to-all-start = ((bf16[32,8,448]{2,1,0:T(8,128)(2,1)}), bf16[32,8,448]{2,1,0:T(8,128)(2,1)S(1)}, u32[]{:S(2)}, u32[]{:S(2)}) async-start(bf16[32,8,448]{2,1,0:T(8,128)(2,1)} %shard_map.95), calls=%async_computation | async-start | bytes 524288 | tf_op jit(solution)/shard_map/all_to_all | solution.py:233
  13.8 1.7 %shard_map.94 = bf16[16,272,128]{2,1,0:T(8,128)(2,1)} custom-call(s32[1]{0:T(128)} %bitcast.where_ref, s32[1,2]{1,0:T(1,128)S(1)} %copy-done.7, s32[2,128]{1,0:T(2,128)S(1)} %bitcast.16, f32[2,128]{1,0:T(2,128)S(1)} %bitcast.14, bf16[128,128]{1,0:T(8,128)(2,1)S(1)} %bitcast.13, bf16[32,7168]{1,0:T(8,128)(2,1)S(1)} %constant_dynamic-slice_fusion.w_ref), custom_call_target="tpu_custom_call" | custom-call | bytes 1607692 | tf_op jit(solution)/shard_map/pallas_call | solution.py:211
  15.5 6.5 %all-to-all-done = bf16[32,8,448]{2,1,0:T(8,128)(2,1)S(1)} async-done(((bf16[32,8,448]{2,1,0:T(8,128)(2,1)}), bf16[32,8,448]{2,1,0:T(8,128)(2,1)S(1)}, u32[]{:S(2)}, u32[]{:S(2)}) %all-to-all-start) | async-done | bytes 229408 | tf_op jit(solution)/shard_map/all_to_all | solution.py:233
  22.0 3.9 %all-to-all-start.1 = ((bf16[16,272,128]{2,1,0:T(8,128)(2,1)}), bf16[16,272,128]{2,1,0:T(8,128)(2,1)S(1)}, u32[]{:S(2)}, u32[]{:S(2)}) async-start(bf16[16,272,128]{2,1,0:T(8,128)(2,1)} %shard_map.94), calls=%async_computation.1 | async-start | bytes 2228224 | tf_op jit(solution)/shard_map/all_to_all | solution.py:243
  25.9 21.4 %all_gather.12.mine_ref = bf16[4,4,64,448]{3,2,1,0:T(8,128)(2,1)} all-gather(bf16[1,4,64,448]{3,2,1,0:T(8,128)(2,1)S(1)} %bitcast.18), channel_id=1, replica_groups=mesh['h'=4,'l'=2,'c'=2,'e'=2,'m'=2,'n'=2,'x'=4] {'e','m'}, dimensions={0}, use_global_device_ids=true | all-gather | bytes 1146880 | tf_op jit(solution)/shard_map/all_gather | solution.py:244
  47.3 1.2 copy-done.1
  48.6 2.4 %shard_map.96 = (bf16[4,4,112,128]{3,2,1,0:T(8,128)(2,1)}, bf16[8,144,128]{2,1,0:T(8,128)(2,1)S(1)}, bf16[8,144,128]{2,1,0:T(8,128)(2,1)S(1)}) custom-call(s32[1]{0:T(128)} %bitcast.2.core_ref, bf16[4,4,64,448]{3,2,1,0:T(8,128)(2,1)S(1)} %copy-done.1, bf16[16,272,128]{2,1,0:T(8,128)(2,1)S(1)} %all-to-all-done.1.pack_ref), custom_call_target="tpu_custom_call" | custom-call | flops 654311424 | bytes 3080196 | tf_op jit(solution)/shard_map/pallas_call | solution.py:211
  51.0 9.0 %all-to-all-start.2 = ((bf16[4,4,112,128]{3,2,1,0:T(8,128)(2,1)}), bf16[4,4,112,128]{3,2,1,0:T(8,128)(2,1)S(1)}, u32[]{:S(2)}, u32[]{:S(2)}) async-start(bf16[4,4,112,128]{3,2,1,0:T(8,128)(2,1)} %get-tuple-element.13), calls=%async_computation.2 | async-start | bytes 917504 | tf_op jit(solution)/shard_map/all_to_all | solution.py:255
  60.0 4.3 %collective-permute-start = (bf16[8,144,128]{2,1,0:T(8,128)(2,1)S(1)}, bf16[8,144,128]{2,1,0:T(8,128)(2,1)S(1)}, u32[]{:S(2)}, u32[]{:S(2)}) collective-permute-start(bf16[8,144,128]{2,1,0:T(8,128)(2,1)S(1)} %get-tuple-element.15), channel_id=1, source_target_pairs={{0,32},{32,0},{1,33},{33,1},{2,34},{34,2},{3,35},{35,3},{4,36},{36... | collective-permute-start | bytes 884744 | tf_op jit(solution)/shard_map/ppermute | solution.py:254
  64.4 1.2 collective-permute-done.other_ref
  65.6 3.7 %all-to-all-done.2.sums_ref = bf16[4,4,112,128]{3,2,1,0:T(8,128)(2,1)S(1)} async-done(((bf16[4,4,112,128]{3,2,1,0:T(8,128)(2,1)}), bf16[4,4,112,128]{3,2,1,0:T(8,128)(2,1)S(1)}, u32[]{:S(2)}, u32[]{:S(2)}) %all-to-all-start.2) | async-done | bytes 458784 | tf_op jit(solution)/shard_map/all_to_all | solution.py:255
  69.2 0.2 shard_map.97
  69.4 18.3 %all_to_all.29.got_ref = bf16[8,256,128]{2,1,0:T(8,128)(2,1)S(1)} all-to-all(bf16[8,256,128]{2,1,0:T(8,128)(2,1)S(1)} %shard_map.97), channel_id=1, replica_groups=mesh['h'=4,'l'=2,'c'=2,'e'=2,'m'=2,'n'=2,'x'=4] {'l','x'}, dimensions={0} | all-to-all | bytes 1048576 | tf_op jit(solution)/shard_map/all_to_all | solution.py:263
  87.8 0.8 shard_map.98
  88.6 4.1 %all-to-all-start.4 = ((f32[8,1,8]{2,1,0:T(1,128)}), f32[8,1,8]{2,1,0:T(1,128)S(1)}, u32[]{:S(2)}, u32[]{:S(2)}) async-start(f32[8,1,8]{2,1,0:T(1,128)} %bitcast.9), calls=%async_computation.4 | async-start | bytes 8192 | tf_op jit(solution)/shard_map/all_to_all | solution.py:270
  92.7 18.8 %all_gather.13 = bf16[128,3584]{1,0:T(8,128)(2,1)S(1)} all-gather(bf16[32,3584]{1,0:T(8,128)(2,1)S(1)} %get-tuple-element.17), channel_id=1, replica_groups=mesh['h'=4,'l'=2,'c'=2,'e'=2,'m'=2,'n'=2,'x'=4] {'h'}, dimensions={0}, use_global_device_ids=true | all-gather | bytes 1146880 | tf_op jit(solution)/shard_map/all_gather | solution.py:273
  111.5 0.1 fusion
  111.6 6.8 %all_gather.14 = bf16[64,7168]{1,0:T(8,128)(2,1)S(1)} all-gather(bf16[64,3584]{1,0:T(8,128)(2,1)S(1)} %get-tuple-element.19), channel_id=1, replica_groups=mesh['h'=4,'l'=2,'c'=2,'e'=2,'m'=2,'n'=2,'x'=4] {'c'}, dimensions={1}, use_global_device_ids=true | all-gather | bytes 1376256 | tf_op jit(solution)/shard_map/all_gather | solution.py:275
  118.4 2.5 %all_gather.15 = bf16[64,7168]{1,0:T(8,128)(2,1)S(1)} all-gather(bf16[64,3584]{1,0:T(8,128)(2,1)S(1)} %get-tuple-element.20), channel_id=1, replica_groups=mesh['h'=4,'l'=2,'c'=2,'e'=2,'m'=2,'n'=2,'x'=4] {'c'}, dimensions={1}, use_global_device_ids=true | all-gather | bytes 1376256 | tf_op jit(solution)/shard_map/all_gather | solution.py:275
  120.9 1.4 %pad_maximum_fusion = bf16[128,7168]{1,0:T(8,128)(2,1)} fusion(bf16[64,7168]{1,0:T(8,128)(2,1)S(1)} %all_gather.15, bf16[64,7168]{1,0:T(8,128)(2,1)S(1)} %all_gather.14), kind=kLoop, calls=%fused_computation | loop fusion | flops 3670016 | bytes 3670016 | tf_op jit(solution)/shard_map/concatenate | solution.py:276
  122.2 0.6 reduce_sum.9
  (16 shorter events, 0.1 us)
Async XLA Ops:
  0.6 13.1 %copy-start = (bf16[128,7168]{1,0:T(8,128)(2,1)S(1)}, bf16[128,7168]{1,0:T(8,128)(2,1)}, u32[]{:S(2)}) copy-start(bf16[128,7168]{1,0:T(8,128)(2,1)} %param.10) | copy-start | bytes 5505028
  0.6 13.1 %copy-start.4 = (f32[1,2,128]{2,1,0:T(2,128)S(1)}, f32[1,2,128]{2,1,0:T(2,128)}, u32[]{:S(2)}) copy-start(f32[1,2,128]{2,1,0:T(2,128)} %param.13) | copy-start | bytes 3076
  0.7 13.1 %copy-start.7 = (s32[1,2]{1,0:T(1,128)S(1)}, s32[1,2]{1,0:T(1,128)}, u32[]{:S(2)}) copy-start(s32[1,2]{1,0:T(1,128)} %count_ref.1) | copy-start | bytes 28
  0.7 1.0 copy-start.2
  1.7 0.7 copy-start.6
  2.4 11.4 %copy-start.3 = (bf16[1,128,128]{2,1,0:T(8,128)(2,1)S(1)}, bf16[1,128,128]{2,1,0:T(8,128)(2,1)}, u32[]{:S(2)}) copy-start(bf16[1,128,128]{2,1,0:T(8,128)(2,1)} %param.9) | copy-start | bytes 98308
  2.4 11.4 %copy-start.5 = (s32[1,2,128]{2,1,0:T(2,128)S(1)}, s32[1,2,128]{2,1,0:T(2,128)}, u32[]{:S(2)}) copy-start(s32[1,2,128]{2,1,0:T(2,128)} %param.11) | copy-start | bytes 3076
  3.2 18.8 %all-to-all-start = ((bf16[32,8,448]{2,1,0:T(8,128)(2,1)}), bf16[32,8,448]{2,1,0:T(8,128)(2,1)S(1)}, u32[]{:S(2)}, u32[]{:S(2)}) async-start(bf16[32,8,448]{2,1,0:T(8,128)(2,1)} %shard_map.95), calls=%async_computation | async-start | bytes 524288 | tf_op jit(solution)/shard_map/all_to_all | solution.py:233
  22.0 25.3 %all-to-all-start.1 = ((bf16[16,272,128]{2,1,0:T(8,128)(2,1)}), bf16[16,272,128]{2,1,0:T(8,128)(2,1)S(1)}, u32[]{:S(2)}, u32[]{:S(2)}) async-start(bf16[16,272,128]{2,1,0:T(8,128)(2,1)} %shard_map.94), calls=%async_computation.1 | async-start | bytes 2228224 | tf_op jit(solution)/shard_map/all_to_all | solution.py:243
  47.3 1.2 copy-start.1
  51.0 18.2 %all-to-all-start.2 = ((bf16[4,4,112,128]{3,2,1,0:T(8,128)(2,1)}), bf16[4,4,112,128]{3,2,1,0:T(8,128)(2,1)S(1)}, u32[]{:S(2)}, u32[]{:S(2)}) async-start(bf16[4,4,112,128]{3,2,1,0:T(8,128)(2,1)} %get-tuple-element.13), calls=%async_computation.2 | async-start | bytes 917504 | tf_op jit(solution)/shard_map/all_to_all | solution.py:255
  60.0 5.5 %collective-permute-start = (bf16[8,144,128]{2,1,0:T(8,128)(2,1)S(1)}, bf16[8,144,128]{2,1,0:T(8,128)(2,1)S(1)}, u32[]{:S(2)}, u32[]{:S(2)}) collective-permute-start(bf16[8,144,128]{2,1,0:T(8,128)(2,1)S(1)} %get-tuple-element.15), channel_id=1, source_target_pairs={{0,32},{32,0},{1,33},{33,1},{2,34},{34,2},{3,35},{35,3},{4,36},{36... | collective-permute-start | bytes 884744 | tf_op jit(solution)/shard_map/ppermute | solution.py:254
  88.6 33.6 %all-to-all-start.4 = ((f32[8,1,8]{2,1,0:T(1,128)}), f32[8,1,8]{2,1,0:T(1,128)S(1)}, u32[]{:S(2)}, u32[]{:S(2)}) async-start(f32[8,1,8]{2,1,0:T(1,128)} %bitcast.9), calls=%async_computation.4 | async-start | bytes 8192 | tf_op jit(solution)/shard_map/all_to_all | solution.py:270

commit v9 on v8

--- a/solution.py
+++ b/solution.py
@@ -19,9 +19,11 @@
 CHUNK = UNITS // H
 EXTRA = 16
 PACK = SLOTS + EXTRA
-WHOLE, HALF = (TILES - 1) * CHUNK, CHUNK // 2
-BACK = WHOLE + HALF
-TAIL = COLS % LANES
+FULL, TAIL = TILES - 1, COLS % LANES
+TOKS = N * X * ROWS
+BACK = FULL * CHUNK + CHUNK // 2
+W_PART = FULL * SHARE + SHARE // 2
+DENSE = FULL * TOKS + TOKS // 2
 OWNED = E * M * N * ROWS
 
 
@@ -44,11 +46,30 @@
     return jnp.where(lanes(a.shape) < COLS, a, 0.0)
 
 
-def tokens_kernel(values_ref, scales_ref, out_ref):
+def dense(a):
+    half = a.shape[0] // 2
+    last = a[:, FULL * LANES :]
+    last = last[:half] + pltpu.roll(last[half:], TAIL, 1)
+    return jnp.concatenate([a[:, t * LANES : (t + 1) * LANES] for t in range(FULL)] + [last], axis=0)
+
+
+def last_tile(a):
+    return jnp.concatenate([a, pltpu.roll(a, TAIL, 1)], axis=0)
+
+
+def tokens_kernel(values_all, scales_all, out_ref, values_ref, scales_ref, sem):
+    loads = [
+        pltpu.make_async_copy(src, dst, sem.at[i])
+        for i, (src, dst) in enumerate(((values_all, values_ref), (scales_all, scales_ref)))
+    ]
+    for load in loads:
+        load.start()
+    for load in loads:
+        load.wait()
     scaled = values_ref[...].astype(F32) * column(scales_ref[...].astype(F32))
     for l in range(L):
         for n in range(C * X):
-            part = slice_of(scaled, n, l)[:, :COLS].astype(BF)
+            part = slice_of(scaled, n, l).astype(BF)
             for i in range(N):
                 out_ref[((l * C + n // X) * N + i) * X + n % X] = part
 
@@ -88,14 +109,15 @@
             at = l * C * X + n
             out_ref[at, 0:SLOTS, :] = hidden_ref[...]
             out_ref[at, SLOTS:PACK, :] = extra
-            part = slice_of(w, n, l).astype(BF)
-            for t in range(TILES):
-                low = PACK + t * SHARE
-                out_ref[at, low : low + SHARE, :] = part[:, t * LANES : (t + 1) * LANES]
+            out_ref[at, PACK:, :] = dense(slice_of(w, n, l)).astype(BF)
+
+
+def dense_kernel(rows_ref, out_ref):
+    for g in range(QUARTERS):
+        out_ref[g] = dense(rows_ref[g].astype(F32)).astype(BF)
 
 
 def weight_kernel(core_ref, mine_ref, pack_ref, part_ref, keep_ref, send_ref, routed_ref):
-    routed_ref[:, COLS:] = jnp.zeros((QUARTERS * SLOTS, WIDE - COLS), BF)
     ids = lax.broadcasted_iota(I32, (GROUP, SLOTS), 0)
     first = (((0,), (0,)), ((), ()))
     gates = []
@@ -103,9 +125,17 @@
         extra = pack_ref[g * X, SLOTS:PACK, :].astype(F32)
         gates.append(column(extra[1:2] + extra[2:3] + extra[3:4]))
         picks = jnp.where(ids == extra[0:1].astype(I32), 1.0, 0.0).astype(BF)
-        rows = mine_ref[:, g].reshape(GROUP, COLS)
+        rows = [mine_ref[:, g, t * TOKS : (t + 1) * TOKS, :].reshape(GROUP, LANES) for t in range(FULL)]
+        rows += [
+            jnp.concatenate(
+                [last_tile(mine_ref[i, g, FULL * TOKS :, :].astype(F32)).astype(BF) for i in range(E * M)],
+                axis=0,
+            )
+        ]
+        rows = jnp.concatenate(rows, axis=1)
         rows = lax.dot_general(picks, rows, first, preferred_element_type=F32)
-        routed_ref[g * SLOTS : (g + 1) * SLOTS, :COLS] = rows.astype(BF)
+        rows = jnp.where(lanes(rows.shape) < COLS, rows, 0.0)
+        routed_ref[g * SLOTS : (g + 1) * SLOTS, :] = rows.astype(BF)
     routed = routed_ref[...]
 
     for x in range(X):
@@ -115,11 +145,7 @@
         weighted = jnp.concatenate(weighted, axis=0)
         part = lax.dot_general(weighted, routed, first, preferred_element_type=F32)
         for h in range(H):
-            rows = part[h * CHUNK : (h + 1) * CHUNK]
-            for t in range(TILES - 1):
-                part_ref[h, x, t * CHUNK : (t + 1) * CHUNK, :] = rows[:, t * LANES : (t + 1) * LANES].astype(BF)
-            rows = rows[:, WIDE - LANES :]
-            part_ref[h, x, WHOLE:, :] = (rows[:HALF] + pltpu.roll(rows[HALF:], TAIL, 1)).astype(BF)
+            part_ref[h, x] = dense(part[h * CHUNK : (h + 1) * CHUNK]).astype(BF)
 
     core = core_ref[0]
     groups = [l * C + c for c in (core, 1 - core) for l in range(L)]
@@ -129,14 +155,14 @@
     )
     sums = [jnp.zeros((SLOTS, 1), F32)] * QUARTERS
     for x in range(X):
-        w = [
-            jnp.concatenate(
-                [pack_ref[q * X + x, PACK + t * SHARE : PACK + (t + 1) * SHARE, :] for q in range(QUARTERS)],
-                axis=0,
-            )
-            for t in range(TILES)
-        ]
-        w = jnp.concatenate(w, axis=1)
+        w = []
+        for q in range(QUARTERS):
+            rows = pack_ref[q * X + x, PACK:, :]
+            rows = [rows[t * SHARE : (t + 1) * SHARE] for t in range(FULL)] + [
+                last_tile(rows[FULL * SHARE :].astype(F32)).astype(BF)
+            ]
+            w.append(jnp.concatenate(rows, axis=1))
+        w = jnp.concatenate(w, axis=0)
         proj = lax.dot_general(routed, w, (((1,), (1,)), ((), ())), preferred_element_type=F32)
         for i, (ref, l) in enumerate(outs):
             rows = proj[i * SLOTS : (i + 1) * SLOTS]
@@ -193,8 +219,7 @@
     for x in range(X):
         a, b = (got_ref[l * X + x, 0:BACK, :].astype(F32) for l in range(L))
         a, b = (
-            [p[t * CHUNK : (t + 1) * CHUNK] for t in range(TILES - 1)]
-            + [jnp.concatenate([p[WHOLE:], pltpu.roll(p[WHOLE:], TAIL, 1)], axis=0)]
+            [p[t * CHUNK : (t + 1) * CHUNK] for t in range(FULL)] + [last_tile(p[FULL * CHUNK :])]
             for p in (a, b)
         )
         b = [pltpu.roll(p, TAIL, 1) for p in b]
@@ -202,10 +227,10 @@
         block_ref[:, x * PAIR : (x + 1) * PAIR] = jnp.concatenate(tiles, axis=1).astype(BF)
 
 
-VM, SM = pl.BlockSpec(memory_space=pltpu.VMEM), pl.BlockSpec(memory_space=pltpu.SMEM)
-
-
-def call(kernel, places, outs, *args, scratch=(), flops=0):
+VM, SM, HBM = (pl.BlockSpec(memory_space=m) for m in (pltpu.VMEM, pltpu.SMEM, pl.ANY))
+
+
+def call(kernel, places, outs, *args, scratch=(), flops=0, vmem=32):
     outs = [jax.ShapeDtypeStruct(s, d) for s, d in outs]
     nbytes = sum(a.size * a.dtype.itemsize for a in list(args) + outs)
     return pl.pallas_call(
@@ -215,7 +240,7 @@
         out_specs=[VM] * len(outs),
         scratch_shapes=scratch,
         cost_estimate=pl.CostEstimate(flops=flops, bytes_accessed=nbytes, transcendentals=0),
-        compiler_params=pltpu.CompilerParams(vmem_limit_bytes=32 * 1024 * 1024),
+        compiler_params=pltpu.CompilerParams(vmem_limit_bytes=vmem * 1024 * 1024),
     )(*args)
 
 
@@ -226,9 +251,13 @@
 
     (send,) = call(
         tokens_kernel,
-        [VM, VM],
-        [((N * PARTS, ROWS, COLS), BF)],
+        [HBM, HBM],
+        [((N * PARTS, ROWS, WIDE), BF)],
         grad_values, grad_scales.reshape(1, ROWS),
+        scratch=[
+            pltpu.VMEM((ROWS, WIDTH), BF), pltpu.VMEM((1, ROWS), BF), pltpu.SemaphoreType.DMA((2,))
+        ],
+        vmem=60,
     )
     mine = lax.all_to_all(send, ("l", "c", "n", "x"), 0, 0)
 
@@ -236,12 +265,15 @@
     (pack,) = call(
         pack_kernel,
         [SM, SM, VM, VM, VM, VM],
-        [((PARTS, PACK + TILES * SHARE, LANES), BF)],
+        [((PARTS, PACK + W_PART, LANES), BF)],
         where, slot_count, tok, gate, hidden, w_rows,
     )
     pack, mine = lax.optimization_barrier((pack, mine))
     pack = lax.all_to_all(pack, SPLIT, 0, 0)
-    mine = lax.all_gather(mine.reshape(QUARTERS, N * X * ROWS, COLS), ("e", "m"), axis=0)
+    (mine,) = call(
+        dense_kernel, [VM], [((QUARTERS, DENSE, LANES), BF)], mine.reshape(QUARTERS, TOKS, WIDE)
+    )
+    mine = lax.all_gather(mine, ("e", "m"), axis=0)
 
     part, keep, other = call(
         weight_kernel,

time: 123 us -> 122 us (level)
  blocking collectives: 67.8 us -> 61.7 us
  starting transfers between devices: 31.8 us -> 36.7 us
  local copies, waits for them, and re-layouts: 3.03 us -> 1.31 us
    all_to_all x1, blocking collectives: 18.3 us -> 12.4 us  [on_device(): got = lax.all_to_all(send, ('l', 'x'), 0, 0)]
    all_to_all x1, starting transfers between devices: 4.11 us -> 9.5 us  [on_device(): spread = lax.all_to_all(spread, ('e', 'm', 'n'), 0, 0, tiled=True)]
    unnamed x16 -> x12, local copies, waits for them, and re-layouts: 2.93 us -> 1.21 us
    all_to_all x1, starting transfers between devices: 9.01 us -> 7.59 us  [on_device(): sums = lax.all_to_all(part, 'h', 0, 0)]
    pallas_call x5 -> x6, Pallas kernels: 6.06 us -> 7.17 us  [call(): pl.pallas_call(kernel, out_shape=outs, in_specs=places, out_specs=[VM] *...]
  transfers between devices with their start and end apart: 5 -> 5, of which waited for: 3 -> 3; matrix products, arithmetic and copies ran while one was open for 1% -> 1% of each run, Pallas kernels for 1% -> 2%
where the time goes in v9:
time: 122 us; the launch traced here: 121 us
  blocking collectives  61.7 us (51%)
  starting transfers between devices  36.7 us (30%)
  waiting for transfers between devices  11.5 us (9%)
  Pallas kernels  7.17 us (6%)
  other arithmetic  1.93 us (2%)
  local copies, waits for them, and re-layouts  1.31 us (1%)
    all_gather x1, blocking collectives, on_device(): mine = lax.all_gather(mine, ('e', 'm'), axis=0)  21.1 us
    all_gather x1, blocking collectives, on_device(): block = lax.all_gather(block, 'h', axis=0, tiled=True)  19.2 us
    all_to_all x1, blocking collectives, on_device(): got = lax.all_to_all(send, ('l', 'x'), 0, 0)  12.4 us
    all_to_all x1, starting transfers between devices, on_device(): mine = lax.all_to_all(send, ('l', 'c', 'n', 'x'), 0, 0)  10.5 us
    all_to_all x1, starting transfers between devices, on_device(): spread = lax.all_to_all(spread, ('e', 'm', 'n'), 0, 0, tiled=True)  9.5 us
    all_gather x2, blocking collectives, on_device(): lax.all_gather(block[i:i + cut], 'c', axis=1, tiled=True)  9.04 us
    all_to_all x1, starting transfers between devices, on_device(): sums = lax.all_to_all(part, 'h', 0, 0)  7.59 us
    pallas_call x6, Pallas kernels, call(): pl.pallas_call(kernel, out_shape=outs, in_specs=places, out_specs=[VM] *...  7.17 us
  transfers between devices with their start and end apart: 5, of which 3 were waited for; matrix products, arithmetic and copies ran while one was open for 1% of the time, Pallas kernels for 2%

profile of v9, /device:TPU:1, one launch (start us, length us, event | category | flops | bytes accessed | tf_op | source)
XLA Modules:
  0.0 121.1 jit_solution(8304455397270195173)
XLA Ops:
  0.6 0.0 copy-start
  0.7 1.9 %shard_map.95 = bf16[32,8,512]{2,1,0:T(8,128)(2,1)} custom-call(bf16[8,7168]{1,0:T(8,128)(2,1)} %values_all.1, bf16[1,8]{1,0:T(2,128)(2,1)} %bitcast.22), custom_call_target="tpu_custom_call" | custom-call | bytes 376848 | tf_op jit(solution)/shard_map/pallas_call | solution.py:236
  2.6 10.5 %all-to-all-start = ((bf16[32,8,512]{2,1,0:T(8,128)(2,1)}), bf16[32,8,512]{2,1,0:T(8,128)(2,1)S(1)}, u32[]{:S(2)}, u32[]{:S(2)}) async-start(bf16[32,8,512]{2,1,0:T(8,128)(2,1)} %shard_map.95), calls=%async_computation | async-start | bytes 524288 | tf_op jit(solution)/shard_map/all_to_all | solution.py:262
  13.2 1.8 %shard_map.94 = bf16[16,256,128]{2,1,0:T(8,128)(2,1)} custom-call(s32[1]{0:T(128)} %bitcast.where_ref, s32[1,2]{1,0:T(1,128)S(1)} %copy-done.5, s32[2,128]{1,0:T(2,128)S(1)} %bitcast.19, f32[2,128]{1,0:T(2,128)S(1)} %bitcast.17, bf16[128,128]{1,0:T(8,128)(2,1)S(1)} %bitcast.16, bf16[32,7168]{1,0:T(8,128)(2,1)S(1)} %constant_dynamic-slice_fusion.w_ref), custom_call_target="tpu_custom_call" | custom-call | bytes 1542156 | tf_op jit(solution)/shard_map/pallas_call | solution.py:236
  14.9 6.5 %all-to-all-done = bf16[32,8,512]{2,1,0:T(8,128)(2,1)S(1)} async-done(((bf16[32,8,512]{2,1,0:T(8,128)(2,1)}), bf16[32,8,512]{2,1,0:T(8,128)(2,1)S(1)}, u32[]{:S(2)}, u32[]{:S(2)}) %all-to-all-start) | async-done | bytes 262176 | tf_op jit(solution)/shard_map/all_to_all | solution.py:262
  21.4 3.9 %all-to-all-start.1 = ((bf16[16,256,128]{2,1,0:T(8,128)(2,1)}), bf16[16,256,128]{2,1,0:T(8,128)(2,1)S(1)}, u32[]{:S(2)}, u32[]{:S(2)}) async-start(bf16[16,256,128]{2,1,0:T(8,128)(2,1)} %shard_map.94), calls=%async_computation.1 | async-start | bytes 2097152 | tf_op jit(solution)/shard_map/all_to_all | solution.py:272
  25.3 0.1 shard_map.96
  25.4 21.1 %all-gather = bf16[16,224,128]{2,1,0:T(8,128)(2,1)} all-gather(bf16[4,224,128]{2,1,0:T(8,128)(2,1)S(1)} %shard_map.96), channel_id=2, replica_groups=mesh['h'=4,'l'=2,'c'=2,'e'=2,'m'=2,'n'=2,'x'=4] {'e','m'}, dimensions={0}, use_global_device_ids=true | all-gather | bytes 1146880 | tf_op jit(solution)/shard_map/all_gather | solution.py:276
  46.5 1.2 copy-done.1
  47.7 2.4 %shard_map.97 = (bf16[4,4,112,128]{3,2,1,0:T(8,128)(2,1)}, bf16[8,144,128]{2,1,0:T(8,128)(2,1)S(1)}, bf16[8,144,128]{2,1,0:T(8,128)(2,1)S(1)}) custom-call(s32[1]{0:T(128)} %bitcast.2.core_ref, bf16[4,4,224,128]{3,2,1,0:T(8,128)(2,1)S(1)} %bitcast.15, bf16[16,256,128]{2,1,0:T(8,128)(2,1)S(1)} %all-to-all-done.1.pack_ref), custom_call_target="tpu_custom_call" | custom-call | flops 654311424 | bytes 3014660 | tf_op jit(solution)/shard_map/pallas_call | solution.py:236
  50.0 7.6 %all-to-all-start.2 = ((bf16[4,4,112,128]{3,2,1,0:T(8,128)(2,1)}), bf16[4,4,112,128]{3,2,1,0:T(8,128)(2,1)S(1)}, u32[]{:S(2)}, u32[]{:S(2)}) async-start(bf16[4,4,112,128]{3,2,1,0:T(8,128)(2,1)} %get-tuple-element.13), calls=%async_computation.2 | async-start | bytes 917504 | tf_op jit(solution)/shard_map/all_to_all | solution.py:287
  57.6 5.3 %collective-permute-start = (bf16[8,144,128]{2,1,0:T(8,128)(2,1)S(1)}, bf16[8,144,128]{2,1,0:T(8,128)(2,1)S(1)}, u32[]{:S(2)}, u32[]{:S(2)}) collective-permute-start(bf16[8,144,128]{2,1,0:T(8,128)(2,1)S(1)} %get-tuple-element.15), channel_id=1, source_target_pairs={{0,32},{32,0},{1,33},{33,1},{2,34},{34,2},{3,35},{35,3},{4,36},{36... | collective-permute-start | bytes 884744 | tf_op jit(solution)/shard_map/ppermute | solution.py:286
  62.9 1.2 collective-permute-done.other_ref
  64.1 3.8 %all-to-all-done.2.sums_ref = bf16[4,4,112,128]{3,2,1,0:T(8,128)(2,1)S(1)} async-done(((bf16[4,4,112,128]{3,2,1,0:T(8,128)(2,1)}), bf16[4,4,112,128]{3,2,1,0:T(8,128)(2,1)S(1)}, u32[]{:S(2)}, u32[]{:S(2)}) %all-to-all-start.2) | async-done | bytes 458784 | tf_op jit(solution)/shard_map/all_to_all | solution.py:287
  67.9 0.2 shard_map.98
  68.1 12.4 %all_to_all.29.got_ref = bf16[8,256,128]{2,1,0:T(8,128)(2,1)S(1)} all-to-all(bf16[8,256,128]{2,1,0:T(8,128)(2,1)S(1)} %shard_map.98), channel_id=1, replica_groups=mesh['h'=4,'l'=2,'c'=2,'e'=2,'m'=2,'n'=2,'x'=4] {'l','x'}, dimensions={0} | all-to-all | bytes 1048576 | tf_op jit(solution)/shard_map/all_to_all | solution.py:295
  80.5 0.8 shard_map.99
  81.4 9.5 %all-to-all-start.4 = ((f32[8,1,8]{2,1,0:T(1,128)}), f32[8,1,8]{2,1,0:T(1,128)S(1)}, u32[]{:S(2)}, u32[]{:S(2)}) async-start(f32[8,1,8]{2,1,0:T(1,128)} %bitcast.10), calls=%async_computation.4 | async-start | bytes 8192 | tf_op jit(solution)/shard_map/all_to_all | solution.py:302
  90.9 19.2 %all_gather.17 = bf16[128,3584]{1,0:T(8,128)(2,1)S(1)} all-gather(bf16[32,3584]{1,0:T(8,128)(2,1)S(1)} %get-tuple-element.17), channel_id=1, replica_groups=mesh['h'=4,'l'=2,'c'=2,'e'=2,'m'=2,'n'=2,'x'=4] {'h'}, dimensions={0}, use_global_device_ids=true | all-gather | bytes 1146880 | tf_op jit(solution)/shard_map/all_gather | solution.py:305
  110.1 0.1 fusion
  110.1 6.6 %all_gather.18 = bf16[64,7168]{1,0:T(8,128)(2,1)S(1)} all-gather(bf16[64,3584]{1,0:T(8,128)(2,1)S(1)} %get-tuple-element.19), channel_id=1, replica_groups=mesh['h'=4,'l'=2,'c'=2,'e'=2,'m'=2,'n'=2,'x'=4] {'c'}, dimensions={1}, use_global_device_ids=true | all-gather | bytes 1376256 | tf_op jit(solution)/shard_map/all_gather | solution.py:307
  116.7 2.5 %all_gather.19 = bf16[64,7168]{1,0:T(8,128)(2,1)S(1)} all-gather(bf16[64,3584]{1,0:T(8,128)(2,1)S(1)} %get-tuple-element.20), channel_id=1, replica_groups=mesh['h'=4,'l'=2,'c'=2,'e'=2,'m'=2,'n'=2,'x'=4] {'c'}, dimensions={1}, use_global_device_ids=true | all-gather | bytes 1376256 | tf_op jit(solution)/shard_map/all_gather | solution.py:307
  119.2 1.4 %pad_maximum_fusion = bf16[128,7168]{1,0:T(8,128)(2,1)} fusion(bf16[64,7168]{1,0:T(8,128)(2,1)S(1)} %all_gather.19, bf16[64,7168]{1,0:T(8,128)(2,1)S(1)} %all_gather.18), kind=kLoop, calls=%fused_computation | loop fusion | flops 3670016 | bytes 3670016 | tf_op jit(solution)/shard_map/concatenate | solution.py:308
  120.5 0.6 reduce_sum.9
  (13 shorter events, 0.1 us)
Async XLA Ops:
  0.6 12.5 %copy-start = (bf16[128,7168]{1,0:T(8,128)(2,1)S(1)}, bf16[128,7168]{1,0:T(8,128)(2,1)}, u32[]{:S(2)}) copy-start(bf16[128,7168]{1,0:T(8,128)(2,1)} %param.10) | copy-start | bytes 5505028
  0.6 12.5 %copy-start.3 = (f32[1,2,128]{2,1,0:T(2,128)S(1)}, f32[1,2,128]{2,1,0:T(2,128)}, u32[]{:S(2)}) copy-start(f32[1,2,128]{2,1,0:T(2,128)} %param.13) | copy-start | bytes 3076
  0.7 12.5 %copy-start.5 = (s32[1,2]{1,0:T(1,128)S(1)}, s32[1,2]{1,0:T(1,128)}, u32[]{:S(2)}) copy-start(s32[1,2]{1,0:T(1,128)} %count_ref.1) | copy-start | bytes 28
  0.7 12.5 %copy-start.4 = (s32[1,2,128]{2,1,0:T(2,128)S(1)}, s32[1,2,128]{2,1,0:T(2,128)}, u32[]{:S(2)}) copy-start(s32[1,2,128]{2,1,0:T(2,128)} %param.11) | copy-start | bytes 3076
  0.7 12.5 %copy-start.2 = (bf16[1,128,128]{2,1,0:T(8,128)(2,1)S(1)}, bf16[1,128,128]{2,1,0:T(8,128)(2,1)}, u32[]{:S(2)}) copy-start(bf16[1,128,128]{2,1,0:T(8,128)(2,1)} %param.9) | copy-start | bytes 98308
  2.6 18.8 %all-to-all-start = ((bf16[32,8,512]{2,1,0:T(8,128)(2,1)}), bf16[32,8,512]{2,1,0:T(8,128)(2,1)S(1)}, u32[]{:S(2)}, u32[]{:S(2)}) async-start(bf16[32,8,512]{2,1,0:T(8,128)(2,1)} %shard_map.95), calls=%async_computation | async-start | bytes 524288 | tf_op jit(solution)/shard_map/all_to_all | solution.py:262
  21.4 25.0 %all-to-all-start.1 = ((bf16[16,256,128]{2,1,0:T(8,128)(2,1)}), bf16[16,256,128]{2,1,0:T(8,128)(2,1)S(1)}, u32[]{:S(2)}, u32[]{:S(2)}) async-start(bf16[16,256,128]{2,1,0:T(8,128)(2,1)} %shard_map.94), calls=%async_computation.1 | async-start | bytes 2097152 | tf_op jit(solution)/shard_map/all_to_all | solution.py:272
  46.5 1.2 copy-start.1
  50.0 17.9 %all-to-all-start.2 = ((bf16[4,4,112,128]{3,2,1,0:T(8,128)(2,1)}), bf16[4,4,112,128]{3,2,1,0:T(8,128)(2,1)S(1)}, u32[]{:S(2)}, u32[]{:S(2)}) async-start(bf16[4,4,112,128]{3,2,1,0:T(8,128)(2,1)} %get-tuple-element.13), calls=%async_computation.2 | async-start | bytes 917504 | tf_op jit(solution)/shard_map/all_to_all | solution.py:287
  57.6 6.5 %collective-permute-start = (bf16[8,144,128]{2,1,0:T(8,128)(2,1)S(1)}, bf16[8,144,128]{2,1,0:T(8,128)(2,1)S(1)}, u32[]{:S(2)}, u32[]{:S(2)}) collective-permute-start(bf16[8,144,128]{2,1,0:T(8,128)(2,1)S(1)} %get-tuple-element.15), channel_id=1, source_target_pairs={{0,32},{32,0},{1,33},{33,1},{2,34},{34,2},{3,35},{35,3},{4,36},{36... | collective-permute-start | bytes 884744 | tf_op jit(solution)/shard_map/ppermute | solution.py:286
  81.4 39.1 %all-to-all-start.4 = ((f32[8,1,8]{2,1,0:T(1,128)}), f32[8,1,8]{2,1,0:T(1,128)S(1)}, u32[]{:S(2)}, u32[]{:S(2)}) async-start(f32[8,1,8]{2,1,0:T(1,128)} %bitcast.10), calls=%async_computation.4 | async-start | bytes 8192 | tf_op jit(solution)/shard_map/all_to_all | solution.py:302

commit v10 on v9

--- a/solution.py
+++ b/solution.py
@@ -227,17 +227,38 @@
         block_ref[:, x * PAIR : (x + 1) * PAIR] = jnp.concatenate(tiles, axis=1).astype(BF)
 
 
+def put_columns(half_ref, out_ref, core, sem):
+    width = X * PAIR
+    copy = pltpu.make_async_copy(
+        half_ref, out_ref.at[:, pl.ds(pl.multiple_of(core * width, LANES), width)], sem
+    )
+    copy.start()
+    return copy
+
+
+def own_half_kernel(core_ref, half_ref, out_ref, sem):
+    put_columns(half_ref, out_ref, core_ref[0], sem).wait()
+
+
+def other_half_kernel(core_ref, half_ref, spread_ref, out_in_ref, out_ref, gate_ref, sem):
+    copy = put_columns(half_ref, out_ref, 1 - core_ref[0], sem)
+    for e in range(E):
+        gate_ref[e : e + 1, :] = jnp.sum(spread_ref[e * M * N : (e + 1) * M * N, :], axis=0, keepdims=True)
+    copy.wait()
+
+
 VM, SM, HBM = (pl.BlockSpec(memory_space=m) for m in (pltpu.VMEM, pltpu.SMEM, pl.ANY))
 
 
-def call(kernel, places, outs, *args, scratch=(), flops=0, vmem=32):
+def call(kernel, places, outs, *args, scratch=(), flops=0, vmem=32, out_places=None, aliases={}):
     outs = [jax.ShapeDtypeStruct(s, d) for s, d in outs]
     nbytes = sum(a.size * a.dtype.itemsize for a in list(args) + outs)
     return pl.pallas_call(
         kernel,
         out_shape=outs,
         in_specs=places,
-        out_specs=[VM] * len(outs),
+        out_specs=out_places or [VM] * len(outs),
+        input_output_aliases=aliases,
         scratch_shapes=scratch,
         cost_estimate=pl.CostEstimate(flops=flops, bytes_accessed=nbytes, transcendentals=0),
         compiler_params=pltpu.CompilerParams(vmem_limit_bytes=vmem * 1024 * 1024),
@@ -300,12 +321,25 @@
         where, gate, got,
     )
     spread = lax.all_to_all(spread, ("e", "m", "n"), 0, 0, tiled=True)
-    gate_grad = spread.reshape(E, M * N, ROWS).sum(axis=1).T
 
     block = lax.all_gather(block, "h", axis=0, tiled=True)
-    cut = UNITS // 2
-    halves = [lax.all_gather(block[i : i + cut], "c", axis=1, tiled=True) for i in (0, cut)]
-    return hidden_grad[None], jnp.concatenate(halves, axis=0), gate_grad
+    block, spread = lax.optimization_barrier((block, spread))
+    other = lax.ppermute(block, "c", [(i, C - 1 - i) for i in range(C)])
+    where = core[None].astype(I32)
+    sem = [pltpu.SemaphoreType.DMA(())]
+    (whole,) = call(
+        own_half_kernel, [SM, VM], [((UNITS, WIDTH), BF)], where, block, scratch=sem, out_places=[HBM]
+    )
+    weight_grad, gate_grad = call(
+        other_half_kernel,
+        [SM, HBM, VM, HBM],
+        [((UNITS, WIDTH), BF), ((E, ROWS), F32)],
+        where, other, spread, whole,
+        scratch=sem,
+        out_places=[HBM, VM],
+        aliases={3: 0},
+    )
+    return hidden_grad[None], weight_grad, gate_grad.T
 
 
 def solution(mesh):

time: 122 us -> 121 us (level)
  blocking collectives: 61.7 us -> 52.7 us
  starting transfers between devices: 36.7 us -> 43.1 us
  Pallas kernels: 7.17 us -> 9.61 us
  other arithmetic: 1.93 us -> 0 us
    all_gather x2 -> x0, blocking collectives: 9.04 us -> none  [on_device(): lax.all_gather(block[i:i + cut], 'c', axis=1, tiled=True)]
    ppermute x0 -> x1, starting transfers between devices: none -> 6.39 us  [on_device(): other = lax.ppermute(block, 'c', [(i, C - 1 - i) for i in range(C)])]
    pallas_call x6 -> x8, Pallas kernels: 7.17 us -> 9.61 us  [call(): pl.pallas_call(kernel, out_shape=outs, in_specs=places, out_specs=out_pla...]
    concatenate x1 -> x0, other arithmetic: 1.35 us -> none  [on_device(): return (hidden_grad[None], jnp.concatenate(halves, axis=0), gate_grad)]
  transfers between devices with their start and end apart: 5 -> 6, of which waited for: 3 -> 4; matrix products, arithmetic and copies ran while one was open for 1% -> 0% of each run, Pallas kernels for 2% -> 2%
where the time goes in v10:
time: 121 us; the launch traced here: 120 us
  blocking collectives  52.7 us (44%)
  starting transfers between devices  43.1 us (36%)
  waiting for transfers between devices  12.6 us (10%)
  Pallas kernels  9.61 us (8%)
  local copies, waits for them, and re-layouts  1.24 us (1%)
    all_gather x1, blocking collectives, on_device(): mine = lax.all_gather(mine, ('e', 'm'), axis=0)  21.1 us
    all_gather x1, blocking collectives, on_device(): block = lax.all_gather(block, 'h', axis=0, tiled=True)  19.2 us
    all_to_all x1, blocking collectives, on_device(): got = lax.all_to_all(send, ('l', 'x'), 0, 0)  12.4 us
    all_to_all x1, starting transfers between devices, on_device(): mine = lax.all_to_all(send, ('l', 'c', 'n', 'x'), 0, 0)  10.5 us
    pallas_call x8, Pallas kernels, call(): pl.pallas_call(kernel, out_shape=outs, in_specs=places, out_specs=out_pla...  9.61 us
    all_to_all x1, starting transfers between devices, on_device(): spread = lax.all_to_all(spread, ('e', 'm', 'n'), 0, 0, tiled=True)  9.5 us
    all_to_all x1, starting transfers between devices, on_device(): sums = lax.all_to_all(part, 'h', 0, 0)  7.59 us
    all_to_all x1, waiting for transfers between devices, on_device(): mine = lax.all_to_all(send, ('l', 'c', 'n', 'x'), 0, 0)  6.48 us
  transfers between devices with their start and end apart: 6, of which 4 were waited for; matrix products, arithmetic and copies ran while one was open for 0% of the time, Pallas kernels for 2%

profile of v10, /device:TPU:1, one launch (start us, length us, event | category | flops | bytes accessed | tf_op | source)
XLA Modules:
  0.0 120.0 jit_solution(9614515738247176130)
XLA Ops:
  0.6 0.0 copy-start
  0.7 1.9 %shard_map.95 = bf16[32,8,512]{2,1,0:T(8,128)(2,1)} custom-call(bf16[8,7168]{1,0:T(8,128)(2,1)} %values_all.1, bf16[1,8]{1,0:T(2,128)(2,1)} %bitcast.21), custom_call_target="tpu_custom_call" | custom-call | bytes 376848 | tf_op jit(solution)/shard_map/pallas_call | solution.py:256
  2.6 10.5 %all-to-all-start = ((bf16[32,8,512]{2,1,0:T(8,128)(2,1)}), bf16[32,8,512]{2,1,0:T(8,128)(2,1)S(1)}, u32[]{:S(2)}, u32[]{:S(2)}) async-start(bf16[32,8,512]{2,1,0:T(8,128)(2,1)} %shard_map.95), calls=%async_computation | async-start | bytes 524288 | tf_op jit(solution)/shard_map/all_to_all | solution.py:283
  13.2 1.8 %shard_map.94 = bf16[16,256,128]{2,1,0:T(8,128)(2,1)} custom-call(s32[1]{0:T(128)} %bitcast.where_ref, s32[1,2]{1,0:T(1,128)S(1)} %copy-done.5, s32[2,128]{1,0:T(2,128)S(1)} %bitcast.20, f32[2,128]{1,0:T(2,128)S(1)} %bitcast.18, bf16[128,128]{1,0:T(8,128)(2,1)S(1)} %bitcast.16, bf16[32,7168]{1,0:T(8,128)(2,1)S(1)} %constant_dynamic-slice_fusion.w_ref), custom_call_target="tpu_custom_call" | custom-call | bytes 1542156 | tf_op jit(solution)/shard_map/pallas_call | solution.py:256
  14.9 6.5 %all-to-all-done = bf16[32,8,512]{2,1,0:T(8,128)(2,1)S(1)} async-done(((bf16[32,8,512]{2,1,0:T(8,128)(2,1)}), bf16[32,8,512]{2,1,0:T(8,128)(2,1)S(1)}, u32[]{:S(2)}, u32[]{:S(2)}) %all-to-all-start) | async-done | bytes 262176 | tf_op jit(solution)/shard_map/all_to_all | solution.py:283
  21.4 3.9 %all-to-all-start.1 = ((bf16[16,256,128]{2,1,0:T(8,128)(2,1)}), bf16[16,256,128]{2,1,0:T(8,128)(2,1)S(1)}, u32[]{:S(2)}, u32[]{:S(2)}) async-start(bf16[16,256,128]{2,1,0:T(8,128)(2,1)} %shard_map.94), calls=%async_computation.1 | async-start | bytes 2097152 | tf_op jit(solution)/shard_map/all_to_all | solution.py:293
  25.3 0.1 shard_map.96
  25.4 21.1 %all-gather = bf16[16,224,128]{2,1,0:T(8,128)(2,1)} all-gather(bf16[4,224,128]{2,1,0:T(8,128)(2,1)S(1)} %shard_map.96), channel_id=2, replica_groups=mesh['h'=4,'l'=2,'c'=2,'e'=2,'m'=2,'n'=2,'x'=4] {'e','m'}, dimensions={0}, use_global_device_ids=true | all-gather | bytes 1146880 | tf_op jit(solution)/shard_map/all_gather | solution.py:297
  46.5 1.2 copy-done.1
  47.7 2.4 %shard_map.97 = (bf16[4,4,112,128]{3,2,1,0:T(8,128)(2,1)}, bf16[8,144,128]{2,1,0:T(8,128)(2,1)S(1)}, bf16[8,144,128]{2,1,0:T(8,128)(2,1)S(1)}) custom-call(s32[1]{0:T(128)} %bitcast.2.core_ref, bf16[4,4,224,128]{3,2,1,0:T(8,128)(2,1)S(1)} %bitcast.15, bf16[16,256,128]{2,1,0:T(8,128)(2,1)S(1)} %all-to-all-done.1.pack_ref), custom_call_target="tpu_custom_call" | custom-call | flops 654311424 | bytes 3014660 | tf_op jit(solution)/shard_map/pallas_call | solution.py:256
  50.0 7.6 %all-to-all-start.2 = ((bf16[4,4,112,128]{3,2,1,0:T(8,128)(2,1)}), bf16[4,4,112,128]{3,2,1,0:T(8,128)(2,1)S(1)}, u32[]{:S(2)}, u32[]{:S(2)}) async-start(bf16[4,4,112,128]{3,2,1,0:T(8,128)(2,1)} %get-tuple-element.17), calls=%async_computation.2 | async-start | bytes 917504 | tf_op jit(solution)/shard_map/all_to_all | solution.py:308
  57.6 5.3 %collective-permute-start = (bf16[8,144,128]{2,1,0:T(8,128)(2,1)S(1)}, bf16[8,144,128]{2,1,0:T(8,128)(2,1)S(1)}, u32[]{:S(2)}, u32[]{:S(2)}) collective-permute-start(bf16[8,144,128]{2,1,0:T(8,128)(2,1)S(1)} %get-tuple-element.19), channel_id=1, source_target_pairs={{0,32},{32,0},{1,33},{33,1},{2,34},{34,2},{3,35},{35,3},{4,36},{36... | collective-permute-start | bytes 884744 | tf_op jit(solution)/shard_map/ppermute | solution.py:307
  62.9 1.2 collective-permute-done.other_ref
  64.1 3.8 %all-to-all-done.2.sums_ref = bf16[4,4,112,128]{3,2,1,0:T(8,128)(2,1)S(1)} async-done(((bf16[4,4,112,128]{3,2,1,0:T(8,128)(2,1)}), bf16[4,4,112,128]{3,2,1,0:T(8,128)(2,1)S(1)}, u32[]{:S(2)}, u32[]{:S(2)}) %all-to-all-start.2) | async-done | bytes 458784 | tf_op jit(solution)/shard_map/all_to_all | solution.py:308
  67.9 0.2 shard_map.98
  68.2 12.4 %all_to_all.32.got_ref = bf16[8,256,128]{2,1,0:T(8,128)(2,1)S(1)} all-to-all(bf16[8,256,128]{2,1,0:T(8,128)(2,1)S(1)} %shard_map.98), channel_id=1, replica_groups=mesh['h'=4,'l'=2,'c'=2,'e'=2,'m'=2,'n'=2,'x'=4] {'l','x'}, dimensions={0} | all-to-all | bytes 1048576 | tf_op jit(solution)/shard_map/all_to_all | solution.py:316
  80.5 0.8 shard_map.99
  81.4 9.5 %all-to-all-start.4 = ((f32[8,1,8]{2,1,0:T(1,128)}), f32[8,1,8]{2,1,0:T(1,128)S(1)}, u32[]{:S(2)}, u32[]{:S(2)}) async-start(f32[8,1,8]{2,1,0:T(1,128)} %bitcast.10), calls=%async_computation.4 | async-start | bytes 8192 | tf_op jit(solution)/shard_map/all_to_all | solution.py:323
  90.9 19.2 %all_gather.11.half_ref = bf16[128,3584]{1,0:T(8,128)(2,1)S(1)} all-gather(bf16[32,3584]{1,0:T(8,128)(2,1)S(1)} %get-tuple-element.21), channel_id=1, replica_groups=mesh['h'=4,'l'=2,'c'=2,'e'=2,'m'=2,'n'=2,'x'=4] {'h'}, dimensions={0}, use_global_device_ids=true | all-gather | bytes 1146880 | tf_op jit(solution)/shard_map/all_gather | solution.py:325
  110.1 0.0 all-to-all-done.4
  110.1 6.4 %collective-permute-start.1 = (bf16[128,3584]{1,0:T(8,128)(2,1)S(1)}, bf16[128,3584]{1,0:T(8,128)(2,1)S(1)}, u32[]{:S(2)}, u32[]{:S(2)}) collective-permute-start(bf16[128,3584]{1,0:T(8,128)(2,1)S(1)} %all_gather.11.half_ref), channel_id=1, source_target_pairs={{0,32},{32,0},{1,33},{33,1},{2,34},{34,2},{3,35},{35,3},{4,36},{36... | collective-permute-start | bytes 2752520 | tf_op jit(solution)/shard_map/ppermute | solution.py:327
  116.5 0.9 shard_map.100.out_in_ref
  117.4 1.1 collective-permute-done.1.half_ref
  118.5 1.5 %shard_map.101 = (bf16[128,7168]{1,0:T(8,128)(2,1)}, f32[2,8]{1,0:T(2,128)}) custom-call(s32[1]{0:T(128)} %bitcast.2.core_ref, bf16[128,3584]{1,0:T(8,128)(2,1)S(1)} %collective-permute-done.1.half_ref, f32[8,8]{1,0:T(8,128)S(1)} %bitcast.17, bf16[128,7168]{1,0:T(8,128)(2,1)} %shard_map.100.out_in_ref), custom_call_target="tpu_custom_call", output_to_operand_aliasing={{0}: (3, {})} | custom-call | bytes 4587844 | tf_op jit(solution)/shard_map/pallas_call | solution.py:256
  (12 shorter events, 0.1 us)
Async XLA Ops:
  0.6 12.5 %copy-start = (bf16[128,7168]{1,0:T(8,128)(2,1)S(1)}, bf16[128,7168]{1,0:T(8,128)(2,1)}, u32[]{:S(2)}) copy-start(bf16[128,7168]{1,0:T(8,128)(2,1)} %param.10) | copy-start | bytes 5505028
  0.6 12.5 %copy-start.3 = (f32[1,2,128]{2,1,0:T(2,128)S(1)}, f32[1,2,128]{2,1,0:T(2,128)}, u32[]{:S(2)}) copy-start(f32[1,2,128]{2,1,0:T(2,128)} %param.13) | copy-start | bytes 3076
  0.7 12.5 %copy-start.5 = (s32[1,2]{1,0:T(1,128)S(1)}, s32[1,2]{1,0:T(1,128)}, u32[]{:S(2)}) copy-start(s32[1,2]{1,0:T(1,128)} %count_ref.1) | copy-start | bytes 28
  0.7 12.5 %copy-start.4 = (s32[1,2,128]{2,1,0:T(2,128)S(1)}, s32[1,2,128]{2,1,0:T(2,128)}, u32[]{:S(2)}) copy-start(s32[1,2,128]{2,1,0:T(2,128)} %param.11) | copy-start | bytes 3076
  0.7 12.5 %copy-start.2 = (bf16[1,128,128]{2,1,0:T(8,128)(2,1)S(1)}, bf16[1,128,128]{2,1,0:T(8,128)(2,1)}, u32[]{:S(2)}) copy-start(bf16[1,128,128]{2,1,0:T(8,128)(2,1)} %param.9) | copy-start | bytes 98308
  2.6 18.8 %all-to-all-start = ((bf16[32,8,512]{2,1,0:T(8,128)(2,1)}), bf16[32,8,512]{2,1,0:T(8,128)(2,1)S(1)}, u32[]{:S(2)}, u32[]{:S(2)}) async-start(bf16[32,8,512]{2,1,0:T(8,128)(2,1)} %shard_map.95), calls=%async_computation | async-start | bytes 524288 | tf_op jit(solution)/shard_map/all_to_all | solution.py:283
  21.4 25.0 %all-to-all-start.1 = ((bf16[16,256,128]{2,1,0:T(8,128)(2,1)}), bf16[16,256,128]{2,1,0:T(8,128)(2,1)S(1)}, u32[]{:S(2)}, u32[]{:S(2)}) async-start(bf16[16,256,128]{2,1,0:T(8,128)(2,1)} %shard_map.94), calls=%async_computation.1 | async-start | bytes 2097152 | tf_op jit(solution)/shard_map/all_to_all | solution.py:293
  46.5 1.2 copy-start.1
  50.0 17.9 %all-to-all-start.2 = ((bf16[4,4,112,128]{3,2,1,0:T(8,128)(2,1)}), bf16[4,4,112,128]{3,2,1,0:T(8,128)(2,1)S(1)}, u32[]{:S(2)}, u32[]{:S(2)}) async-start(bf16[4,4,112,128]{3,2,1,0:T(8,128)(2,1)} %get-tuple-element.17), calls=%async_computation.2 | async-start | bytes 917504 | tf_op jit(solution)/shard_map/all_to_all | solution.py:308
  57.6 6.5 %collective-permute-start = (bf16[8,144,128]{2,1,0:T(8,128)(2,1)S(1)}, bf16[8,144,128]{2,1,0:T(8,128)(2,1)S(1)}, u32[]{:S(2)}, u32[]{:S(2)}) collective-permute-start(bf16[8,144,128]{2,1,0:T(8,128)(2,1)S(1)} %get-tuple-element.19), channel_id=1, source_target_pairs={{0,32},{32,0},{1,33},{33,1},{2,34},{34,2},{3,35},{35,3},{4,36},{36... | collective-permute-start | bytes 884744 | tf_op jit(solution)/shard_map/ppermute | solution.py:307
  81.4 28.7 %all-to-all-start.4 = ((f32[8,1,8]{2,1,0:T(1,128)}), f32[8,1,8]{2,1,0:T(1,128)S(1)}, u32[]{:S(2)}, u32[]{:S(2)}) async-start(f32[8,1,8]{2,1,0:T(1,128)} %bitcast.10), calls=%async_computation.4 | async-start | bytes 8192 | tf_op jit(solution)/shard_map/all_to_all | solution.py:323
  110.1 8.5 %collective-permute-start.1 = (bf16[128,3584]{1,0:T(8,128)(2,1)S(1)}, bf16[128,3584]{1,0:T(8,128)(2,1)S(1)}, u32[]{:S(2)}, u32[]{:S(2)}) collective-permute-start(bf16[128,3584]{1,0:T(8,128)(2,1)S(1)} %all_gather.11.half_ref), channel_id=1, source_target_pairs={{0,32},{32,0},{1,33},{33,1},{2,34},{34,2},{3,35},{35,3},{4,36},{36... | collective-permute-start | bytes 2752520 | tf_op jit(solution)/shard_map/ppermute | solution.py:327

commit v11 on v10

--- a/solution.py
+++ b/solution.py
@@ -57,15 +57,7 @@
     return jnp.concatenate([a, pltpu.roll(a, TAIL, 1)], axis=0)
 
 
-def tokens_kernel(values_all, scales_all, out_ref, values_ref, scales_ref, sem):
-    loads = [
-        pltpu.make_async_copy(src, dst, sem.at[i])
-        for i, (src, dst) in enumerate(((values_all, values_ref), (scales_all, scales_ref)))
-    ]
-    for load in loads:
-        load.start()
-    for load in loads:
-        load.wait()
+def tokens_kernel(values_ref, scales_ref, out_ref):
     scaled = values_ref[...].astype(F32) * column(scales_ref[...].astype(F32))
     for l in range(L):
         for n in range(C * X):
@@ -272,12 +264,9 @@
 
     (send,) = call(
         tokens_kernel,
-        [HBM, HBM],
+        [VM, VM],
         [((N * PARTS, ROWS, WIDE), BF)],
         grad_values, grad_scales.reshape(1, ROWS),
-        scratch=[
-            pltpu.VMEM((ROWS, WIDTH), BF), pltpu.VMEM((1, ROWS), BF), pltpu.SemaphoreType.DMA((2,))
-        ],
         vmem=60,
     )
     mine = lax.all_to_all(send, ("l", "c", "n", "x"), 0, 0)

time: 121 us -> 121 us (level)
  no operation moved by 1% of the time
where the time goes in v11:
time: 121 us; the launch traced here: 120 us
  blocking collectives  52.7 us (44%)
  starting transfers between devices  43.1 us (36%)
  waiting for transfers between devices  12.6 us (10%)
  Pallas kernels  9.59 us (8%)
  local copies, waits for them, and re-layouts  1.24 us (1%)
    all_gather x1, blocking collectives, on_device(): mine = lax.all_gather(mine, ('e', 'm'), axis=0)  21.1 us
    all_gather x1, blocking collectives, on_device(): block = lax.all_gather(block, 'h', axis=0, tiled=True)  19.2 us
    all_to_all x1, blocking collectives, on_device(): got = lax.all_to_all(send, ('l', 'x'), 0, 0)  12.4 us
    all_to_all x1, starting transfers between devices, on_device(): mine = lax.all_to_all(send, ('l', 'c', 'n', 'x'), 0, 0)  10.4 us
    pallas_call x8, Pallas kernels, call(): pl.pallas_call(kernel, out_shape=outs, in_specs=places, out_specs=out_pla...  9.59 us
    all_to_all x1, starting transfers between devices, on_device(): spread = lax.all_to_all(spread, ('e', 'm', 'n'), 0, 0, tiled=True)  9.5 us
    all_to_all x1, starting transfers between devices, on_device(): sums = lax.all_to_all(part, 'h', 0, 0)  7.59 us
    all_to_all x1, waiting for transfers between devices, on_device(): mine = lax.all_to_all(send, ('l', 'c', 'n', 'x'), 0, 0)  6.48 us
  transfers between devices with their start and end apart: 6, of which 4 were waited for; matrix products, arithmetic and copies ran while one was open for 0% of the time, Pallas kernels for 2%

profile of v11, /device:TPU:1, one launch (start us, length us, event | category | flops | bytes accessed | tf_op | source)
XLA Modules:
  0.0 120.0 jit_solution(16993063181549944646)
XLA Ops:
  0.6 0.0 copy-start
  0.7 1.9 %shard_map.95 = bf16[32,8,512]{2,1,0:T(8,128)(2,1)} custom-call(bf16[8,7168]{1,0:T(8,128)(2,1)} %values_ref.1, bf16[1,8]{1,0:T(2,128)(2,1)} %bitcast.21), custom_call_target="tpu_custom_call" | custom-call | bytes 376848 | tf_op jit(solution)/shard_map/pallas_call | solution.py:248
  2.6 10.4 %all-to-all-start = ((bf16[32,8,512]{2,1,0:T(8,128)(2,1)}), bf16[32,8,512]{2,1,0:T(8,128)(2,1)S(1)}, u32[]{:S(2)}, u32[]{:S(2)}) async-start(bf16[32,8,512]{2,1,0:T(8,128)(2,1)} %shard_map.95), calls=%async_computation | async-start | bytes 524288 | tf_op jit(solution)/shard_map/all_to_all | solution.py:272
  13.2 1.8 %shard_map.94 = bf16[16,256,128]{2,1,0:T(8,128)(2,1)} custom-call(s32[1]{0:T(128)} %bitcast.where_ref, s32[1,2]{1,0:T(1,128)S(1)} %copy-done.5, s32[2,128]{1,0:T(2,128)S(1)} %bitcast.20, f32[2,128]{1,0:T(2,128)S(1)} %bitcast.18, bf16[128,128]{1,0:T(8,128)(2,1)S(1)} %bitcast.16, bf16[32,7168]{1,0:T(8,128)(2,1)S(1)} %constant_dynamic-slice_fusion.w_ref), custom_call_target="tpu_custom_call" | custom-call | bytes 1542156 | tf_op jit(solution)/shard_map/pallas_call | solution.py:248
  14.9 6.5 %all-to-all-done = bf16[32,8,512]{2,1,0:T(8,128)(2,1)S(1)} async-done(((bf16[32,8,512]{2,1,0:T(8,128)(2,1)}), bf16[32,8,512]{2,1,0:T(8,128)(2,1)S(1)}, u32[]{:S(2)}, u32[]{:S(2)}) %all-to-all-start) | async-done | bytes 262176 | tf_op jit(solution)/shard_map/all_to_all | solution.py:272
  21.4 3.9 %all-to-all-start.1 = ((bf16[16,256,128]{2,1,0:T(8,128)(2,1)}), bf16[16,256,128]{2,1,0:T(8,128)(2,1)S(1)}, u32[]{:S(2)}, u32[]{:S(2)}) async-start(bf16[16,256,128]{2,1,0:T(8,128)(2,1)} %shard_map.94), calls=%async_computation.1 | async-start | bytes 2097152 | tf_op jit(solution)/shard_map/all_to_all | solution.py:282
  25.3 0.1 shard_map.96
  25.3 21.1 %all-gather = bf16[16,224,128]{2,1,0:T(8,128)(2,1)} all-gather(bf16[4,224,128]{2,1,0:T(8,128)(2,1)S(1)} %shard_map.96), channel_id=2, replica_groups=mesh['h'=4,'l'=2,'c'=2,'e'=2,'m'=2,'n'=2,'x'=4] {'e','m'}, dimensions={0}, use_global_device_ids=true | all-gather | bytes 1146880 | tf_op jit(solution)/shard_map/all_gather | solution.py:286
  46.4 0.0 all-to-all-done.1.pack_ref
  46.4 1.2 copy-done.1
  47.6 2.4 %shard_map.97 = (bf16[4,4,112,128]{3,2,1,0:T(8,128)(2,1)}, bf16[8,144,128]{2,1,0:T(8,128)(2,1)S(1)}, bf16[8,144,128]{2,1,0:T(8,128)(2,1)S(1)}) custom-call(s32[1]{0:T(128)} %bitcast.2.core_ref, bf16[4,4,224,128]{3,2,1,0:T(8,128)(2,1)S(1)} %bitcast.15, bf16[16,256,128]{2,1,0:T(8,128)(2,1)S(1)} %all-to-all-done.1.pack_ref), custom_call_target="tpu_custom_call" | custom-call | flops 654311424 | bytes 3014660 | tf_op jit(solution)/shard_map/pallas_call | solution.py:248
  50.0 7.6 %all-to-all-start.2 = ((bf16[4,4,112,128]{3,2,1,0:T(8,128)(2,1)}), bf16[4,4,112,128]{3,2,1,0:T(8,128)(2,1)S(1)}, u32[]{:S(2)}, u32[]{:S(2)}) async-start(bf16[4,4,112,128]{3,2,1,0:T(8,128)(2,1)} %get-tuple-element.17), calls=%async_computation.2 | async-start | bytes 917504 | tf_op jit(solution)/shard_map/all_to_all | solution.py:297
  57.6 5.3 %collective-permute-start = (bf16[8,144,128]{2,1,0:T(8,128)(2,1)S(1)}, bf16[8,144,128]{2,1,0:T(8,128)(2,1)S(1)}, u32[]{:S(2)}, u32[]{:S(2)}) collective-permute-start(bf16[8,144,128]{2,1,0:T(8,128)(2,1)S(1)} %get-tuple-element.19), channel_id=1, source_target_pairs={{0,32},{32,0},{1,33},{33,1},{2,34},{34,2},{3,35},{35,3},{4,36},{36... | collective-permute-start | bytes 884744 | tf_op jit(solution)/shard_map/ppermute | solution.py:296
  62.9 1.2 collective-permute-done.other_ref
  64.1 3.8 %all-to-all-done.2.sums_ref = bf16[4,4,112,128]{3,2,1,0:T(8,128)(2,1)S(1)} async-done(((bf16[4,4,112,128]{3,2,1,0:T(8,128)(2,1)}), bf16[4,4,112,128]{3,2,1,0:T(8,128)(2,1)S(1)}, u32[]{:S(2)}, u32[]{:S(2)}) %all-to-all-start.2) | async-done | bytes 458784 | tf_op jit(solution)/shard_map/all_to_all | solution.py:297
  67.9 0.2 shard_map.98
  68.1 12.4 %all_to_all.32.got_ref = bf16[8,256,128]{2,1,0:T(8,128)(2,1)S(1)} all-to-all(bf16[8,256,128]{2,1,0:T(8,128)(2,1)S(1)} %shard_map.98), channel_id=1, replica_groups=mesh['h'=4,'l'=2,'c'=2,'e'=2,'m'=2,'n'=2,'x'=4] {'l','x'}, dimensions={0} | all-to-all | bytes 1048576 | tf_op jit(solution)/shard_map/all_to_all | solution.py:305
  80.5 0.8 shard_map.99
  81.3 9.5 %all-to-all-start.4 = ((f32[8,1,8]{2,1,0:T(1,128)}), f32[8,1,8]{2,1,0:T(1,128)S(1)}, u32[]{:S(2)}, u32[]{:S(2)}) async-start(f32[8,1,8]{2,1,0:T(1,128)} %bitcast.10), calls=%async_computation.4 | async-start | bytes 8192 | tf_op jit(solution)/shard_map/all_to_all | solution.py:312
  90.8 19.2 %all_gather.11.half_ref = bf16[128,3584]{1,0:T(8,128)(2,1)S(1)} all-gather(bf16[32,3584]{1,0:T(8,128)(2,1)S(1)} %get-tuple-element.21), channel_id=1, replica_groups=mesh['h'=4,'l'=2,'c'=2,'e'=2,'m'=2,'n'=2,'x'=4] {'h'}, dimensions={0}, use_global_device_ids=true | all-gather | bytes 1146880 | tf_op jit(solution)/shard_map/all_gather | solution.py:314
  110.0 6.4 %collective-permute-start.1 = (bf16[128,3584]{1,0:T(8,128)(2,1)S(1)}, bf16[128,3584]{1,0:T(8,128)(2,1)S(1)}, u32[]{:S(2)}, u32[]{:S(2)}) collective-permute-start(bf16[128,3584]{1,0:T(8,128)(2,1)S(1)} %all_gather.11.half_ref), channel_id=1, source_target_pairs={{0,32},{32,0},{1,33},{33,1},{2,34},{34,2},{3,35},{35,3},{4,36},{36... | collective-permute-start | bytes 2752520 | tf_op jit(solution)/shard_map/ppermute | solution.py:316
  116.4 0.9 shard_map.100.out_in_ref
  117.4 1.1 collective-permute-done.1.half_ref
  118.5 1.5 %shard_map.101 = (bf16[128,7168]{1,0:T(8,128)(2,1)}, f32[2,8]{1,0:T(2,128)}) custom-call(s32[1]{0:T(128)} %bitcast.2.core_ref, bf16[128,3584]{1,0:T(8,128)(2,1)S(1)} %collective-permute-done.1.half_ref, f32[8,8]{1,0:T(8,128)S(1)} %bitcast.17, bf16[128,7168]{1,0:T(8,128)(2,1)} %shard_map.100.out_in_ref), custom_call_target="tpu_custom_call", output_to_operand_aliasing={{0}: (3, {})} | custom-call | bytes 4587844 | tf_op jit(solution)/shard_map/pallas_call | solution.py:248
  (12 shorter events, 0.1 us)
Async XLA Ops:
  0.6 12.4 %copy-start = (bf16[128,7168]{1,0:T(8,128)(2,1)S(1)}, bf16[128,7168]{1,0:T(8,128)(2,1)}, u32[]{:S(2)}) copy-start(bf16[128,7168]{1,0:T(8,128)(2,1)} %param.10) | copy-start | bytes 5505028
  0.6 12.5 %copy-start.3 = (f32[1,2,128]{2,1,0:T(2,128)S(1)}, f32[1,2,128]{2,1,0:T(2,128)}, u32[]{:S(2)}) copy-start(f32[1,2,128]{2,1,0:T(2,128)} %param.13) | copy-start | bytes 3076
  0.7 12.5 %copy-start.5 = (s32[1,2]{1,0:T(1,128)S(1)}, s32[1,2]{1,0:T(1,128)}, u32[]{:S(2)}) copy-start(s32[1,2]{1,0:T(1,128)} %count_ref.1) | copy-start | bytes 28
  0.7 12.5 %copy-start.4 = (s32[1,2,128]{2,1,0:T(2,128)S(1)}, s32[1,2,128]{2,1,0:T(2,128)}, u32[]{:S(2)}) copy-start(s32[1,2,128]{2,1,0:T(2,128)} %param.11) | copy-start | bytes 3076
  0.7 12.5 %copy-start.2 = (bf16[1,128,128]{2,1,0:T(8,128)(2,1)S(1)}, bf16[1,128,128]{2,1,0:T(8,128)(2,1)}, u32[]{:S(2)}) copy-start(bf16[1,128,128]{2,1,0:T(8,128)(2,1)} %param.9) | copy-start | bytes 98308
  2.6 18.8 %all-to-all-start = ((bf16[32,8,512]{2,1,0:T(8,128)(2,1)}), bf16[32,8,512]{2,1,0:T(8,128)(2,1)S(1)}, u32[]{:S(2)}, u32[]{:S(2)}) async-start(bf16[32,8,512]{2,1,0:T(8,128)(2,1)} %shard_map.95), calls=%async_computation | async-start | bytes 524288 | tf_op jit(solution)/shard_map/all_to_all | solution.py:272
  21.4 25.0 %all-to-all-start.1 = ((bf16[16,256,128]{2,1,0:T(8,128)(2,1)}), bf16[16,256,128]{2,1,0:T(8,128)(2,1)S(1)}, u32[]{:S(2)}, u32[]{:S(2)}) async-start(bf16[16,256,128]{2,1,0:T(8,128)(2,1)} %shard_map.94), calls=%async_computation.1 | async-start | bytes 2097152 | tf_op jit(solution)/shard_map/all_to_all | solution.py:282
  46.4 1.2 copy-start.1
  50.0 17.9 %all-to-all-start.2 = ((bf16[4,4,112,128]{3,2,1,0:T(8,128)(2,1)}), bf16[4,4,112,128]{3,2,1,0:T(8,128)(2,1)S(1)}, u32[]{:S(2)}, u32[]{:S(2)}) async-start(bf16[4,4,112,128]{3,2,1,0:T(8,128)(2,1)} %get-tuple-element.17), calls=%async_computation.2 | async-start | bytes 917504 | tf_op jit(solution)/shard_map/all_to_all | solution.py:297
  57.6 6.5 %collective-permute-start = (bf16[8,144,128]{2,1,0:T(8,128)(2,1)S(1)}, bf16[8,144,128]{2,1,0:T(8,128)(2,1)S(1)}, u32[]{:S(2)}, u32[]{:S(2)}) collective-permute-start(bf16[8,144,128]{2,1,0:T(8,128)(2,1)S(1)} %get-tuple-element.19), channel_id=1, source_target_pairs={{0,32},{32,0},{1,33},{33,1},{2,34},{34,2},{3,35},{35,3},{4,36},{36... | collective-permute-start | bytes 884744 | tf_op jit(solution)/shard_map/ppermute | solution.py:296
  81.3 28.7 %all-to-all-start.4 = ((f32[8,1,8]{2,1,0:T(1,128)}), f32[8,1,8]{2,1,0:T(1,128)S(1)}, u32[]{:S(2)}, u32[]{:S(2)}) async-start(f32[8,1,8]{2,1,0:T(1,128)} %bitcast.10), calls=%async_computation.4 | async-start | bytes 8192 | tf_op jit(solution)/shard_map/all_to_all | solution.py:312
  110.0 8.5 %collective-permute-start.1 = (bf16[128,3584]{1,0:T(8,128)(2,1)S(1)}, bf16[128,3584]{1,0:T(8,128)(2,1)S(1)}, u32[]{:S(2)}, u32[]{:S(2)}) collective-permute-start(bf16[128,3584]{1,0:T(8,128)(2,1)S(1)} %all_gather.11.half_ref), channel_id=1, source_target_pairs={{0,32},{32,0},{1,33},{33,1},{2,34},{34,2},{3,35},{35,3},{4,36},{36... | collective-permute-start | bytes 2752520 | tf_op jit(solution)/shard_map/ppermute | solution.py:316

commit v12 on v11

--- a/solution.py
+++ b/solution.py
@@ -8,14 +8,13 @@
 BF, F32, I32 = jnp.bfloat16, jnp.float32, jnp.int32
 DP, EXPERT = ("h", "l", "c"), ("e", "m", "n", "x")
 H, L, C, E, M, N, X = SIZES = (4, 2, 2, 2, 2, 2, 4)
-SPLIT = ("l", "c", "x")
 QUARTERS, PARTS = L * C, L * C * X
 LANES, TILES = 128, 4
 WIDTH, SLOTS, UNITS, ROWS = 7168, 128, 128, 8
 GROUP = E * M * N * X * ROWS
 COLS, WIDE = WIDTH // PARTS, TILES * LANES
 PAIR = 2 * COLS
-SHARE = UNITS // QUARTERS
+SHARE = UNITS // L
 CHUNK = UNITS // H
 EXTRA = 16
 PACK = SLOTS + EXTRA
@@ -91,17 +90,19 @@
     return out.astype(BF)
 
 
-def pack_kernel(where_ref, count_ref, tok_ref, gate_ref, hidden_ref, w_ref, out_ref):
+def pack_kernel(where_ref, count_ref, tok_ref, gate_ref, hidden_ref, out_ref):
     gate = jnp.where(where_ref[0] == 0, gate_ref[0:1, :], gate_ref[1:2, :])
     tok = own_slots(where_ref, tok_ref, count_ref).astype(F32)
-    extra = stack_rows((tok,) + split3(gate))
+    out_ref[0:SLOTS, :] = hidden_ref[...]
+    out_ref[SLOTS:PACK, :] = stack_rows((tok,) + split3(gate))
+
+
+def send_kernel(packs_ref, w_ref, out_ref):
     w = w_ref[...].astype(F32)
     for l in range(L):
-        for n in range(C * X):
-            at = l * C * X + n
-            out_ref[at, 0:SLOTS, :] = hidden_ref[...]
-            out_ref[at, SLOTS:PACK, :] = extra
-            out_ref[at, PACK:, :] = dense(slice_of(w, n, l)).astype(BF)
+        for x in range(X):
+            out_ref[l * X + x, 0 : C * PACK, :] = packs_ref[...]
+            out_ref[l * X + x, C * PACK :, :] = dense(slice_of(w, x, l)).astype(BF)
 
 
 def dense_kernel(rows_ref, out_ref):
@@ -114,7 +115,7 @@
     first = (((0,), (0,)), ((), ()))
     gates = []
     for g in range(QUARTERS):
-        extra = pack_ref[g * X, SLOTS:PACK, :].astype(F32)
+        extra = pack_ref[g // C * X, g % C * PACK + SLOTS : (g % C + 1) * PACK, :].astype(F32)
         gates.append(column(extra[1:2] + extra[2:3] + extra[3:4]))
         picks = jnp.where(ids == extra[0:1].astype(I32), 1.0, 0.0).astype(BF)
         rows = [mine_ref[:, g, t * TOKS : (t + 1) * TOKS, :].reshape(GROUP, LANES) for t in range(FULL)]
@@ -132,7 +133,8 @@
 
     for x in range(X):
         weighted = [
-            (gates[g] * pack_ref[g * X + x, :SLOTS, :].astype(F32)).astype(BF) for g in range(QUARTERS)
+            (gates[g] * pack_ref[g // C * X + x, pl.ds(g % C * PACK, SLOTS), :].astype(F32)).astype(BF)
+            for g in range(QUARTERS)
         ]
         weighted = jnp.concatenate(weighted, axis=0)
         part = lax.dot_general(weighted, routed, first, preferred_element_type=F32)
@@ -140,16 +142,16 @@
             part_ref[h, x] = dense(part[h * CHUNK : (h + 1) * CHUNK]).astype(BF)
 
     core = core_ref[0]
-    groups = [l * C + c for c in (core, 1 - core) for l in range(L)]
+    groups = [(l, c) for c in (core, 1 - core) for l in range(L)]
     outs = [(ref, l) for ref in (keep_ref, send_ref) for l in range(L)]
     routed = jnp.concatenate(
-        [routed_ref[pl.ds(pl.multiple_of(g * SLOTS, SLOTS), SLOTS), :] for g in groups], axis=0
+        [routed_ref[pl.ds(pl.multiple_of((l * C + c) * SLOTS, SLOTS), SLOTS), :] for l, c in groups], axis=0
     )
     sums = [jnp.zeros((SLOTS, 1), F32)] * QUARTERS
     for x in range(X):
         w = []
-        for q in range(QUARTERS):
-            rows = pack_ref[q * X + x, PACK:, :]
+        for l in range(L):
+            rows = pack_ref[l * X + x, C * PACK :, :]
             rows = [rows[t * SHARE : (t + 1) * SHARE] for t in range(FULL)] + [
                 last_tile(rows[FULL * SHARE :].astype(F32)).astype(BF)
             ]
@@ -159,11 +161,13 @@
         for i, (ref, l) in enumerate(outs):
             rows = proj[i * SLOTS : (i + 1) * SLOTS]
             ref[l * X + x, 0:SLOTS, :] = rows.astype(BF)
-            hidden = pack_ref[groups[i] * X + x, :SLOTS, :].astype(F32)
+            at = pl.multiple_of(groups[i][1] * PACK, EXTRA)
+            hidden = pack_ref[l * X + x, pl.ds(at, SLOTS), :].astype(F32)
             sums[i] = sums[i] + jnp.sum(hidden * rows, axis=1, keepdims=True)
     at = lanes((SLOTS, LANES))
     for i, (ref, l) in enumerate(outs):
-        tok = column(pack_ref[groups[i] * X, SLOTS:PACK, :].astype(F32)[0:1]).astype(I32)
+        row = pl.multiple_of(groups[i][1] * PACK + SLOTS, EXTRA)
+        tok = column(pack_ref[l * X, pl.ds(row, EXTRA), :].astype(F32)[0:1]).astype(I32)
         device, spot = tok // ROWS, tok % ROWS
         spot = jnp.where(tok < GROUP, device // X * ROWS + spot, LANES)
         for x in range(X):
@@ -271,15 +275,18 @@
     )
     mine = lax.all_to_all(send, ("l", "c", "n", "x"), 0, 0)
 
-    w_rows = lax.dynamic_slice_in_dim(down_weight, (low * C + core) * SHARE, SHARE, 0)
     (pack,) = call(
         pack_kernel,
-        [SM, SM, VM, VM, VM, VM],
-        [((PARTS, PACK + W_PART, LANES), BF)],
-        where, slot_count, tok, gate, hidden, w_rows,
-    )
+        [SM, SM, VM, VM, VM],
+        [((PACK, LANES), BF)],
+        where, slot_count, tok, gate, hidden,
+    )
+    packs = lax.all_gather(pack, "c", axis=0, tiled=True)
+    width = X * PAIR
+    w_part = lax.dynamic_slice(down_weight, (low * SHARE, core * width), (SHARE, width))
+    (pack,) = call(send_kernel, [VM, VM], [((L * X, C * PACK + W_PART, LANES), BF)], packs, w_part)
     pack, mine = lax.optimization_barrier((pack, mine))
-    pack = lax.all_to_all(pack, SPLIT, 0, 0)
+    pack = lax.all_to_all(pack, ("l", "x"), 0, 0)
     (mine,) = call(
         dense_kernel, [VM], [((QUARTERS, DENSE, LANES), BF)], mine.reshape(QUARTERS, TOKS, WIDE)
     )

time: 121 us -> 116 us (0.959)
  waiting for transfers between devices: 12.6 us -> 9.7 us
    all_to_all x1, waiting for transfers between devices: 6.48 us -> 3.6 us  [on_device(): mine = lax.all_to_all(send, ('l', 'c', 'n', 'x'), 0, 0)]
    all_to_all x1, starting transfers between devices: 9.5 us -> 7.07 us  [on_device(): spread = lax.all_to_all(spread, ('e', 'm', 'n'), 0, 0, tiled=True)]
    all_gather x1, blocking collectives: 21.1 us -> 19.1 us  [on_device(): mine = lax.all_gather(mine, ('e', 'm'), axis=0)]
    all_gather x0 -> x1, blocking collectives: none -> 1.86 us  [on_device(): packs = lax.all_gather(pack, 'c', axis=0, tiled=True)]
    pallas_call x8 -> x9, Pallas kernels: 9.59 us -> 9.5 us  [call(): pl.pallas_call(kernel, out_shape=outs, in_specs=places, out_specs=out_pla...]
  transfers between devices with their start and end apart: 6 -> 6, of which waited for: 4 -> 4; matrix products, arithmetic and copies ran while one was open for 0% -> 1% of each run, Pallas kernels for 2% -> 2%
where the time goes in v12:
time: 116 us; the launch traced here: 115 us
  blocking collectives  51.7 us (45%)
  starting transfers between devices  42.3 us (36%)
  waiting for transfers between devices  9.7 us (8%)
  Pallas kernels  9.5 us (8%)
    all_gather x1, blocking collectives, on_device(): mine = lax.all_gather(mine, ('e', 'm'), axis=0)  19.1 us
    all_gather x1, blocking collectives, on_device(): block = lax.all_gather(block, 'h', axis=0, tiled=True)  18.4 us
    all_to_all x1, blocking collectives, on_device(): got = lax.all_to_all(send, ('l', 'x'), 0, 0)  12.3 us
    all_to_all x1, starting transfers between devices, on_device(): mine = lax.all_to_all(send, ('l', 'c', 'n', 'x'), 0, 0)  10.4 us
    pallas_call x9, Pallas kernels, call(): pl.pallas_call(kernel, out_shape=outs, in_specs=places, out_specs=out_pla...  9.5 us
    all_to_all x1, starting transfers between devices, on_device(): sums = lax.all_to_all(part, 'h', 0, 0)  8.74 us
    ppermute x1, starting transfers between devices, on_device(): other = lax.ppermute(block, 'c', [(i, C - 1 - i) for i in range(C)])  7.12 us
    all_to_all x1, starting transfers between devices, on_device(): spread = lax.all_to_all(spread, ('e', 'm', 'n'), 0, 0, tiled=True)  7.07 us
  transfers between devices with their start and end apart: 6, of which 4 were waited for; matrix products, arithmetic and copies ran while one was open for 1% of the time, Pallas kernels for 2%

profile of v12, /device:TPU:1, one launch (start us, length us, event | category | flops | bytes accessed | tf_op | source)
XLA Modules:
  0.0 115.0 jit_solution(8032644754876336617)
XLA Ops:
  0.7 1.8 %shard_map.96 = bf16[32,8,512]{2,1,0:T(8,128)(2,1)} custom-call(bf16[8,7168]{1,0:T(8,128)(2,1)} %values_ref.1, bf16[1,8]{1,0:T(2,128)(2,1)} %bitcast.21), custom_call_target="tpu_custom_call" | custom-call | bytes 376848 | tf_op jit(solution)/shard_map/pallas_call | solution.py:252
  2.5 10.4 %all-to-all-start = ((bf16[32,8,512]{2,1,0:T(8,128)(2,1)}), bf16[32,8,512]{2,1,0:T(8,128)(2,1)S(1)}, u32[]{:S(2)}, u32[]{:S(2)}) async-start(bf16[32,8,512]{2,1,0:T(8,128)(2,1)} %shard_map.96), calls=%async_computation | async-start | bytes 524288 | tf_op jit(solution)/shard_map/all_to_all | solution.py:276
  12.9 1.1 dynamic_slice.3.w_ref
  14.0 0.6 shard_map.94
  14.6 1.9 %all_gather.12.packs_ref = bf16[288,128]{1,0:T(8,128)(2,1)S(1)} all-gather(bf16[144,128]{1,0:T(8,128)(2,1)S(1)} %shard_map.94), channel_id=1, replica_groups=mesh['h'=4,'l'=2,'c'=2,'e'=2,'m'=2,'n'=2,'x'=4] {'c'}, dimensions={0}, use_global_device_ids=true | all-gather | bytes 110592 | tf_op jit(solution)/shard_map/all_gather | solution.py:284
  16.4 1.2 %shard_map.95 = bf16[8,512,128]{2,1,0:T(8,128)(2,1)} custom-call(bf16[288,128]{1,0:T(8,128)(2,1)S(1)} %all_gather.12.packs_ref, bf16[64,3584]{1,0:T(8,128)(2,1)S(1)} %dynamic_slice.3.w_ref), custom_call_target="tpu_custom_call" | custom-call | bytes 1581056 | tf_op jit(solution)/shard_map/pallas_call | solution.py:252
  17.7 3.6 %all-to-all-done = bf16[32,8,512]{2,1,0:T(8,128)(2,1)S(1)} async-done(((bf16[32,8,512]{2,1,0:T(8,128)(2,1)}), bf16[32,8,512]{2,1,0:T(8,128)(2,1)S(1)}, u32[]{:S(2)}, u32[]{:S(2)}) %all-to-all-start) | async-done | bytes 262176 | tf_op jit(solution)/shard_map/all_to_all | solution.py:276
  21.3 3.6 %all-to-all-start.1 = ((bf16[8,512,128]{2,1,0:T(8,128)(2,1)}), bf16[8,512,128]{2,1,0:T(8,128)(2,1)S(1)}, u32[]{:S(2)}, u32[]{:S(2)}) async-start(bf16[8,512,128]{2,1,0:T(8,128)(2,1)} %shard_map.95), calls=%async_computation.1 | async-start | bytes 2097152 | tf_op jit(solution)/shard_map/all_to_all | solution.py:289
  24.8 0.1 shard_map.97
  24.9 19.1 %all-gather = bf16[16,224,128]{2,1,0:T(8,128)(2,1)S(1)} all-gather(bf16[4,224,128]{2,1,0:T(8,128)(2,1)S(1)} %shard_map.97), channel_id=2, replica_groups=mesh['h'=4,'l'=2,'c'=2,'e'=2,'m'=2,'n'=2,'x'=4] {'e','m'}, dimensions={0}, use_global_device_ids=true | all-gather | bytes 1146880 | tf_op jit(solution)/shard_map/all_gather | solution.py:293
  44.0 2.4 %shard_map.98 = (bf16[4,4,112,128]{3,2,1,0:T(8,128)(2,1)}, bf16[8,144,128]{2,1,0:T(8,128)(2,1)S(1)}, bf16[8,144,128]{2,1,0:T(8,128)(2,1)S(1)}) custom-call(s32[1]{0:T(128)} %bitcast.2.core_ref, bf16[4,4,224,128]{3,2,1,0:T(8,128)(2,1)S(1)} %bitcast.15, bf16[8,512,128]{2,1,0:T(8,128)(2,1)S(1)} %all-to-all-done.1.pack_ref), custom_call_target="tpu_custom_call" | custom-call | flops 654311424 | bytes 3014660 | tf_op jit(solution)/shard_map/pallas_call | solution.py:252
  46.4 8.7 %all-to-all-start.2 = ((bf16[4,4,112,128]{3,2,1,0:T(8,128)(2,1)}), bf16[4,4,112,128]{3,2,1,0:T(8,128)(2,1)S(1)}, u32[]{:S(2)}, u32[]{:S(2)}) async-start(bf16[4,4,112,128]{3,2,1,0:T(8,128)(2,1)} %get-tuple-element.17), calls=%async_computation.2 | async-start | bytes 917504 | tf_op jit(solution)/shard_map/all_to_all | solution.py:304
  55.1 5.3 %collective-permute-start = (bf16[8,144,128]{2,1,0:T(8,128)(2,1)S(1)}, bf16[8,144,128]{2,1,0:T(8,128)(2,1)S(1)}, u32[]{:S(2)}, u32[]{:S(2)}) collective-permute-start(bf16[8,144,128]{2,1,0:T(8,128)(2,1)S(1)} %get-tuple-element.19), channel_id=1, source_target_pairs={{0,32},{32,0},{1,33},{33,1},{2,34},{34,2},{3,35},{35,3},{4,36},{36... | collective-permute-start | bytes 884744 | tf_op jit(solution)/shard_map/ppermute | solution.py:303
  60.5 1.2 %collective-permute-done.other_ref = bf16[8,144,128]{2,1,0:T(8,128)(2,1)S(1)} collective-permute-done((bf16[8,144,128]{2,1,0:T(8,128)(2,1)S(1)}, bf16[8,144,128]{2,1,0:T(8,128)(2,1)S(1)}, u32[]{:S(2)}, u32[]{:S(2)}) %collective-permute-start) | collective-permute-done | bytes 294944 | tf_op jit(solution)/shard_map/ppermute | solution.py:303
  61.7 3.8 %all-to-all-done.2.sums_ref = bf16[4,4,112,128]{3,2,1,0:T(8,128)(2,1)S(1)} async-done(((bf16[4,4,112,128]{3,2,1,0:T(8,128)(2,1)}), bf16[4,4,112,128]{3,2,1,0:T(8,128)(2,1)S(1)}, u32[]{:S(2)}, u32[]{:S(2)}) %all-to-all-start.2) | async-done | bytes 458784 | tf_op jit(solution)/shard_map/all_to_all | solution.py:304
  65.5 0.2 shard_map.99
  65.7 12.3 %all_to_all.32.got_ref = bf16[8,256,128]{2,1,0:T(8,128)(2,1)S(1)} all-to-all(bf16[8,256,128]{2,1,0:T(8,128)(2,1)S(1)} %shard_map.99), channel_id=1, replica_groups=mesh['h'=4,'l'=2,'c'=2,'e'=2,'m'=2,'n'=2,'x'=4] {'l','x'}, dimensions={0} | all-to-all | bytes 1048576 | tf_op jit(solution)/shard_map/all_to_all | solution.py:312
  78.0 0.8 shard_map.100
  78.8 7.1 %all-to-all-start.4 = ((f32[8,1,8]{2,1,0:T(1,128)}), f32[8,1,8]{2,1,0:T(1,128)S(1)}, u32[]{:S(2)}, u32[]{:S(2)}) async-start(f32[8,1,8]{2,1,0:T(1,128)} %bitcast.10), calls=%async_computation.4 | async-start | bytes 8192 | tf_op jit(solution)/shard_map/all_to_all | solution.py:319
  85.9 18.4 %all_gather.15.half_ref = bf16[128,3584]{1,0:T(8,128)(2,1)S(1)} all-gather(bf16[32,3584]{1,0:T(8,128)(2,1)S(1)} %get-tuple-element.21), channel_id=1, replica_groups=mesh['h'=4,'l'=2,'c'=2,'e'=2,'m'=2,'n'=2,'x'=4] {'h'}, dimensions={0}, use_global_device_ids=true | all-gather | bytes 1146880 | tf_op jit(solution)/shard_map/all_gather | solution.py:321
  104.3 7.1 %collective-permute-start.1 = (bf16[128,3584]{1,0:T(8,128)(2,1)S(1)}, bf16[128,3584]{1,0:T(8,128)(2,1)S(1)}, u32[]{:S(2)}, u32[]{:S(2)}) collective-permute-start(bf16[128,3584]{1,0:T(8,128)(2,1)S(1)} %all_gather.15.half_ref), channel_id=1, source_target_pairs={{0,32},{32,0},{1,33},{33,1},{2,34},{34,2},{3,35},{35,3},{4,36},{36... | collective-permute-start | bytes 2752520 | tf_op jit(solution)/shard_map/ppermute | solution.py:323
  111.4 0.9 shard_map.101.out_in_ref
  112.4 1.1 collective-permute-done.1.half_ref
  113.5 1.5 %shard_map.102 = (bf16[128,7168]{1,0:T(8,128)(2,1)}, f32[2,8]{1,0:T(2,128)}) custom-call(s32[1]{0:T(128)} %bitcast.2.core_ref, bf16[128,3584]{1,0:T(8,128)(2,1)S(1)} %collective-permute-done.1.half_ref, f32[8,8]{1,0:T(8,128)S(1)} %bitcast.17, bf16[128,7168]{1,0:T(8,128)(2,1)} %shard_map.101.out_in_ref), custom_call_target="tpu_custom_call", output_to_operand_aliasing={{0}: (3, {})} | custom-call | bytes 4587844 | tf_op jit(solution)/shard_map/pallas_call | solution.py:252
  (10 shorter events, 0.0 us)
Async XLA Ops:
  0.6 13.4 %copy-start.1 = (f32[1,2,128]{2,1,0:T(2,128)S(1)}, f32[1,2,128]{2,1,0:T(2,128)}, u32[]{:S(2)}) copy-start(f32[1,2,128]{2,1,0:T(2,128)} %param.13) | copy-start | bytes 3076
  0.6 13.4 %copy-start.3 = (s32[1,2]{1,0:T(1,128)S(1)}, s32[1,2]{1,0:T(1,128)}, u32[]{:S(2)}) copy-start(s32[1,2]{1,0:T(1,128)} %count_ref.1) | copy-start | bytes 28
  0.7 13.4 %copy-start.2 = (s32[1,2,128]{2,1,0:T(2,128)S(1)}, s32[1,2,128]{2,1,0:T(2,128)}, u32[]{:S(2)}) copy-start(s32[1,2,128]{2,1,0:T(2,128)} %param.11) | copy-start | bytes 3076
  0.7 13.4 %copy-start = (bf16[1,128,128]{2,1,0:T(8,128)(2,1)S(1)}, bf16[1,128,128]{2,1,0:T(8,128)(2,1)}, u32[]{:S(2)}) copy-start(bf16[1,128,128]{2,1,0:T(8,128)(2,1)} %param.9) | copy-start | bytes 98308
  2.5 18.8 %all-to-all-start = ((bf16[32,8,512]{2,1,0:T(8,128)(2,1)}), bf16[32,8,512]{2,1,0:T(8,128)(2,1)S(1)}, u32[]{:S(2)}, u32[]{:S(2)}) async-start(bf16[32,8,512]{2,1,0:T(8,128)(2,1)} %shard_map.96), calls=%async_computation | async-start | bytes 524288 | tf_op jit(solution)/shard_map/all_to_all | solution.py:276
  21.3 22.8 %all-to-all-start.1 = ((bf16[8,512,128]{2,1,0:T(8,128)(2,1)}), bf16[8,512,128]{2,1,0:T(8,128)(2,1)S(1)}, u32[]{:S(2)}, u32[]{:S(2)}) async-start(bf16[8,512,128]{2,1,0:T(8,128)(2,1)} %shard_map.95), calls=%async_computation.1 | async-start | bytes 2097152 | tf_op jit(solution)/shard_map/all_to_all | solution.py:289
  46.4 19.1 %all-to-all-start.2 = ((bf16[4,4,112,128]{3,2,1,0:T(8,128)(2,1)}), bf16[4,4,112,128]{3,2,1,0:T(8,128)(2,1)S(1)}, u32[]{:S(2)}, u32[]{:S(2)}) async-start(bf16[4,4,112,128]{3,2,1,0:T(8,128)(2,1)} %get-tuple-element.17), calls=%async_computation.2 | async-start | bytes 917504 | tf_op jit(solution)/shard_map/all_to_all | solution.py:304
  55.1 6.5 %collective-permute-start = (bf16[8,144,128]{2,1,0:T(8,128)(2,1)S(1)}, bf16[8,144,128]{2,1,0:T(8,128)(2,1)S(1)}, u32[]{:S(2)}, u32[]{:S(2)}) collective-permute-start(bf16[8,144,128]{2,1,0:T(8,128)(2,1)S(1)} %get-tuple-element.19), channel_id=1, source_target_pairs={{0,32},{32,0},{1,33},{33,1},{2,34},{34,2},{3,35},{35,3},{4,36},{36... | collective-permute-start | bytes 884744 | tf_op jit(solution)/shard_map/ppermute | solution.py:303
  78.8 25.5 %all-to-all-start.4 = ((f32[8,1,8]{2,1,0:T(1,128)}), f32[8,1,8]{2,1,0:T(1,128)S(1)}, u32[]{:S(2)}, u32[]{:S(2)}) async-start(f32[8,1,8]{2,1,0:T(1,128)} %bitcast.10), calls=%async_computation.4 | async-start | bytes 8192 | tf_op jit(solution)/shard_map/all_to_all | solution.py:319
  104.3 9.2 %collective-permute-start.1 = (bf16[128,3584]{1,0:T(8,128)(2,1)S(1)}, bf16[128,3584]{1,0:T(8,128)(2,1)S(1)}, u32[]{:S(2)}, u32[]{:S(2)}) collective-permute-start(bf16[128,3584]{1,0:T(8,128)(2,1)S(1)} %all_gather.15.half_ref), channel_id=1, source_target_pairs={{0,32},{32,0},{1,33},{33,1},{2,34},{34,2},{3,35},{35,3},{4,36},{36... | collective-permute-start | bytes 2752520 | tf_op jit(solution)/shard_map/ppermute | solution.py:323

commit v13 on v12

--- a/solution.py
+++ b/solution.py
@@ -23,6 +23,7 @@
 BACK = FULL * CHUNK + CHUNK // 2
 W_PART = FULL * SHARE + SHARE // 2
 DENSE = FULL * TOKS + TOKS // 2
+FLAT = ROWS * WIDTH // LANES
 OWNED = E * M * N * ROWS
 
 
@@ -56,15 +57,6 @@
     return jnp.concatenate([a, pltpu.roll(a, TAIL, 1)], axis=0)
 
 
-def tokens_kernel(values_ref, scales_ref, out_ref):
-    scaled = values_ref[...].astype(F32) * column(scales_ref[...].astype(F32))
-    for l in range(L):
-        for n in range(C * X):
-            part = slice_of(scaled, n, l).astype(BF)
-            for i in range(N):
-                out_ref[((l * C + n // X) * N + i) * X + n % X] = part
-
-
 def own_slots(where_ref, tok_ref, count_ref):
     owner = where_ref[0]
     tok = jnp.where(owner == 0, tok_ref[0:1, :], tok_ref[1:2, :])
@@ -90,24 +82,46 @@
     return out.astype(BF)
 
 
-def pack_kernel(where_ref, count_ref, tok_ref, gate_ref, hidden_ref, out_ref):
+def first_kernel(where_ref, count_ref, tok_ref, gate_ref, hidden_ref, values_ref, scales_ref, out_ref):
+    scaled = values_ref[...].astype(F32) * column(scales_ref[...].astype(F32))
+    for t in range(0, WIDTH // LANES, 2):
+        two = [scaled[:, i * LANES : (i + 1) * LANES] for i in (t, t + 1)]
+        out_ref[t * ROWS : (t + 2) * ROWS, :] = jnp.concatenate(two, axis=0).astype(BF)
     gate = jnp.where(where_ref[0] == 0, gate_ref[0:1, :], gate_ref[1:2, :])
     tok = own_slots(where_ref, tok_ref, count_ref).astype(F32)
-    out_ref[0:SLOTS, :] = hidden_ref[...]
-    out_ref[SLOTS:PACK, :] = stack_rows((tok,) + split3(gate))
-
-
-def send_kernel(packs_ref, w_ref, out_ref):
+    out_ref[FLAT : FLAT + SLOTS, :] = hidden_ref[...]
+    out_ref[FLAT + SLOTS :, :] = stack_rows((tok,) + split3(gate))
+
+
+def tokens_kernel(core_ref, both_ref, out_ref):
+    half = FLAT // C
+    rows = []
+    for c in range(C):
+        a = both_ref[c, pl.ds(pl.multiple_of(core_ref[0] * half, EXTRA), half), :].astype(F32)
+        rows.append(jnp.concatenate([a[i : i + ROWS] for i in range(0, half, ROWS)], axis=1))
+    rows = jnp.concatenate(rows, axis=0)
+    for l in range(L):
+        for x in range(X):
+            part = slice_of(rows, x, l).astype(BF)
+            for i in range(N):
+                out_ref[(l * N + i) * X + x] = part
+
+
+def send_kernel(both_ref, w_ref, out_ref):
     w = w_ref[...].astype(F32)
     for l in range(L):
         for x in range(X):
-            out_ref[l * X + x, 0 : C * PACK, :] = packs_ref[...]
+            for c in range(C):
+                out_ref[l * X + x, c * PACK : (c + 1) * PACK, :] = both_ref[c, FLAT:, :]
             out_ref[l * X + x, C * PACK :, :] = dense(slice_of(w, x, l)).astype(BF)
 
 
 def dense_kernel(rows_ref, out_ref):
-    for g in range(QUARTERS):
-        out_ref[g] = dense(rows_ref[g].astype(F32)).astype(BF)
+    for l in range(L):
+        rows = [rows_ref[l * N * X + i].astype(F32) for i in range(N * X)]
+        for c in range(C):
+            part = jnp.concatenate([a[c * ROWS : (c + 1) * ROWS] for a in rows], axis=0)
+            out_ref[l * C + c] = dense(part).astype(BF)
 
 
 def weight_kernel(core_ref, mine_ref, pack_ref, part_ref, keep_ref, send_ref, routed_ref):
@@ -266,29 +280,30 @@
     hidden, tok, gate = hidden_act[0], slot_token[0], slot_gate[0]
     where = owner[None].astype(I32)
 
+    (both,) = call(
+        first_kernel,
+        [SM, SM, VM, VM, VM, VM, VM],
+        [((FLAT + PACK, LANES), BF)],
+        where, slot_count, tok, gate, hidden, grad_values, grad_scales.reshape(1, ROWS),
+        vmem=60,
+    )
+    both = lax.all_gather(both, "c", axis=0)
+
     (send,) = call(
         tokens_kernel,
-        [VM, VM],
-        [((N * PARTS, ROWS, WIDE), BF)],
-        grad_values, grad_scales.reshape(1, ROWS),
-        vmem=60,
-    )
-    mine = lax.all_to_all(send, ("l", "c", "n", "x"), 0, 0)
-
-    (pack,) = call(
-        pack_kernel,
-        [SM, SM, VM, VM, VM],
-        [((PACK, LANES), BF)],
-        where, slot_count, tok, gate, hidden,
-    )
-    packs = lax.all_gather(pack, "c", axis=0, tiled=True)
+        [SM, VM],
+        [((L * N * X, C * ROWS, WIDE), BF)],
+        core[None].astype(I32), both,
+    )
+    mine = lax.all_to_all(send, ("l", "n", "x"), 0, 0)
+
     width = X * PAIR
     w_part = lax.dynamic_slice(down_weight, (low * SHARE, core * width), (SHARE, width))
-    (pack,) = call(send_kernel, [VM, VM], [((L * X, C * PACK + W_PART, LANES), BF)], packs, w_part)
+    (pack,) = call(send_kernel, [VM, VM], [((L * X, C * PACK + W_PART, LANES), BF)], both, w_part)
     pack, mine = lax.optimization_barrier((pack, mine))
     pack = lax.all_to_all(pack, ("l", "x"), 0, 0)
     (mine,) = call(
-        dense_kernel, [VM], [((QUARTERS, DENSE, LANES), BF)], mine.reshape(QUARTERS, TOKS, WIDE)
+        dense_kernel, [VM], [((QUARTERS, DENSE, LANES), BF)], mine
     )
     mine = lax.all_gather(mine, ("e", "m"), axis=0)
 

time: 116 us -> 115 us (level)
  starting transfers between devices: 42.3 us -> 35.9 us
  blocking collectives: 51.7 us -> 55.5 us
  waiting for transfers between devices: 9.7 us -> 11.5 us
    all_to_all x1, starting transfers between devices: 10.4 us -> 3.53 us  [on_device(): mine = lax.all_to_all(send, ('l', 'n', 'x'), 0, 0)]
    all_gather x1, blocking collectives: 1.86 us -> 8.74 us  [on_device(): both = lax.all_gather(both, 'c', axis=0)]
    ppermute x1, starting transfers between devices: 7.12 us -> 9.55 us  [on_device(): other = lax.ppermute(block, 'c', [(i, C - 1 - i) for i in range(C)])]
    all_gather x1, blocking collectives: 19.1 us -> 17 us  [on_device(): mine = lax.all_gather(mine, ('e', 'm'), axis=0)]
    all_to_all x1, starting transfers between devices: 7.07 us -> 5.14 us  [on_device(): spread = lax.all_to_all(spread, ('e', 'm', 'n'), 0, 0, tiled=True)]
    all_to_all x1, waiting for transfers between devices: 3.6 us -> 5.51 us  [on_device(): mine = lax.all_to_all(send, ('l', 'n', 'x'), 0, 0)]
    all_gather x1, blocking collectives: 18.4 us -> 16.7 us  [on_device(): block = lax.all_gather(block, 'h', axis=0, tiled=True)]
where the time goes in v13:
time: 115 us; the launch traced here: 114 us
  blocking collectives  55.5 us (48%)
  starting transfers between devices  35.9 us (31%)
  waiting for transfers between devices  11.5 us (10%)
  Pallas kernels  9.61 us (8%)
    all_gather x1, blocking collectives, on_device(): mine = lax.all_gather(mine, ('e', 'm'), axis=0)  17 us
    all_gather x1, blocking collectives, on_device(): block = lax.all_gather(block, 'h', axis=0, tiled=True)  16.7 us
    all_to_all x1, blocking collectives, on_device(): got = lax.all_to_all(send, ('l', 'x'), 0, 0)  13.1 us
    pallas_call x9, Pallas kernels, call(): pl.pallas_call(kernel, out_shape=outs, in_specs=places, out_specs=out_pla...  9.61 us
    ppermute x1, starting transfers between devices, on_device(): other = lax.ppermute(block, 'c', [(i, C - 1 - i) for i in range(C)])  9.55 us
    all_to_all x1, starting transfers between devices, on_device(): sums = lax.all_to_all(part, 'h', 0, 0)  9.49 us
    all_gather x1, blocking collectives, on_device(): both = lax.all_gather(both, 'c', axis=0)  8.74 us
    all_to_all x1, waiting for transfers between devices, on_device(): mine = lax.all_to_all(send, ('l', 'n', 'x'), 0, 0)  5.51 us
  transfers between devices with their start and end apart: 6, of which 4 were waited for; matrix products, arithmetic and copies ran while one was open for 1% of the time, Pallas kernels for 2%

profile of v13, /device:TPU:1, one launch (start us, length us, event | category | flops | bytes accessed | tf_op | source)
XLA Modules:
  0.0 114.3 jit_solution(17561687942148727772)
XLA Ops:
  0.6 1.7 %shard_map.94 = bf16[592,128]{1,0:T(8,128)(2,1)} custom-call(s32[1]{0:T(128)} %bitcast.where_ref, s32[1,2]{1,0:T(1,128)} %count_ref.1, s32[2,128]{1,0:T(2,128)} %bitcast.21, f32[2,128]{1,0:T(2,128)} %bitcast.18, bf16[128,128]{1,0:T(8,128)(2,1)} %bitcast.20, bf16[8,7168]{1,0:T(8,128)(2,1)} %values_ref.1, bf16[1,8]{1,0:T(2,128)(2,1)} %bitcast.22), custom_call_target="tpu_custom_call" | custom-call | bytes 301084 | tf_op jit(solution)/shard_map/pallas_call | solution.py:266
  2.3 8.7 %all-gather = bf16[1184,128]{1,0:T(8,128)(2,1)S(1)} all-gather(bf16[592,128]{1,0:T(8,128)(2,1)} %shard_map.94), channel_id=2, replica_groups=mesh['h'=4,'l'=2,'c'=2,'e'=2,'m'=2,'n'=2,'x'=4] {'c'}, dimensions={0}, use_global_device_ids=true | all-gather | bytes 454656 | tf_op jit(solution)/shard_map/all_gather | solution.py:290
  11.1 0.8 shard_map.96
  11.9 3.5 %all-to-all-start = ((bf16[16,16,512]{2,1,0:T(8,128)(2,1)}), bf16[16,16,512]{2,1,0:T(8,128)(2,1)S(1)}, u32[]{:S(2)}, u32[]{:S(2)}) async-start(bf16[16,16,512]{2,1,0:T(8,128)(2,1)} %shard_map.96), calls=%async_computation | async-start | bytes 524288 | tf_op jit(solution)/shard_map/all_to_all | solution.py:298
  15.4 1.1 dynamic_slice.3.w_ref
  16.5 1.2 %shard_map.95 = bf16[8,512,128]{2,1,0:T(8,128)(2,1)} custom-call(bf16[2,592,128]{2,1,0:T(8,128)(2,1)S(1)} %bitcast.15, bf16[64,3584]{1,0:T(8,128)(2,1)S(1)} %dynamic_slice.3.w_ref), custom_call_target="tpu_custom_call" | custom-call | bytes 1810432 | tf_op jit(solution)/shard_map/pallas_call | solution.py:266
  17.7 5.5 %all-to-all-done.rows_ref = bf16[16,16,512]{2,1,0:T(8,128)(2,1)S(1)} async-done(((bf16[16,16,512]{2,1,0:T(8,128)(2,1)}), bf16[16,16,512]{2,1,0:T(8,128)(2,1)S(1)}, u32[]{:S(2)}, u32[]{:S(2)}) %all-to-all-start) | async-done | bytes 262176 | tf_op jit(solution)/shard_map/all_to_all | solution.py:298
  23.2 3.6 %all-to-all-start.1 = ((bf16[8,512,128]{2,1,0:T(8,128)(2,1)}), bf16[8,512,128]{2,1,0:T(8,128)(2,1)S(1)}, u32[]{:S(2)}, u32[]{:S(2)}) async-start(bf16[8,512,128]{2,1,0:T(8,128)(2,1)} %shard_map.95), calls=%async_computation.1 | async-start | bytes 2097152 | tf_op jit(solution)/shard_map/all_to_all | solution.py:304
  26.8 0.1 shard_map.97
  26.8 17.0 %all-gather.1 = bf16[16,224,128]{2,1,0:T(8,128)(2,1)S(1)} all-gather(bf16[4,224,128]{2,1,0:T(8,128)(2,1)S(1)} %shard_map.97), channel_id=3, replica_groups=mesh['h'=4,'l'=2,'c'=2,'e'=2,'m'=2,'n'=2,'x'=4] {'e','m'}, dimensions={0}, use_global_device_ids=true | all-gather | bytes 1146880 | tf_op jit(solution)/shard_map/all_gather | solution.py:308
  43.9 2.4 %shard_map.98 = (bf16[4,4,112,128]{3,2,1,0:T(8,128)(2,1)}, bf16[8,144,128]{2,1,0:T(8,128)(2,1)S(1)}, bf16[8,144,128]{2,1,0:T(8,128)(2,1)S(1)}) custom-call(s32[1]{0:T(128)} %bitcast.2.core_ref, bf16[4,4,224,128]{3,2,1,0:T(8,128)(2,1)S(1)} %bitcast.16, bf16[8,512,128]{2,1,0:T(8,128)(2,1)S(1)} %all-to-all-done.1.pack_ref), custom_call_target="tpu_custom_call" | custom-call | flops 654311424 | bytes 3014660 | tf_op jit(solution)/shard_map/pallas_call | solution.py:266
  46.2 9.5 %all-to-all-start.2 = ((bf16[4,4,112,128]{3,2,1,0:T(8,128)(2,1)}), bf16[4,4,112,128]{3,2,1,0:T(8,128)(2,1)S(1)}, u32[]{:S(2)}, u32[]{:S(2)}) async-start(bf16[4,4,112,128]{3,2,1,0:T(8,128)(2,1)} %get-tuple-element.17), calls=%async_computation.2 | async-start | bytes 917504 | tf_op jit(solution)/shard_map/all_to_all | solution.py:319
  55.7 4.6 %collective-permute-start = (bf16[8,144,128]{2,1,0:T(8,128)(2,1)S(1)}, bf16[8,144,128]{2,1,0:T(8,128)(2,1)S(1)}, u32[]{:S(2)}, u32[]{:S(2)}) collective-permute-start(bf16[8,144,128]{2,1,0:T(8,128)(2,1)S(1)} %get-tuple-element.19), channel_id=1, source_target_pairs={{0,32},{32,0},{1,33},{33,1},{2,34},{34,2},{3,35},{35,3},{4,36},{36... | collective-permute-start | bytes 884744 | tf_op jit(solution)/shard_map/ppermute | solution.py:318
  60.4 1.2 %collective-permute-done.other_ref = bf16[8,144,128]{2,1,0:T(8,128)(2,1)S(1)} collective-permute-done((bf16[8,144,128]{2,1,0:T(8,128)(2,1)S(1)}, bf16[8,144,128]{2,1,0:T(8,128)(2,1)S(1)}, u32[]{:S(2)}, u32[]{:S(2)}) %collective-permute-start) | collective-permute-done | bytes 294944 | tf_op jit(solution)/shard_map/ppermute | solution.py:318
  61.6 3.7 %all-to-all-done.2.sums_ref = bf16[4,4,112,128]{3,2,1,0:T(8,128)(2,1)S(1)} async-done(((bf16[4,4,112,128]{3,2,1,0:T(8,128)(2,1)}), bf16[4,4,112,128]{3,2,1,0:T(8,128)(2,1)S(1)}, u32[]{:S(2)}, u32[]{:S(2)}) %all-to-all-start.2) | async-done | bytes 458784 | tf_op jit(solution)/shard_map/all_to_all | solution.py:319
  65.2 0.2 shard_map.99
  65.5 13.1 %all_to_all.32.got_ref = bf16[8,256,128]{2,1,0:T(8,128)(2,1)S(1)} all-to-all(bf16[8,256,128]{2,1,0:T(8,128)(2,1)S(1)} %shard_map.99), channel_id=1, replica_groups=mesh['h'=4,'l'=2,'c'=2,'e'=2,'m'=2,'n'=2,'x'=4] {'l','x'}, dimensions={0} | all-to-all | bytes 1048576 | tf_op jit(solution)/shard_map/all_to_all | solution.py:327
  78.5 0.8 shard_map.100
  79.4 5.1 %all-to-all-start.4 = ((f32[8,1,8]{2,1,0:T(1,128)}), f32[8,1,8]{2,1,0:T(1,128)S(1)}, u32[]{:S(2)}, u32[]{:S(2)}) async-start(f32[8,1,8]{2,1,0:T(1,128)} %bitcast.10), calls=%async_computation.4 | async-start | bytes 8192 | tf_op jit(solution)/shard_map/all_to_all | solution.py:334
  84.5 16.7 %all_gather.19.half_ref = bf16[128,3584]{1,0:T(8,128)(2,1)S(1)} all-gather(bf16[32,3584]{1,0:T(8,128)(2,1)S(1)} %get-tuple-element.21), channel_id=1, replica_groups=mesh['h'=4,'l'=2,'c'=2,'e'=2,'m'=2,'n'=2,'x'=4] {'h'}, dimensions={0}, use_global_device_ids=true | all-gather | bytes 1146880 | tf_op jit(solution)/shard_map/all_gather | solution.py:336
  101.2 9.5 %collective-permute-start.1 = (bf16[128,3584]{1,0:T(8,128)(2,1)S(1)}, bf16[128,3584]{1,0:T(8,128)(2,1)S(1)}, u32[]{:S(2)}, u32[]{:S(2)}) collective-permute-start(bf16[128,3584]{1,0:T(8,128)(2,1)S(1)} %all_gather.19.half_ref), channel_id=1, source_target_pairs={{0,32},{32,0},{1,33},{33,1},{2,34},{34,2},{3,35},{35,3},{4,36},{36... | collective-permute-start | bytes 2752520 | tf_op jit(solution)/shard_map/ppermute | solution.py:338
  110.7 0.9 shard_map.101.out_in_ref
  111.7 1.1 collective-permute-done.1.half_ref
  112.8 1.5 %shard_map.102 = (bf16[128,7168]{1,0:T(8,128)(2,1)}, f32[2,8]{1,0:T(2,128)}) custom-call(s32[1]{0:T(128)} %bitcast.2.core_ref, bf16[128,3584]{1,0:T(8,128)(2,1)S(1)} %collective-permute-done.1.half_ref, f32[8,8]{1,0:T(8,128)S(1)} %bitcast.17, bf16[128,7168]{1,0:T(8,128)(2,1)} %shard_map.101.out_in_ref), custom_call_target="tpu_custom_call", output_to_operand_aliasing={{0}: (3, {})} | custom-call | bytes 4587844 | tf_op jit(solution)/shard_map/pallas_call | solution.py:266
  (4 shorter events, 0.0 us)
Async XLA Ops:
  11.9 11.3 %all-to-all-start = ((bf16[16,16,512]{2,1,0:T(8,128)(2,1)}), bf16[16,16,512]{2,1,0:T(8,128)(2,1)S(1)}, u32[]{:S(2)}, u32[]{:S(2)}) async-start(bf16[16,16,512]{2,1,0:T(8,128)(2,1)} %shard_map.96), calls=%async_computation | async-start | bytes 524288 | tf_op jit(solution)/shard_map/all_to_all | solution.py:298
  23.2 20.7 %all-to-all-start.1 = ((bf16[8,512,128]{2,1,0:T(8,128)(2,1)}), bf16[8,512,128]{2,1,0:T(8,128)(2,1)S(1)}, u32[]{:S(2)}, u32[]{:S(2)}) async-start(bf16[8,512,128]{2,1,0:T(8,128)(2,1)} %shard_map.95), calls=%async_computation.1 | async-start | bytes 2097152 | tf_op jit(solution)/shard_map/all_to_all | solution.py:304
  46.2 32.3 %copy-start = (f32[1,2,128]{2,1,0:T(2,128)S(1)}, f32[1,2,128]{2,1,0:T(2,128)}, u32[]{:S(2)}) copy-start(f32[1,2,128]{2,1,0:T(2,128)} %param.13) | copy-start | bytes 3076
  46.2 19.0 %all-to-all-start.2 = ((bf16[4,4,112,128]{3,2,1,0:T(8,128)(2,1)}), bf16[4,4,112,128]{3,2,1,0:T(8,128)(2,1)S(1)}, u32[]{:S(2)}, u32[]{:S(2)}) async-start(bf16[4,4,112,128]{3,2,1,0:T(8,128)(2,1)} %get-tuple-element.17), calls=%async_computation.2 | async-start | bytes 917504 | tf_op jit(solution)/shard_map/all_to_all | solution.py:319
  55.7 5.8 %collective-permute-start = (bf16[8,144,128]{2,1,0:T(8,128)(2,1)S(1)}, bf16[8,144,128]{2,1,0:T(8,128)(2,1)S(1)}, u32[]{:S(2)}, u32[]{:S(2)}) collective-permute-start(bf16[8,144,128]{2,1,0:T(8,128)(2,1)S(1)} %get-tuple-element.19), channel_id=1, source_target_pairs={{0,32},{32,0},{1,33},{33,1},{2,34},{34,2},{3,35},{35,3},{4,36},{36... | collective-permute-start | bytes 884744 | tf_op jit(solution)/shard_map/ppermute | solution.py:318
  79.4 21.8 %all-to-all-start.4 = ((f32[8,1,8]{2,1,0:T(1,128)}), f32[8,1,8]{2,1,0:T(1,128)S(1)}, u32[]{:S(2)}, u32[]{:S(2)}) async-start(f32[8,1,8]{2,1,0:T(1,128)} %bitcast.10), calls=%async_computation.4 | async-start | bytes 8192 | tf_op jit(solution)/shard_map/all_to_all | solution.py:334
  101.2 11.6 %collective-permute-start.1 = (bf16[128,3584]{1,0:T(8,128)(2,1)S(1)}, bf16[128,3584]{1,0:T(8,128)(2,1)S(1)}, u32[]{:S(2)}, u32[]{:S(2)}) collective-permute-start(bf16[128,3584]{1,0:T(8,128)(2,1)S(1)} %all_gather.19.half_ref), channel_id=1, source_target_pairs={{0,32},{32,0},{1,33},{33,1},{2,34},{34,2},{3,35},{35,3},{4,36},{36... | collective-permute-start | bytes 2752520 | tf_op jit(solution)/shard_map/ppermute | solution.py:338

commit v14 on v12

--- a/solution.py
+++ b/solution.py
@@ -110,7 +110,7 @@
         out_ref[g] = dense(rows_ref[g].astype(F32)).astype(BF)
 
 
-def weight_kernel(core_ref, mine_ref, pack_ref, part_ref, keep_ref, send_ref, routed_ref):
+def weight_kernel(mine_ref, pack_ref, part_ref, routed_ref):
     ids = lax.broadcasted_iota(I32, (GROUP, SLOTS), 0)
     first = (((0,), (0,)), ((), ()))
     gates = []
@@ -141,6 +141,8 @@
         for h in range(H):
             part_ref[h, x] = dense(part[h * CHUNK : (h + 1) * CHUNK]).astype(BF)
 
+
+def project_kernel(core_ref, routed_ref, pack_ref, keep_ref, send_ref):
     core = core_ref[0]
     groups = [(l, c) for c in (core, 1 - core) for l in range(L)]
     outs = [(ref, l) for ref in (keep_ref, send_ref) for l in range(L)]
@@ -292,13 +294,19 @@
     )
     mine = lax.all_gather(mine, ("e", "m"), axis=0)
 
-    part, keep, other = call(
+    part, routed = call(
         weight_kernel,
+        [VM, VM],
+        [((H, X, BACK, LANES), BF), ((QUARTERS * SLOTS, WIDE), BF)],
+        mine, pack,
+        flops=2 * QUARTERS * SLOTS * WIDE * (GROUP + X * UNITS),
+    )
+    keep, other = call(
+        project_kernel,
         [SM, VM, VM],
-        [((H, X, BACK, LANES), BF), ((L * X, PACK, LANES), BF), ((L * X, PACK, LANES), BF)],
-        core[None].astype(I32), mine, pack,
-        scratch=[pltpu.VMEM((QUARTERS * SLOTS, WIDE), BF)],
-        flops=2 * QUARTERS * SLOTS * (COLS * GROUP + 2 * WIDE * X * UNITS),
+        [((L * X, PACK, LANES), BF), ((L * X, PACK, LANES), BF)],
+        core[None].astype(I32), routed, pack,
+        flops=2 * QUARTERS * SLOTS * WIDE * X * UNITS,
     )
     other = lax.ppermute(other, "c", [(i, C - 1 - i) for i in range(C)])
     sums = lax.all_to_all(part, "h", 0, 0)

time: 116 us -> 115 us (level)
    pallas_call x9 -> x10, Pallas kernels: 9.5 us -> 9.89 us  [call(): pl.pallas_call(kernel, out_shape=outs, in_specs=places, out_specs=out_pla...]
  transfers between devices with their start and end apart: 6 -> 6, of which waited for: 4 -> 4; matrix products, arithmetic and copies ran while one was open for 1% -> 1% of each run, Pallas kernels for 2% -> 3%
where the time goes in v14:
time: 115 us; the launch traced here: 114 us
  blocking collectives  51.6 us (45%)
  starting transfers between devices  42.3 us (37%)
  Pallas kernels  9.89 us (9%)
  waiting for transfers between devices  8.57 us (7%)
    all_gather x1, blocking collectives, on_device(): mine = lax.all_gather(mine, ('e', 'm'), axis=0)  19.1 us
    all_gather x1, blocking collectives, on_device(): block = lax.all_gather(block, 'h', axis=0, tiled=True)  18.3 us
    all_to_all x1, blocking collectives, on_device(): got = lax.all_to_all(send, ('l', 'x'), 0, 0)  12.3 us
    all_to_all x1, starting transfers between devices, on_device(): mine = lax.all_to_all(send, ('l', 'c', 'n', 'x'), 0, 0)  10.4 us
    pallas_call x10, Pallas kernels, call(): pl.pallas_call(kernel, out_shape=outs, in_specs=places, out_specs=out_pla...  9.89 us
    all_to_all x1, starting transfers between devices, on_device(): sums = lax.all_to_all(part, 'h', 0, 0)  8.74 us
    ppermute x1, starting transfers between devices, on_device(): other = lax.ppermute(block, 'c', [(i, C - 1 - i) for i in range(C)])  7.13 us
    all_to_all x1, starting transfers between devices, on_device(): spread = lax.all_to_all(spread, ('e', 'm', 'n'), 0, 0, tiled=True)  7.07 us
  transfers between devices with their start and end apart: 6, of which 4 were waited for; matrix products, arithmetic and copies ran while one was open for 1% of the time, Pallas kernels for 3%

profile of v14, /device:TPU:1, one launch (start us, length us, event | category | flops | bytes accessed | tf_op | source)
XLA Modules:
  0.0 114.2 jit_solution(342851834574759805)
XLA Ops:
  0.7 1.8 %shard_map.96 = bf16[32,8,512]{2,1,0:T(8,128)(2,1)} custom-call(bf16[8,7168]{1,0:T(8,128)(2,1)} %values_ref.1, bf16[1,8]{1,0:T(2,128)(2,1)} %bitcast.21), custom_call_target="tpu_custom_call" | custom-call | bytes 376848 | tf_op jit(solution)/shard_map/pallas_call | solution.py:254
  2.5 10.4 %all-to-all-start = ((bf16[32,8,512]{2,1,0:T(8,128)(2,1)}), bf16[32,8,512]{2,1,0:T(8,128)(2,1)S(1)}, u32[]{:S(2)}, u32[]{:S(2)}) async-start(bf16[32,8,512]{2,1,0:T(8,128)(2,1)} %shard_map.96), calls=%async_computation | async-start | bytes 524288 | tf_op jit(solution)/shard_map/all_to_all | solution.py:278
  12.9 1.1 dynamic_slice.3.w_ref
  14.0 0.6 shard_map.94
  14.6 1.9 %all_gather.12.packs_ref = bf16[288,128]{1,0:T(8,128)(2,1)S(1)} all-gather(bf16[144,128]{1,0:T(8,128)(2,1)S(1)} %shard_map.94), channel_id=1, replica_groups=mesh['h'=4,'l'=2,'c'=2,'e'=2,'m'=2,'n'=2,'x'=4] {'c'}, dimensions={0}, use_global_device_ids=true | all-gather | bytes 110592 | tf_op jit(solution)/shard_map/all_gather | solution.py:286
  16.4 1.2 %shard_map.95 = bf16[8,512,128]{2,1,0:T(8,128)(2,1)} custom-call(bf16[288,128]{1,0:T(8,128)(2,1)S(1)} %all_gather.12.packs_ref, bf16[64,3584]{1,0:T(8,128)(2,1)S(1)} %dynamic_slice.3.w_ref), custom_call_target="tpu_custom_call" | custom-call | bytes 1581056 | tf_op jit(solution)/shard_map/pallas_call | solution.py:254
  17.7 3.6 %all-to-all-done = bf16[32,8,512]{2,1,0:T(8,128)(2,1)S(1)} async-done(((bf16[32,8,512]{2,1,0:T(8,128)(2,1)}), bf16[32,8,512]{2,1,0:T(8,128)(2,1)S(1)}, u32[]{:S(2)}, u32[]{:S(2)}) %all-to-all-start) | async-done | bytes 262176 | tf_op jit(solution)/shard_map/all_to_all | solution.py:278
  21.3 3.6 %all-to-all-start.1 = ((bf16[8,512,128]{2,1,0:T(8,128)(2,1)}), bf16[8,512,128]{2,1,0:T(8,128)(2,1)S(1)}, u32[]{:S(2)}, u32[]{:S(2)}) async-start(bf16[8,512,128]{2,1,0:T(8,128)(2,1)} %shard_map.95), calls=%async_computation.1 | async-start | bytes 2097152 | tf_op jit(solution)/shard_map/all_to_all | solution.py:291
  24.9 19.1 %all-gather = bf16[16,224,128]{2,1,0:T(8,128)(2,1)S(1)} all-gather(bf16[4,224,128]{2,1,0:T(8,128)(2,1)S(1)} %shard_map.97), channel_id=2, replica_groups=mesh['h'=4,'l'=2,'c'=2,'e'=2,'m'=2,'n'=2,'x'=4] {'e','m'}, dimensions={0}, use_global_device_ids=true | all-gather | bytes 1146880 | tf_op jit(solution)/shard_map/all_gather | solution.py:295
  44.0 1.6 %shard_map.98 = (bf16[4,4,112,128]{3,2,1,0:T(8,128)(2,1)}, bf16[512,512]{1,0:T(8,128)(2,1)S(1)}) custom-call(bf16[4,4,224,128]{3,2,1,0:T(8,128)(2,1)S(1)} %bitcast.14, bf16[8,512,128]{2,1,0:T(8,128)(2,1)S(1)} %all-to-all-done.1.pack_ref), custom_call_target="tpu_custom_call" | custom-call | flops 402653184 | bytes 2949120 | tf_op jit(solution)/shard_map/pallas_call | solution.py:254
  45.7 8.7 %all-to-all-start.2 = ((bf16[4,4,112,128]{3,2,1,0:T(8,128)(2,1)}), bf16[4,4,112,128]{3,2,1,0:T(8,128)(2,1)S(1)}, u32[]{:S(2)}, u32[]{:S(2)}) async-start(bf16[4,4,112,128]{3,2,1,0:T(8,128)(2,1)} %get-tuple-element.18), calls=%async_computation.2 | async-start | bytes 917504 | tf_op jit(solution)/shard_map/all_to_all | solution.py:312
  54.4 1.1 shard_map.99
  55.5 5.3 %collective-permute-start = (bf16[8,144,128]{2,1,0:T(8,128)(2,1)S(1)}, bf16[8,144,128]{2,1,0:T(8,128)(2,1)S(1)}, u32[]{:S(2)}, u32[]{:S(2)}) collective-permute-start(bf16[8,144,128]{2,1,0:T(8,128)(2,1)S(1)} %get-tuple-element.21), channel_id=1, source_target_pairs={{0,32},{32,0},{1,33},{33,1},{2,34},{34,2},{3,35},{35,3},{4,36},{36... | collective-permute-start | bytes 884744 | tf_op jit(solution)/shard_map/ppermute | solution.py:311
  60.9 1.2 %collective-permute-done.other_ref = bf16[8,144,128]{2,1,0:T(8,128)(2,1)S(1)} collective-permute-done((bf16[8,144,128]{2,1,0:T(8,128)(2,1)S(1)}, bf16[8,144,128]{2,1,0:T(8,128)(2,1)S(1)}, u32[]{:S(2)}, u32[]{:S(2)}) %collective-permute-start) | collective-permute-done | bytes 294944 | tf_op jit(solution)/shard_map/ppermute | solution.py:311
  62.1 2.6 %all-to-all-done.2.sums_ref = bf16[4,4,112,128]{3,2,1,0:T(8,128)(2,1)S(1)} async-done(((bf16[4,4,112,128]{3,2,1,0:T(8,128)(2,1)}), bf16[4,4,112,128]{3,2,1,0:T(8,128)(2,1)S(1)}, u32[]{:S(2)}, u32[]{:S(2)}) %all-to-all-start.2) | async-done | bytes 458784 | tf_op jit(solution)/shard_map/all_to_all | solution.py:312
  64.7 0.2 shard_map.100
  64.9 12.3 %all_to_all.32.got_ref = bf16[8,256,128]{2,1,0:T(8,128)(2,1)S(1)} all-to-all(bf16[8,256,128]{2,1,0:T(8,128)(2,1)S(1)} %shard_map.100), channel_id=1, replica_groups=mesh['h'=4,'l'=2,'c'=2,'e'=2,'m'=2,'n'=2,'x'=4] {'l','x'}, dimensions={0} | all-to-all | bytes 1048576 | tf_op jit(solution)/shard_map/all_to_all | solution.py:320
  77.2 0.8 shard_map.101
  78.1 7.1 %all-to-all-start.4 = ((f32[8,1,8]{2,1,0:T(1,128)}), f32[8,1,8]{2,1,0:T(1,128)S(1)}, u32[]{:S(2)}, u32[]{:S(2)}) async-start(f32[8,1,8]{2,1,0:T(1,128)} %bitcast.10), calls=%async_computation.4 | async-start | bytes 8192 | tf_op jit(solution)/shard_map/all_to_all | solution.py:327
  85.1 18.3 %all_gather.15.half_ref = bf16[128,3584]{1,0:T(8,128)(2,1)S(1)} all-gather(bf16[32,3584]{1,0:T(8,128)(2,1)S(1)} %get-tuple-element.23), channel_id=1, replica_groups=mesh['h'=4,'l'=2,'c'=2,'e'=2,'m'=2,'n'=2,'x'=4] {'h'}, dimensions={0}, use_global_device_ids=true | all-gather | bytes 1146880 | tf_op jit(solution)/shard_map/all_gather | solution.py:329
  103.4 7.1 %collective-permute-start.1 = (bf16[128,3584]{1,0:T(8,128)(2,1)S(1)}, bf16[128,3584]{1,0:T(8,128)(2,1)S(1)}, u32[]{:S(2)}, u32[]{:S(2)}) collective-permute-start(bf16[128,3584]{1,0:T(8,128)(2,1)S(1)} %all_gather.15.half_ref), channel_id=1, source_target_pairs={{0,32},{32,0},{1,33},{33,1},{2,34},{34,2},{3,35},{35,3},{4,36},{36... | collective-permute-start | bytes 2752520 | tf_op jit(solution)/shard_map/ppermute | solution.py:331
  110.6 0.9 shard_map.102.out_in_ref
  111.5 1.1 collective-permute-done.1.half_ref
  112.7 1.5 %shard_map.103 = (bf16[128,7168]{1,0:T(8,128)(2,1)}, f32[2,8]{1,0:T(2,128)}) custom-call(s32[1]{0:T(128)} %bitcast.7.core_ref, bf16[128,3584]{1,0:T(8,128)(2,1)S(1)} %collective-permute-done.1.half_ref, f32[8,8]{1,0:T(8,128)S(1)} %bitcast.17, bf16[128,7168]{1,0:T(8,128)(2,1)} %shard_map.102.out_in_ref), custom_call_target="tpu_custom_call", output_to_operand_aliasing={{0}: (3, {})} | custom-call | bytes 4587844 | tf_op jit(solution)/shard_map/pallas_call | solution.py:254
  (11 shorter events, 0.1 us)
Async XLA Ops:
  0.6 13.3 %copy-start.1 = (f32[1,2,128]{2,1,0:T(2,128)S(1)}, f32[1,2,128]{2,1,0:T(2,128)}, u32[]{:S(2)}) copy-start(f32[1,2,128]{2,1,0:T(2,128)} %param.13) | copy-start | bytes 3076
  0.6 13.3 %copy-start.3 = (s32[1,2]{1,0:T(1,128)S(1)}, s32[1,2]{1,0:T(1,128)}, u32[]{:S(2)}) copy-start(s32[1,2]{1,0:T(1,128)} %count_ref.1) | copy-start | bytes 28
  0.7 13.3 %copy-start.2 = (s32[1,2,128]{2,1,0:T(2,128)S(1)}, s32[1,2,128]{2,1,0:T(2,128)}, u32[]{:S(2)}) copy-start(s32[1,2,128]{2,1,0:T(2,128)} %param.11) | copy-start | bytes 3076
  0.7 13.3 %copy-start = (bf16[1,128,128]{2,1,0:T(8,128)(2,1)S(1)}, bf16[1,128,128]{2,1,0:T(8,128)(2,1)}, u32[]{:S(2)}) copy-start(bf16[1,128,128]{2,1,0:T(8,128)(2,1)} %param.9) | copy-start | bytes 98308
  2.5 18.8 %all-to-all-start = ((bf16[32,8,512]{2,1,0:T(8,128)(2,1)}), bf16[32,8,512]{2,1,0:T(8,128)(2,1)S(1)}, u32[]{:S(2)}, u32[]{:S(2)}) async-start(bf16[32,8,512]{2,1,0:T(8,128)(2,1)} %shard_map.96), calls=%async_computation | async-start | bytes 524288 | tf_op jit(solution)/shard_map/all_to_all | solution.py:278
  21.3 22.8 %all-to-all-start.1 = ((bf16[8,512,128]{2,1,0:T(8,128)(2,1)}), bf16[8,512,128]{2,1,0:T(8,128)(2,1)S(1)}, u32[]{:S(2)}, u32[]{:S(2)}) async-start(bf16[8,512,128]{2,1,0:T(8,128)(2,1)} %shard_map.95), calls=%async_computation.1 | async-start | bytes 2097152 | tf_op jit(solution)/shard_map/all_to_all | solution.py:291
  45.7 19.1 %all-to-all-start.2 = ((bf16[4,4,112,128]{3,2,1,0:T(8,128)(2,1)}), bf16[4,4,112,128]{3,2,1,0:T(8,128)(2,1)S(1)}, u32[]{:S(2)}, u32[]{:S(2)}) async-start(bf16[4,4,112,128]{3,2,1,0:T(8,128)(2,1)} %get-tuple-element.18), calls=%async_computation.2 | async-start | bytes 917504 | tf_op jit(solution)/shard_map/all_to_all | solution.py:312
  55.5 6.5 %collective-permute-start = (bf16[8,144,128]{2,1,0:T(8,128)(2,1)S(1)}, bf16[8,144,128]{2,1,0:T(8,128)(2,1)S(1)}, u32[]{:S(2)}, u32[]{:S(2)}) collective-permute-start(bf16[8,144,128]{2,1,0:T(8,128)(2,1)S(1)} %get-tuple-element.21), channel_id=1, source_target_pairs={{0,32},{32,0},{1,33},{33,1},{2,34},{34,2},{3,35},{35,3},{4,36},{36... | collective-permute-start | bytes 884744 | tf_op jit(solution)/shard_map/ppermute | solution.py:311
  78.1 25.4 %all-to-all-start.4 = ((f32[8,1,8]{2,1,0:T(1,128)}), f32[8,1,8]{2,1,0:T(1,128)S(1)}, u32[]{:S(2)}, u32[]{:S(2)}) async-start(f32[8,1,8]{2,1,0:T(1,128)} %bitcast.10), calls=%async_computation.4 | async-start | bytes 8192 | tf_op jit(solution)/shard_map/all_to_all | solution.py:327
  103.4 9.2 %collective-permute-start.1 = (bf16[128,3584]{1,0:T(8,128)(2,1)S(1)}, bf16[128,3584]{1,0:T(8,128)(2,1)S(1)}, u32[]{:S(2)}, u32[]{:S(2)}) collective-permute-start(bf16[128,3584]{1,0:T(8,128)(2,1)S(1)} %all_gather.15.half_ref), channel_id=1, source_target_pairs={{0,32},{32,0},{1,33},{33,1},{2,34},{34,2},{3,35},{35,3},{4,36},{36... | collective-permute-start | bytes 2752520 | tf_op jit(solution)/shard_map/ppermute | solution.py:331

commit v15 on v13

--- a/solution.py
+++ b/solution.py
@@ -124,7 +124,7 @@
             out_ref[l * C + c] = dense(part).astype(BF)
 
 
-def weight_kernel(core_ref, mine_ref, pack_ref, part_ref, keep_ref, send_ref, routed_ref):
+def weight_kernel(mine_ref, pack_ref, part_ref, routed_ref):
     ids = lax.broadcasted_iota(I32, (GROUP, SLOTS), 0)
     first = (((0,), (0,)), ((), ()))
     gates = []
@@ -155,6 +155,8 @@
         for h in range(H):
             part_ref[h, x] = dense(part[h * CHUNK : (h + 1) * CHUNK]).astype(BF)
 
+
+def project_kernel(core_ref, routed_ref, pack_ref, keep_ref, send_ref):
     core = core_ref[0]
     groups = [(l, c) for c in (core, 1 - core) for l in range(L)]
     outs = [(ref, l) for ref in (keep_ref, send_ref) for l in range(L)]
@@ -307,13 +309,19 @@
     )
     mine = lax.all_gather(mine, ("e", "m"), axis=0)
 
-    part, keep, other = call(
+    part, routed = call(
         weight_kernel,
+        [VM, VM],
+        [((H, X, BACK, LANES), BF), ((QUARTERS * SLOTS, WIDE), BF)],
+        mine, pack,
+        flops=2 * QUARTERS * SLOTS * WIDE * (GROUP + X * UNITS),
+    )
+    keep, other = call(
+        project_kernel,
         [SM, VM, VM],
-        [((H, X, BACK, LANES), BF), ((L * X, PACK, LANES), BF), ((L * X, PACK, LANES), BF)],
-        core[None].astype(I32), mine, pack,
-        scratch=[pltpu.VMEM((QUARTERS * SLOTS, WIDE), BF)],
-        flops=2 * QUARTERS * SLOTS * (COLS * GROUP + 2 * WIDE * X * UNITS),
+        [((L * X, PACK, LANES), BF), ((L * X, PACK, LANES), BF)],
+        core[None].astype(I32), routed, pack,
+        flops=2 * QUARTERS * SLOTS * WIDE * X * UNITS,
     )
     other = lax.ppermute(other, "c", [(i, C - 1 - i) for i in range(C)])
     sums = lax.all_to_all(part, "h", 0, 0)

time: 115 us -> 114 us (level)
  waiting for transfers between devices: 11.5 us -> 10.3 us
    pallas_call x9 -> x10, Pallas kernels: 9.61 us -> 10 us  [call(): pl.pallas_call(kernel, out_shape=outs, in_specs=places, out_specs=out_pla...]
  transfers between devices with their start and end apart: 6 -> 6, of which waited for: 4 -> 4; matrix products, arithmetic and copies ran while one was open for 1% -> 1% of each run, Pallas kernels for 2% -> 3%
where the time goes in v15:
time: 114 us
  blocking collectives  55.3 us (49%)
  starting transfers between devices  36.4 us (32%)
  waiting for transfers between devices  10.3 us (9%)
  Pallas kernels  10 us (9%)
    all_gather x1, blocking collectives, on_device(): mine = lax.all_gather(mine, ('e', 'm'), axis=0)  17 us
    all_gather x1, blocking collectives, on_device(): block = lax.all_gather(block, 'h', axis=0, tiled=True)  16.4 us
    all_to_all x1, blocking collectives, on_device(): got = lax.all_to_all(send, ('l', 'x'), 0, 0)  13.1 us
    ppermute x1, starting transfers between devices, on_device(): other = lax.ppermute(block, 'c', [(i, C - 1 - i) for i in range(C)])  10.1 us
    pallas_call x10, Pallas kernels, call(): pl.pallas_call(kernel, out_shape=outs, in_specs=places, out_specs=out_pla...  10 us
    all_to_all x1, starting transfers between devices, on_device(): sums = lax.all_to_all(part, 'h', 0, 0)  9.36 us
    all_gather x1, blocking collectives, on_device(): both = lax.all_gather(both, 'c', axis=0)  8.74 us
    all_to_all x1, waiting for transfers between devices, on_device(): mine = lax.all_to_all(send, ('l', 'n', 'x'), 0, 0)  5.51 us
  transfers between devices with their start and end apart: 6, of which 4 were waited for; matrix products, arithmetic and copies ran while one was open for 1% of the time, Pallas kernels for 3%

profile of v15, /device:TPU:1, one launch (start us, length us, event | category | flops | bytes accessed | tf_op | source)
XLA Modules:
  0.0 113.9 jit_solution(14321451767951453610)
XLA Ops:
  0.6 1.7 %shard_map.94 = bf16[592,128]{1,0:T(8,128)(2,1)} custom-call(s32[1]{0:T(128)} %bitcast.where_ref, s32[1,2]{1,0:T(1,128)} %count_ref.1, s32[2,128]{1,0:T(2,128)} %bitcast.21, f32[2,128]{1,0:T(2,128)} %bitcast.18, bf16[128,128]{1,0:T(8,128)(2,1)} %bitcast.20, bf16[8,7168]{1,0:T(8,128)(2,1)} %values_ref.1, bf16[1,8]{1,0:T(2,128)(2,1)} %bitcast.22), custom_call_target="tpu_custom_call" | custom-call | bytes 301084 | tf_op jit(solution)/shard_map/pallas_call | solution.py:268
  2.3 8.7 %all-gather = bf16[1184,128]{1,0:T(8,128)(2,1)S(1)} all-gather(bf16[592,128]{1,0:T(8,128)(2,1)} %shard_map.94), channel_id=2, replica_groups=mesh['h'=4,'l'=2,'c'=2,'e'=2,'m'=2,'n'=2,'x'=4] {'c'}, dimensions={0}, use_global_device_ids=true | all-gather | bytes 454656 | tf_op jit(solution)/shard_map/all_gather | solution.py:292
  11.1 0.8 shard_map.96
  11.9 3.5 %all-to-all-start = ((bf16[16,16,512]{2,1,0:T(8,128)(2,1)}), bf16[16,16,512]{2,1,0:T(8,128)(2,1)S(1)}, u32[]{:S(2)}, u32[]{:S(2)}) async-start(bf16[16,16,512]{2,1,0:T(8,128)(2,1)} %shard_map.96), calls=%async_computation | async-start | bytes 524288 | tf_op jit(solution)/shard_map/all_to_all | solution.py:300
  15.4 1.1 dynamic_slice.3.w_ref
  16.5 1.2 %shard_map.95 = bf16[8,512,128]{2,1,0:T(8,128)(2,1)} custom-call(bf16[2,592,128]{2,1,0:T(8,128)(2,1)S(1)} %bitcast.16, bf16[64,3584]{1,0:T(8,128)(2,1)S(1)} %dynamic_slice.3.w_ref), custom_call_target="tpu_custom_call" | custom-call | bytes 1810432 | tf_op jit(solution)/shard_map/pallas_call | solution.py:268
  17.7 5.5 %all-to-all-done.rows_ref = bf16[16,16,512]{2,1,0:T(8,128)(2,1)S(1)} async-done(((bf16[16,16,512]{2,1,0:T(8,128)(2,1)}), bf16[16,16,512]{2,1,0:T(8,128)(2,1)S(1)}, u32[]{:S(2)}, u32[]{:S(2)}) %all-to-all-start) | async-done | bytes 262176 | tf_op jit(solution)/shard_map/all_to_all | solution.py:300
  23.2 3.6 %all-to-all-start.1 = ((bf16[8,512,128]{2,1,0:T(8,128)(2,1)}), bf16[8,512,128]{2,1,0:T(8,128)(2,1)S(1)}, u32[]{:S(2)}, u32[]{:S(2)}) async-start(bf16[8,512,128]{2,1,0:T(8,128)(2,1)} %shard_map.95), calls=%async_computation.1 | async-start | bytes 2097152 | tf_op jit(solution)/shard_map/all_to_all | solution.py:306
  26.8 17.0 %all-gather.1 = bf16[16,224,128]{2,1,0:T(8,128)(2,1)S(1)} all-gather(bf16[4,224,128]{2,1,0:T(8,128)(2,1)S(1)} %shard_map.97), channel_id=3, replica_groups=mesh['h'=4,'l'=2,'c'=2,'e'=2,'m'=2,'n'=2,'x'=4] {'e','m'}, dimensions={0}, use_global_device_ids=true | all-gather | bytes 1146880 | tf_op jit(solution)/shard_map/all_gather | solution.py:310
  43.9 1.6 %shard_map.98 = (bf16[4,4,112,128]{3,2,1,0:T(8,128)(2,1)}, bf16[512,512]{1,0:T(8,128)(2,1)S(1)}) custom-call(bf16[4,4,224,128]{3,2,1,0:T(8,128)(2,1)S(1)} %bitcast.14, bf16[8,512,128]{2,1,0:T(8,128)(2,1)S(1)} %all-to-all-done.1.pack_ref), custom_call_target="tpu_custom_call" | custom-call | flops 402653184 | bytes 2949120 | tf_op jit(solution)/shard_map/pallas_call | solution.py:268
  45.5 9.4 %all-to-all-start.2 = ((bf16[4,4,112,128]{3,2,1,0:T(8,128)(2,1)}), bf16[4,4,112,128]{3,2,1,0:T(8,128)(2,1)S(1)}, u32[]{:S(2)}, u32[]{:S(2)}) async-start(bf16[4,4,112,128]{3,2,1,0:T(8,128)(2,1)} %get-tuple-element.18), calls=%async_computation.2 | async-start | bytes 917504 | tf_op jit(solution)/shard_map/all_to_all | solution.py:327
  54.9 1.1 shard_map.99
  56.0 4.7 %collective-permute-start = (bf16[8,144,128]{2,1,0:T(8,128)(2,1)S(1)}, bf16[8,144,128]{2,1,0:T(8,128)(2,1)S(1)}, u32[]{:S(2)}, u32[]{:S(2)}) collective-permute-start(bf16[8,144,128]{2,1,0:T(8,128)(2,1)S(1)} %get-tuple-element.21), channel_id=1, source_target_pairs={{0,32},{32,0},{1,33},{33,1},{2,34},{34,2},{3,35},{35,3},{4,36},{36... | collective-permute-start | bytes 884744 | tf_op jit(solution)/shard_map/ppermute | solution.py:326
  60.7 1.2 %collective-permute-done.other_ref = bf16[8,144,128]{2,1,0:T(8,128)(2,1)S(1)} collective-permute-done((bf16[8,144,128]{2,1,0:T(8,128)(2,1)S(1)}, bf16[8,144,128]{2,1,0:T(8,128)(2,1)S(1)}, u32[]{:S(2)}, u32[]{:S(2)}) %collective-permute-start) | collective-permute-done | bytes 294944 | tf_op jit(solution)/shard_map/ppermute | solution.py:326
  61.9 2.5 %all-to-all-done.2.sums_ref = bf16[4,4,112,128]{3,2,1,0:T(8,128)(2,1)S(1)} async-done(((bf16[4,4,112,128]{3,2,1,0:T(8,128)(2,1)}), bf16[4,4,112,128]{3,2,1,0:T(8,128)(2,1)S(1)}, u32[]{:S(2)}, u32[]{:S(2)}) %all-to-all-start.2) | async-done | bytes 458784 | tf_op jit(solution)/shard_map/all_to_all | solution.py:327
  64.4 0.2 shard_map.100
  64.6 13.1 %all_to_all.32.got_ref = bf16[8,256,128]{2,1,0:T(8,128)(2,1)S(1)} all-to-all(bf16[8,256,128]{2,1,0:T(8,128)(2,1)S(1)} %shard_map.100), channel_id=1, replica_groups=mesh['h'=4,'l'=2,'c'=2,'e'=2,'m'=2,'n'=2,'x'=4] {'l','x'}, dimensions={0} | all-to-all | bytes 1048576 | tf_op jit(solution)/shard_map/all_to_all | solution.py:335
  77.7 0.8 shard_map.101
  78.5 5.1 %all-to-all-start.4 = ((f32[8,1,8]{2,1,0:T(1,128)}), f32[8,1,8]{2,1,0:T(1,128)S(1)}, u32[]{:S(2)}, u32[]{:S(2)}) async-start(f32[8,1,8]{2,1,0:T(1,128)} %bitcast.10), calls=%async_computation.4 | async-start | bytes 8192 | tf_op jit(solution)/shard_map/all_to_all | solution.py:342
  83.7 16.4 %all_gather.19.half_ref = bf16[128,3584]{1,0:T(8,128)(2,1)S(1)} all-gather(bf16[32,3584]{1,0:T(8,128)(2,1)S(1)} %get-tuple-element.23), channel_id=1, replica_groups=mesh['h'=4,'l'=2,'c'=2,'e'=2,'m'=2,'n'=2,'x'=4] {'h'}, dimensions={0}, use_global_device_ids=true | all-gather | bytes 1146880 | tf_op jit(solution)/shard_map/all_gather | solution.py:344
  100.1 10.1 %collective-permute-start.1 = (bf16[128,3584]{1,0:T(8,128)(2,1)S(1)}, bf16[128,3584]{1,0:T(8,128)(2,1)S(1)}, u32[]{:S(2)}, u32[]{:S(2)}) collective-permute-start(bf16[128,3584]{1,0:T(8,128)(2,1)S(1)} %all_gather.19.half_ref), channel_id=1, source_target_pairs={{0,32},{32,0},{1,33},{33,1},{2,34},{34,2},{3,35},{35,3},{4,36},{36... | collective-permute-start | bytes 2752520 | tf_op jit(solution)/shard_map/ppermute | solution.py:346
  110.3 0.9 shard_map.102.out_in_ref
  111.2 1.1 collective-permute-done.1.half_ref
  112.4 1.5 %shard_map.103 = (bf16[128,7168]{1,0:T(8,128)(2,1)}, f32[2,8]{1,0:T(2,128)}) custom-call(s32[1]{0:T(128)} %bitcast.6.core_ref, bf16[128,3584]{1,0:T(8,128)(2,1)S(1)} %collective-permute-done.1.half_ref, f32[8,8]{1,0:T(8,128)S(1)} %bitcast.17, bf16[128,7168]{1,0:T(8,128)(2,1)} %shard_map.102.out_in_ref), custom_call_target="tpu_custom_call", output_to_operand_aliasing={{0}: (3, {})} | custom-call | bytes 4587844 | tf_op jit(solution)/shard_map/pallas_call | solution.py:268
  (5 shorter events, 0.1 us)
Async XLA Ops:
  11.9 11.3 %all-to-all-start = ((bf16[16,16,512]{2,1,0:T(8,128)(2,1)}), bf16[16,16,512]{2,1,0:T(8,128)(2,1)S(1)}, u32[]{:S(2)}, u32[]{:S(2)}) async-start(bf16[16,16,512]{2,1,0:T(8,128)(2,1)} %shard_map.96), calls=%async_computation | async-start | bytes 524288 | tf_op jit(solution)/shard_map/all_to_all | solution.py:300
  23.2 20.7 %all-to-all-start.1 = ((bf16[8,512,128]{2,1,0:T(8,128)(2,1)}), bf16[8,512,128]{2,1,0:T(8,128)(2,1)S(1)}, u32[]{:S(2)}, u32[]{:S(2)}) async-start(bf16[8,512,128]{2,1,0:T(8,128)(2,1)} %shard_map.95), calls=%async_computation.1 | async-start | bytes 2097152 | tf_op jit(solution)/shard_map/all_to_all | solution.py:306
  45.5 18.9 %all-to-all-start.2 = ((bf16[4,4,112,128]{3,2,1,0:T(8,128)(2,1)}), bf16[4,4,112,128]{3,2,1,0:T(8,128)(2,1)S(1)}, u32[]{:S(2)}, u32[]{:S(2)}) async-start(bf16[4,4,112,128]{3,2,1,0:T(8,128)(2,1)} %get-tuple-element.18), calls=%async_computation.2 | async-start | bytes 917504 | tf_op jit(solution)/shard_map/all_to_all | solution.py:327
  54.9 22.8 %copy-start = (f32[1,2,128]{2,1,0:T(2,128)S(1)}, f32[1,2,128]{2,1,0:T(2,128)}, u32[]{:S(2)}) copy-start(f32[1,2,128]{2,1,0:T(2,128)} %param.13) | copy-start | bytes 3076
  56.0 5.8 %collective-permute-start = (bf16[8,144,128]{2,1,0:T(8,128)(2,1)S(1)}, bf16[8,144,128]{2,1,0:T(8,128)(2,1)S(1)}, u32[]{:S(2)}, u32[]{:S(2)}) collective-permute-start(bf16[8,144,128]{2,1,0:T(8,128)(2,1)S(1)} %get-tuple-element.21), channel_id=1, source_target_pairs={{0,32},{32,0},{1,33},{33,1},{2,34},{34,2},{3,35},{35,3},{4,36},{36... | collective-permute-start | bytes 884744 | tf_op jit(solution)/shard_map/ppermute | solution.py:326
  78.5 21.6 %all-to-all-start.4 = ((f32[8,1,8]{2,1,0:T(1,128)}), f32[8,1,8]{2,1,0:T(1,128)S(1)}, u32[]{:S(2)}, u32[]{:S(2)}) async-start(f32[8,1,8]{2,1,0:T(1,128)} %bitcast.10), calls=%async_computation.4 | async-start | bytes 8192 | tf_op jit(solution)/shard_map/all_to_all | solution.py:342
  100.1 12.2 %collective-permute-start.1 = (bf16[128,3584]{1,0:T(8,128)(2,1)S(1)}, bf16[128,3584]{1,0:T(8,128)(2,1)S(1)}, u32[]{:S(2)}, u32[]{:S(2)}) collective-permute-start(bf16[128,3584]{1,0:T(8,128)(2,1)S(1)} %all_gather.19.half_ref), channel_id=1, source_target_pairs={{0,32},{32,0},{1,33},{33,1},{2,34},{34,2},{3,35},{35,3},{4,36},{36... | collective-permute-start | bytes 2752520 | tf_op jit(solution)/shard_map/ppermute | solution.py:346

commit v16 on v15

--- a/solution.py
+++ b/solution.py
@@ -240,23 +240,27 @@
 
 
 def put_columns(half_ref, out_ref, core, sem):
-    width = X * PAIR
-    copy = pltpu.make_async_copy(
-        half_ref, out_ref.at[:, pl.ds(pl.multiple_of(core * width, LANES), width)], sem
-    )
-    copy.start()
-    return copy
+    width, step = X * PAIR, UNITS // 4
+    columns = pl.ds(pl.multiple_of(core * width, LANES), width)
+    copies = []
+    for i in range(4):
+        rows = pl.ds(i * step, step)
+        copies.append(pltpu.make_async_copy(half_ref.at[rows], out_ref.at[rows, columns], sem.at[i]))
+        copies[-1].start()
+    return copies
 
 
 def own_half_kernel(core_ref, half_ref, out_ref, sem):
-    put_columns(half_ref, out_ref, core_ref[0], sem).wait()
+    for copy in put_columns(half_ref, out_ref, core_ref[0], sem):
+        copy.wait()
 
 
 def other_half_kernel(core_ref, half_ref, spread_ref, out_in_ref, out_ref, gate_ref, sem):
-    copy = put_columns(half_ref, out_ref, 1 - core_ref[0], sem)
+    copies = put_columns(half_ref, out_ref, 1 - core_ref[0], sem)
     for e in range(E):
         gate_ref[e : e + 1, :] = jnp.sum(spread_ref[e * M * N : (e + 1) * M * N, :], axis=0, keepdims=True)
-    copy.wait()
+    for copy in copies:
+        copy.wait()
 
 
 VM, SM, HBM = (pl.BlockSpec(memory_space=m) for m in (pltpu.VMEM, pltpu.SMEM, pl.ANY))
@@ -345,7 +349,7 @@
     block, spread = lax.optimization_barrier((block, spread))
     other = lax.ppermute(block, "c", [(i, C - 1 - i) for i in range(C)])
     where = core[None].astype(I32)
-    sem = [pltpu.SemaphoreType.DMA(())]
+    sem = [pltpu.SemaphoreType.DMA((4,))]
     (whole,) = call(
         own_half_kernel, [SM, VM], [((UNITS, WIDTH), BF)], where, block, scratch=sem, out_places=[HBM]
     )

time: 114 us -> 114 us (level)
  no operation moved by 1% of the time
where the time goes in v16:
time: 114 us
  blocking collectives  55.3 us (49%)
  starting transfers between devices  36.4 us (32%)
  waiting for transfers between devices  10.3 us (9%)
  Pallas kernels  10.1 us (9%)
    all_gather x1, blocking collectives, on_device(): mine = lax.all_gather(mine, ('e', 'm'), axis=0)  17 us
    all_gather x1, blocking collectives, on_device(): block = lax.all_gather(block, 'h', axis=0, tiled=True)  16.4 us
    all_to_all x1, blocking collectives, on_device(): got = lax.all_to_all(send, ('l', 'x'), 0, 0)  13.1 us
    ppermute x1, starting transfers between devices, on_device(): other = lax.ppermute(block, 'c', [(i, C - 1 - i) for i in range(C)])  10.1 us
    pallas_call x10, Pallas kernels, call(): pl.pallas_call(kernel, out_shape=outs, in_specs=places, out_specs=out_pla...  10.1 us
    all_to_all x1, starting transfers between devices, on_device(): sums = lax.all_to_all(part, 'h', 0, 0)  9.36 us
    all_gather x1, blocking collectives, on_device(): both = lax.all_gather(both, 'c', axis=0)  8.74 us
    all_to_all x1, waiting for transfers between devices, on_device(): mine = lax.all_to_all(send, ('l', 'n', 'x'), 0, 0)  5.51 us
  transfers between devices with their start and end apart: 6, of which 4 were waited for; matrix products, arithmetic and copies ran while one was open for 1% of the time, Pallas kernels for 3%

profile of v16, /device:TPU:1, one launch (start us, length us, event | category | flops | bytes accessed | tf_op | source)
XLA Modules:
  0.0 113.9 jit_solution(9915609347791384425)
XLA Ops:
  0.6 1.7 %shard_map.94 = bf16[592,128]{1,0:T(8,128)(2,1)} custom-call(s32[1]{0:T(128)} %bitcast.where_ref, s32[1,2]{1,0:T(1,128)} %count_ref.1, s32[2,128]{1,0:T(2,128)} %bitcast.21, f32[2,128]{1,0:T(2,128)} %bitcast.18, bf16[128,128]{1,0:T(8,128)(2,1)} %bitcast.20, bf16[8,7168]{1,0:T(8,128)(2,1)} %values_ref.1, bf16[1,8]{1,0:T(2,128)(2,1)} %bitcast.22), custom_call_target="tpu_custom_call" | custom-call | bytes 301084 | tf_op jit(solution)/shard_map/pallas_call | solution.py:272
  2.3 8.7 %all-gather = bf16[1184,128]{1,0:T(8,128)(2,1)S(1)} all-gather(bf16[592,128]{1,0:T(8,128)(2,1)} %shard_map.94), channel_id=2, replica_groups=mesh['h'=4,'l'=2,'c'=2,'e'=2,'m'=2,'n'=2,'x'=4] {'c'}, dimensions={0}, use_global_device_ids=true | all-gather | bytes 454656 | tf_op jit(solution)/shard_map/all_gather | solution.py:296
  11.1 0.8 shard_map.96
  11.9 3.5 %all-to-all-start = ((bf16[16,16,512]{2,1,0:T(8,128)(2,1)}), bf16[16,16,512]{2,1,0:T(8,128)(2,1)S(1)}, u32[]{:S(2)}, u32[]{:S(2)}) async-start(bf16[16,16,512]{2,1,0:T(8,128)(2,1)} %shard_map.96), calls=%async_computation | async-start | bytes 524288 | tf_op jit(solution)/shard_map/all_to_all | solution.py:304
  15.4 1.1 dynamic_slice.3.w_ref
  16.5 1.2 %shard_map.95 = bf16[8,512,128]{2,1,0:T(8,128)(2,1)} custom-call(bf16[2,592,128]{2,1,0:T(8,128)(2,1)S(1)} %bitcast.16, bf16[64,3584]{1,0:T(8,128)(2,1)S(1)} %dynamic_slice.3.w_ref), custom_call_target="tpu_custom_call" | custom-call | bytes 1810432 | tf_op jit(solution)/shard_map/pallas_call | solution.py:272
  17.7 5.5 %all-to-all-done.rows_ref = bf16[16,16,512]{2,1,0:T(8,128)(2,1)S(1)} async-done(((bf16[16,16,512]{2,1,0:T(8,128)(2,1)}), bf16[16,16,512]{2,1,0:T(8,128)(2,1)S(1)}, u32[]{:S(2)}, u32[]{:S(2)}) %all-to-all-start) | async-done | bytes 262176 | tf_op jit(solution)/shard_map/all_to_all | solution.py:304
  23.2 3.6 %all-to-all-start.1 = ((bf16[8,512,128]{2,1,0:T(8,128)(2,1)}), bf16[8,512,128]{2,1,0:T(8,128)(2,1)S(1)}, u32[]{:S(2)}, u32[]{:S(2)}) async-start(bf16[8,512,128]{2,1,0:T(8,128)(2,1)} %shard_map.95), calls=%async_computation.1 | async-start | bytes 2097152 | tf_op jit(solution)/shard_map/all_to_all | solution.py:310
  26.8 17.0 %all-gather.1 = bf16[16,224,128]{2,1,0:T(8,128)(2,1)S(1)} all-gather(bf16[4,224,128]{2,1,0:T(8,128)(2,1)S(1)} %shard_map.97), channel_id=3, replica_groups=mesh['h'=4,'l'=2,'c'=2,'e'=2,'m'=2,'n'=2,'x'=4] {'e','m'}, dimensions={0}, use_global_device_ids=true | all-gather | bytes 1146880 | tf_op jit(solution)/shard_map/all_gather | solution.py:314
  43.9 1.6 %shard_map.98 = (bf16[4,4,112,128]{3,2,1,0:T(8,128)(2,1)}, bf16[512,512]{1,0:T(8,128)(2,1)S(1)}) custom-call(bf16[4,4,224,128]{3,2,1,0:T(8,128)(2,1)S(1)} %bitcast.14, bf16[8,512,128]{2,1,0:T(8,128)(2,1)S(1)} %all-to-all-done.1.pack_ref), custom_call_target="tpu_custom_call" | custom-call | flops 402653184 | bytes 2949120 | tf_op jit(solution)/shard_map/pallas_call | solution.py:272
  45.5 9.4 %all-to-all-start.2 = ((bf16[4,4,112,128]{3,2,1,0:T(8,128)(2,1)}), bf16[4,4,112,128]{3,2,1,0:T(8,128)(2,1)S(1)}, u32[]{:S(2)}, u32[]{:S(2)}) async-start(bf16[4,4,112,128]{3,2,1,0:T(8,128)(2,1)} %get-tuple-element.18), calls=%async_computation.2 | async-start | bytes 917504 | tf_op jit(solution)/shard_map/all_to_all | solution.py:331
  54.9 1.1 shard_map.99
  56.0 4.7 %collective-permute-start = (bf16[8,144,128]{2,1,0:T(8,128)(2,1)S(1)}, bf16[8,144,128]{2,1,0:T(8,128)(2,1)S(1)}, u32[]{:S(2)}, u32[]{:S(2)}) collective-permute-start(bf16[8,144,128]{2,1,0:T(8,128)(2,1)S(1)} %get-tuple-element.21), channel_id=1, source_target_pairs={{0,32},{32,0},{1,33},{33,1},{2,34},{34,2},{3,35},{35,3},{4,36},{36... | collective-permute-start | bytes 884744 | tf_op jit(solution)/shard_map/ppermute | solution.py:330
  60.7 1.2 %collective-permute-done.other_ref = bf16[8,144,128]{2,1,0:T(8,128)(2,1)S(1)} collective-permute-done((bf16[8,144,128]{2,1,0:T(8,128)(2,1)S(1)}, bf16[8,144,128]{2,1,0:T(8,128)(2,1)S(1)}, u32[]{:S(2)}, u32[]{:S(2)}) %collective-permute-start) | collective-permute-done | bytes 294944 | tf_op jit(solution)/shard_map/ppermute | solution.py:330
  61.9 2.5 %all-to-all-done.2.sums_ref = bf16[4,4,112,128]{3,2,1,0:T(8,128)(2,1)S(1)} async-done(((bf16[4,4,112,128]{3,2,1,0:T(8,128)(2,1)}), bf16[4,4,112,128]{3,2,1,0:T(8,128)(2,1)S(1)}, u32[]{:S(2)}, u32[]{:S(2)}) %all-to-all-start.2) | async-done | bytes 458784 | tf_op jit(solution)/shard_map/all_to_all | solution.py:331
  64.4 0.2 shard_map.100
  64.6 13.1 %all_to_all.32.got_ref = bf16[8,256,128]{2,1,0:T(8,128)(2,1)S(1)} all-to-all(bf16[8,256,128]{2,1,0:T(8,128)(2,1)S(1)} %shard_map.100), channel_id=1, replica_groups=mesh['h'=4,'l'=2,'c'=2,'e'=2,'m'=2,'n'=2,'x'=4] {'l','x'}, dimensions={0} | all-to-all | bytes 1048576 | tf_op jit(solution)/shard_map/all_to_all | solution.py:339
  77.7 0.8 shard_map.101
  78.5 5.1 %all-to-all-start.4 = ((f32[8,1,8]{2,1,0:T(1,128)}), f32[8,1,8]{2,1,0:T(1,128)S(1)}, u32[]{:S(2)}, u32[]{:S(2)}) async-start(f32[8,1,8]{2,1,0:T(1,128)} %bitcast.10), calls=%async_computation.4 | async-start | bytes 8192 | tf_op jit(solution)/shard_map/all_to_all | solution.py:346
  83.7 16.4 %all_gather.19.half_ref = bf16[128,3584]{1,0:T(8,128)(2,1)S(1)} all-gather(bf16[32,3584]{1,0:T(8,128)(2,1)S(1)} %get-tuple-element.23), channel_id=1, replica_groups=mesh['h'=4,'l'=2,'c'=2,'e'=2,'m'=2,'n'=2,'x'=4] {'h'}, dimensions={0}, use_global_device_ids=true | all-gather | bytes 1146880 | tf_op jit(solution)/shard_map/all_gather | solution.py:348
  100.1 10.1 %collective-permute-start.1 = (bf16[128,3584]{1,0:T(8,128)(2,1)S(1)}, bf16[128,3584]{1,0:T(8,128)(2,1)S(1)}, u32[]{:S(2)}, u32[]{:S(2)}) collective-permute-start(bf16[128,3584]{1,0:T(8,128)(2,1)S(1)} %all_gather.19.half_ref), channel_id=1, source_target_pairs={{0,32},{32,0},{1,33},{33,1},{2,34},{34,2},{3,35},{35,3},{4,36},{36... | collective-permute-start | bytes 2752520 | tf_op jit(solution)/shard_map/ppermute | solution.py:350
  110.3 1.0 shard_map.102.out_in_ref
  111.2 1.1 collective-permute-done.1.half_ref
  112.4 1.5 %shard_map.103 = (bf16[128,7168]{1,0:T(8,128)(2,1)}, f32[2,8]{1,0:T(2,128)}) custom-call(s32[1]{0:T(128)} %bitcast.6.core_ref, bf16[128,3584]{1,0:T(8,128)(2,1)S(1)} %collective-permute-done.1.half_ref, f32[8,8]{1,0:T(8,128)S(1)} %bitcast.17, bf16[128,7168]{1,0:T(8,128)(2,1)} %shard_map.102.out_in_ref), custom_call_target="tpu_custom_call", output_to_operand_aliasing={{0}: (3, {})} | custom-call | bytes 4587844 | tf_op jit(solution)/shard_map/pallas_call | solution.py:272
  (5 shorter events, 0.1 us)
Async XLA Ops:
  11.9 11.3 %all-to-all-start = ((bf16[16,16,512]{2,1,0:T(8,128)(2,1)}), bf16[16,16,512]{2,1,0:T(8,128)(2,1)S(1)}, u32[]{:S(2)}, u32[]{:S(2)}) async-start(bf16[16,16,512]{2,1,0:T(8,128)(2,1)} %shard_map.96), calls=%async_computation | async-start | bytes 524288 | tf_op jit(solution)/shard_map/all_to_all | solution.py:304
  23.2 20.7 %all-to-all-start.1 = ((bf16[8,512,128]{2,1,0:T(8,128)(2,1)}), bf16[8,512,128]{2,1,0:T(8,128)(2,1)S(1)}, u32[]{:S(2)}, u32[]{:S(2)}) async-start(bf16[8,512,128]{2,1,0:T(8,128)(2,1)} %shard_map.95), calls=%async_computation.1 | async-start | bytes 2097152 | tf_op jit(solution)/shard_map/all_to_all | solution.py:310
  45.5 18.9 %all-to-all-start.2 = ((bf16[4,4,112,128]{3,2,1,0:T(8,128)(2,1)}), bf16[4,4,112,128]{3,2,1,0:T(8,128)(2,1)S(1)}, u32[]{:S(2)}, u32[]{:S(2)}) async-start(bf16[4,4,112,128]{3,2,1,0:T(8,128)(2,1)} %get-tuple-element.18), calls=%async_computation.2 | async-start | bytes 917504 | tf_op jit(solution)/shard_map/all_to_all | solution.py:331
  54.9 22.8 %copy-start = (f32[1,2,128]{2,1,0:T(2,128)S(1)}, f32[1,2,128]{2,1,0:T(2,128)}, u32[]{:S(2)}) copy-start(f32[1,2,128]{2,1,0:T(2,128)} %param.13) | copy-start | bytes 3076
  56.0 5.8 %collective-permute-start = (bf16[8,144,128]{2,1,0:T(8,128)(2,1)S(1)}, bf16[8,144,128]{2,1,0:T(8,128)(2,1)S(1)}, u32[]{:S(2)}, u32[]{:S(2)}) collective-permute-start(bf16[8,144,128]{2,1,0:T(8,128)(2,1)S(1)} %get-tuple-element.21), channel_id=1, source_target_pairs={{0,32},{32,0},{1,33},{33,1},{2,34},{34,2},{3,35},{35,3},{4,36},{36... | collective-permute-start | bytes 884744 | tf_op jit(solution)/shard_map/ppermute | solution.py:330
  78.5 21.6 %all-to-all-start.4 = ((f32[8,1,8]{2,1,0:T(1,128)}), f32[8,1,8]{2,1,0:T(1,128)S(1)}, u32[]{:S(2)}, u32[]{:S(2)}) async-start(f32[8,1,8]{2,1,0:T(1,128)} %bitcast.10), calls=%async_computation.4 | async-start | bytes 8192 | tf_op jit(solution)/shard_map/all_to_all | solution.py:346
  100.1 12.2 %collective-permute-start.1 = (bf16[128,3584]{1,0:T(8,128)(2,1)S(1)}, bf16[128,3584]{1,0:T(8,128)(2,1)S(1)}, u32[]{:S(2)}, u32[]{:S(2)}) collective-permute-start(bf16[128,3584]{1,0:T(8,128)(2,1)S(1)} %all_gather.19.half_ref), channel_id=1, source_target_pairs={{0,32},{32,0},{1,33},{33,1},{2,34},{34,2},{3,35},{35,3},{4,36},{36... | collective-permute-start | bytes 2752520 | tf_op jit(solution)/shard_map/ppermute | solution.py:350
